TPU v7x, 256 devices: a whole 4x4x8 slice. The times are simulated.
256 devices in a mesh: section: 8 (over y, core), expert: 32 (over x, z).
Axes of the slice: x: 4, y: 4, z: 8, core: 2. Of those that a mesh axis runs over, the one named last changes fastest.
Arguments:
- out_grad: bfloat16 [8, 4096, 7168], P('section', 'expert'), may hold values from -6 to 6
- router_weight: bfloat16 [8, 7168, 8], P('section'), may hold values from -0.25 to 0.25
- down_weight: bfloat16 [8, 8192, 7168], P('section', 'expert'), may hold values from -0.1875 to 0.1875
- hidden_saved: bfloat16 [8, 32, 32, 32, 256], P('section', 'expert'), may hold values from -1.5 to 1.5
- slot_token: int32 [8, 32, 8, 32], P('section', 'expert'), may hold values from 0 to 127, as said below
- slot_count: int32 [8, 32, 8], P('section', 'expert'), may hold values from 8 to 32, as said below
- slot_gate: float32 [8, 32, 8, 32], P('section', 'expert'), may hold values from 0.02 to 1
Outputs:
- down_grad: bfloat16 [8, 8192, 7168], P('section', 'expert')
- hidden_grad: bfloat16 [8, 32, 32, 32, 256], P('section', 'expert')
- passed_grad: bfloat16 [8, 4096, 7168], P('section', 'expert')
Inputs may be any that keep to these rules, and one draw needn't show every extreme that they name: `slot_token`: within each block the used slots name distinct tokens; entries at slots from the count onward are ignored. `slot_count`: in every section one expert has 32 used slots in the block of every source device.
All inputs are finite; a program needn't handle non-finite values.
Results may differ from a plain program's by a relative error of at most 0.015.
Values may be sent and summed in bfloat16 or wider, within the bound.
No kernel may reach another device: no remote copies, remote signals or barrier semaphores. Data moves between devices by JAX's collectives and lax.ppermute only.
A program may use at most 128 MiB of HBM per device.

v0:
```python
import jax
import jax.numpy as jnp
from jax import lax
from jax.sharding import PartitionSpec as P


def passed_along(value, axis, steps):
    count = lax.axis_size(axis)
    initial, last = (max(0, -steps), min(count, count - steps))
    return lax.ppermute(value, axis, [(source, source + steps) for source in range(initial, last)])


def shards(out_grad, router_weight, down_weight, hidden_saved, slot_token, slot_count, slot_gate):
    high = lax.Precision.HIGHEST
    grad = out_grad[0]
    tokens = slot_token[0, 0]
    counts = slot_count[0, 0]
    gates = slot_gate[0, 0]
    experts, capacity = tokens.shape
    width = grad.shape[1]
    group = lax.axis_size("expert") // experts
    slots = lax.broadcasted_iota(jnp.int32, (experts, capacity), 1)
    live = slots < counts[:, None]
    gate_live = jnp.where(live, gates, jnp.float32(0.0))
    rows = jnp.where(live[..., None], grad[tokens], jnp.zeros((), grad.dtype))
    gate_sent = jnp.broadcast_to(gate_live[:, None], (experts, group, capacity)).reshape(
        experts * group, capacity
    )
    sent = jnp.broadcast_to(rows[:, None], (experts, group, capacity, width)).reshape(
        experts * group, capacity, width
    )
    got_rows, got_gate = (
        lax.all_to_all(sent, "expert", split_axis=0, concat_axis=0, tiled=True),
        lax.all_to_all(
            gate_sent.astype(jnp.bfloat16), "expert", split_axis=0, concat_axis=0, tiled=True
        ).astype(gate_sent.dtype),
    )
    w_block = down_weight[0]
    held = hidden_saved[0, 0]
    proj = jnp.einsum("scd,hd->sch", got_rows, w_block, preferred_element_type=jnp.float32)
    hidden_grad = (got_gate[..., None] * proj).astype(jnp.bfloat16)
    partial_value = jnp.sum(held.astype(jnp.float32) * proj, axis=-1)
    scaled = (got_gate[..., None] * got_rows.astype(jnp.float32)).astype(jnp.bfloat16)
    down_grad = jnp.einsum("sch,scd->hd", held, scaled, preferred_element_type=jnp.float32).astype(
        jnp.bfloat16
    )
    returned = lax.all_to_all(partial_value, "expert", split_axis=0, concat_axis=0, tiled=True)
    gate_grad = returned.reshape(experts, group, capacity).sum(axis=1)
    tok_count = grad.shape[0]
    positions = lax.broadcasted_iota(jnp.int32, (experts, capacity, tok_count), 2)
    match = jnp.where(
        (tokens[..., None] == positions) & live[..., None], jnp.float32(1.0), jnp.float32(0.0)
    )
    logit_grad = jnp.einsum("ec,ect->te", gate_grad, match, precision=high)
    input_grad = grad.astype(jnp.float32) + jnp.dot(
        logit_grad, router_weight[0].astype(jnp.float32).T, precision=high
    )
    passed = passed_along(input_grad.astype(jnp.bfloat16), "section", -1)
    return (down_grad[None], hidden_grad[None, None], passed[None])


def solution(mesh):
    return jax.shard_map(
        shards,
        mesh=mesh,
        in_specs=(
            P("section", "expert", None),
            P("section", None, None),
            P("section", "expert", None),
            P("section", "expert", None, None, None),
            P("section", "expert", None, None),
            P("section", "expert", None),
            P("section", "expert", None, None),
        ),
        out_specs=(
            P("section", "expert", None),
            P("section", "expert", None, None, None),
            P("section", "expert", None),
        ),
        check_vma=False,
    )
```

profile of v0, /device:TPU:1, one launch (start us, length us, event | category | flops | bytes accessed | tf_op | source)
XLA Modules:
  0.0 464.7 jit_solution(12028493933433557631)
XLA Ops:
  0.6 0.0 copy-start
  0.6 0.8 fusion.19
  1.4 0.6 copy.16
  2.1 11.9 %all-to-all-start = ((bf16[32,1,32]{2,1,0:T(2,128)(2,1)}), bf16[32,1,32]{2,1,0:T(2,128)(2,1)S(1)}, u32[]{:S(2)}, u32[]{:S(2)}) async-start(bf16[32,1,32]{2,1,0:T(2,128)(2,1)} %copy.16), calls=%async_computation | async-start | bytes 32768 | tf_op jit(solution)/shard_map/all_to_all | solution.py:34
  13.9 0.7 iota_compare_fusion.1
  14.7 0.7 compare_select_fusion
  15.4 0.1 reshape.117
  15.5 9.8 %gather_fusion = bf16[256,7168]{1,0:T(8,128)(2,1)} fusion(bf16[128,7168]{1,0:T(8,128)(2,1)} %bitcast.52, s32[1024]{0:T(1024)S(1)} %pad_clamp_fusion), kind=kCustom, calls=%fused_computation | custom fusion | bytes 7341056 | tf_op jit(solution)/shard_map/gather | solution.py:25
  25.2 4.2 broadcast_select_fusion
  29.4 0.0 all-to-all-done
  29.4 6.6 %broadcast_in_dim.54 = bf16[8,4,32,7168]{3,2,1,0:T(8,128)(2,1)} broadcast(bf16[8,32,7168]{2,1,0:T(8,128)(2,1)} %broadcast_select_fusion), dimensions={0,2,3} | broadcast | bytes 18350080 | tf_op jit(solution)/shard_map/broadcast_in_dim | solution.py:29
  36.1 0.0 copy-start.3
  36.1 9.5 %all-to-all-start.1 = ((bf16[32,32,7168]{2,1,0:T(8,128)(2,1)}), bf16[32,32,7168]{2,1,0:T(8,128)(2,1)}, u32[]{:S(2)}, u32[]{:S(2)}) async-start(bf16[32,32,7168]{2,1,0:T(8,128)(2,1)} %bitcast.53), calls=%async_computation.1 | async-start | bytes 29360128 | tf_op jit(solution)/shard_map/all_to_all | solution.py:33
  45.6 330.9 %all-to-all-done.1 = bf16[32,32,7168]{2,1,0:T(8,128)(2,1)} async-done(((bf16[32,32,7168]{2,1,0:T(8,128)(2,1)}), bf16[32,32,7168]{2,1,0:T(8,128)(2,1)}, u32[]{:S(2)}, u32[]{:S(2)}) %all-to-all-start.1) | async-done | bytes 14680096 | tf_op jit(solution)/shard_map/all_to_all | solution.py:33
  376.4 0.0 copy-done.3
  376.4 0.0 copy-start.2
  376.4 0.0 copy-start.1
  376.4 11.1 %multiply_reduce_fusion = (f32[32,32]{1,0:T(8,128)S(1)}, bf16[1,1,32,32,256]{4,3,2,1,0:T(8,128)(2,1)}) fusion(bf16[1,1,32,32,256]{4,3,2,1,0:T(8,128)(2,1)S(1)} %copy-done.3, f32[32,32]{1,0:T(8,128)S(1)} %bitcast.58, bf16[32,32,7168]{2,1,0:T(8,128)(2,1)} %all-to-all-done.1, bf16[1,256,7168]{2,1,0:T(8,128)(2,1)} %param.9), kind=kOutput, calls=%fused_computation.12 | convolution fusion | flops 3759406080 | bytes 19406848 | tf_op jit(solution)/shard_map/scd,hd->sch/dot_general | solution.py:40
  387.6 46.4 %all_to_all.20 = f32[32,1,32]{2,1,0:T(1,128)S(1)} all-to-all(f32[32,1,32]{2,1,0:T(1,128)S(1)} %bitcast.60), channel_id=1, replica_groups=mesh['section'=8,'expert'=32] {'expert'}, dimensions={0} | all-to-all | bytes 8192 | tf_op jit(solution)/shard_map/all_to_all | solution.py:47
  434.0 0.0 copy-done.2
  434.0 0.3 fusion.10
  434.4 0.0 copy-done
  434.4 0.0 copy-done.1
  434.4 2.9 fusion.5
  437.3 3.9 collective-permute-start
  441.2 12.0 %fusion.4 = bf16[1,256,7168]{1,2,0:T(8,128)(2,1)} fusion(bf16[32,32,7168]{2,1,0:T(8,128)(2,1)} %all-to-all-done.1, f32[32,32]{1,0:T(8,128)S(1)} %bitcast.59, bf16[1,1,32,32,256]{4,3,2,1,0:T(8,128)(2,1)S(1)} %copy-done.3), kind=kOutput, calls=%fused_computation.6 | convolution fusion | flops 3781951488 | bytes 18878464 | tf_op jit(solution)/shard_map/sch,scd->hd/dot_general | solution.py:44
  453.2 5.9 %copy.17 = bf16[1,256,7168]{2,1,0:T(8,128)(2,1)} copy(bf16[1,256,7168]{1,2,0:T(8,128)(2,1)} %fusion.4) | data formatting | bytes 7340032
  459.1 4.3 collective-permute-done
  463.5 1.2 copy.21
  (4 shorter events, 0.1 us)
Async XLA Ops:
  0.6 433.7 %copy-start = (bf16[1,7168,8]{1,2,0:T(8,128)(2,1)S(1)}, bf16[1,7168,8]{1,2,0:T(8,128)(2,1)}, u32[]{:S(2)}) copy-start(bf16[1,7168,8]{1,2,0:T(8,128)(2,1)} %param.8) | copy-start | bytes 344068
  2.1 27.3 %all-to-all-start = ((bf16[32,1,32]{2,1,0:T(2,128)(2,1)}), bf16[32,1,32]{2,1,0:T(2,128)(2,1)S(1)}, u32[]{:S(2)}, u32[]{:S(2)}) async-start(bf16[32,1,32]{2,1,0:T(2,128)(2,1)} %copy.16), calls=%async_computation | async-start | bytes 32768 | tf_op jit(solution)/shard_map/all_to_all | solution.py:34
  36.1 340.4 %copy-start.3 = (bf16[1,1,32,32,256]{4,3,2,1,0:T(8,128)(2,1)S(1)}, bf16[1,1,32,32,256]{4,3,2,1,0:T(8,128)(2,1)}, u32[]{:S(2)}) copy-start(bf16[1,1,32,32,256]{4,3,2,1,0:T(8,128)(2,1)} %param.10) | copy-start | bytes 1572868
  36.1 340.4 %all-to-all-start.1 = ((bf16[32,32,7168]{2,1,0:T(8,128)(2,1)}), bf16[32,32,7168]{2,1,0:T(8,128)(2,1)}, u32[]{:S(2)}, u32[]{:S(2)}) async-start(bf16[32,32,7168]{2,1,0:T(8,128)(2,1)} %bitcast.53), calls=%async_computation.1 | async-start | bytes 29360128 | tf_op jit(solution)/shard_map/all_to_all | solution.py:33
  376.4 57.6 %copy-start.2 = (s32[1,1,8,32]{3,2,1,0:T(8,128)S(1)}, s32[1,1,8,32]{3,2,1,0:T(8,128)}, u32[]{:S(2)}) copy-start(s32[1,1,8,32]{3,2,1,0:T(8,128)} %param.11) | copy-start | bytes 3076
  376.4 57.9 %copy-start.1 = (bf16[1,128,7168]{2,1,0:T(8,128)(2,1)S(1)}, bf16[1,128,7168]{2,1,0:T(8,128)(2,1)}, u32[]{:S(2)}) copy-start(bf16[1,128,7168]{2,1,0:T(8,128)(2,1)} %param.7) | copy-start | bytes 5505028
  437.3 26.2 %collective-permute-start = (bf16[128,7168]{1,0:T(8,128)(2,1)}, bf16[128,7168]{1,0:T(8,128)(2,1)S(1)}, u32[]{:S(2)}, u32[]{:S(2)}) collective-permute-start(bf16[128,7168]{1,0:T(8,128)(2,1)} %fusion.5), channel_id=1, source_target_pairs={{32,0},{64,32},{96,64},{128,96},{160,128},{192,160},{224,192},{33,... | collective-permute-start | bytes 5505032 | tf_op jit(solution)/shard_map/ppermute | solution.py:10
where the time goes:
time: 465 us
  waiting for transfers between devices  335 us (72%)
  blocking collectives  46.4 us (10%)
  matrix products  26.4 us (6%)
  starting transfers between devices  25.2 us (5%)
  local copies, waits for them, and re-layouts  24.3 us (5%)
  other arithmetic  6.44 us (1%)
    all_to_all x1, waiting for transfers between devices, shards(): lax.all_to_all(sent, 'expert', split_axis=0, concat_axis=0, tiled=True)  331 us
    all_to_all x1, blocking collectives, shards(): lax.all_to_all(partial_value, 'expert', split_axis=0, concat_axis=0, tile...  46.4 us
    dot_general x1, matrix products, shards(): jnp.einsum('sch,scd->hd', held, scaled, preferred_element_type=jnp.float32)  12 us
    all_to_all x1, starting transfers between devices, shards(): lax.all_to_all(gate_sent.astype(jnp.bfloat16), 'expert', split_axis=0, co...  11.9 us
    dot_general x1, matrix products, shards(): jnp.einsum('scd,hd->sch', got_rows, w_block, preferred_element_type=jnp.f...  11.1 us
    gather x1, local copies, waits for them, and re-layouts, shards(): rows = jnp.where(live[..., None], grad[tokens], jnp.zeros((), grad.dtype))  9.77 us
    all_to_all x1, starting transfers between devices, shards(): lax.all_to_all(sent, 'expert', split_axis=0, concat_axis=0, tiled=True)  9.47 us
  transfers between devices with their start and end apart: 3, of which 2 were waited for; matrix products, arithmetic and copies ran while one was open for 7% of the time, Pallas kernels for 0%

commit v1 on v0

v1 whole, which is shorter than its diff:
```python
import jax
import jax.numpy as jnp
from jax import lax
from jax.experimental import pallas as pl
from jax.experimental.pallas import tpu as pltpu
from jax.sharding import PartitionSpec as P

NX, NZ = 4, 8
TILE = 1792
WIDE = 1792
LANES = 128
META = 4
BF, F32 = jnp.bfloat16, jnp.float32


def shift_x(k):
    return [(x * NZ + z, (x + k) % NX * NZ + z) for x in range(NX) for z in range(NZ)]


def shift_z(k):
    return [(x * NZ + z, x * NZ + (z + k) % NZ) for x in range(NX) for z in range(NZ)]


def passed_along(value, axis, steps):
    count = lax.axis_size(axis)
    initial, last = (max(0, -steps), min(count, count - steps))
    return lax.ppermute(value, axis, [(source, source + steps) for source in range(initial, last)])


def call(kernel, grid, in_specs, out_specs, out_shape, scratch=(), aliases=None, flops=0, nbytes=0, vmem=63):
    return pl.pallas_call(
        kernel,
        grid_spec=pltpu.PrefetchScalarGridSpec(
            num_scalar_prefetch=1,
            grid=grid,
            in_specs=in_specs,
            out_specs=out_specs,
            scratch_shapes=list(scratch),
        ),
        out_shape=out_shape,
        input_output_aliases=aliases or {},
        compiler_params=pltpu.CompilerParams(vmem_limit_bytes=vmem * 1024 * 1024),
        cost_estimate=pl.CostEstimate(flops=flops, bytes_accessed=nbytes, transcendentals=0),
    )


def whole(shape):
    return pl.BlockSpec(shape, lambda j, w: (0,) * len(shape))


def columns(rows, tile, start):
    return pl.BlockSpec((rows, tile), lambda j, w: (0, j + start // tile))


HBM = pl.BlockSpec(memory_space=pl.ANY)


def picked(w_ref, meta, parts, outs, at_row):
    slots, tokens = meta.shape[0], parts[0].shape[0]
    cap = slots // NX
    half = w_ref[1] // (NZ // 2)
    lane = lax.broadcasted_iota(jnp.int32, (slots, LANES), 1)
    wanted = jnp.sum(jnp.where(lane == META * half, meta.astype(F32), F32(0.0)), axis=1, keepdims=True)
    place = lax.broadcasted_iota(jnp.int32, (slots, tokens), 1).astype(F32)
    hot = jnp.where(wanted == place, F32(1.0), F32(0.0)).astype(BF)
    at = 0
    for part in parts:
        got = jnp.dot(hot, part[...], preferred_element_type=F32).astype(BF)
        for k in range(NX):
            outs[k][at_row : at_row + cap, at : at + part.shape[1]] = got[k * cap : (k + 1) * cap]
        at += part.shape[1]
    for k in range(NX):
        outs[k][at_row : at_row + cap, at:] = meta[k * cap : (k + 1) * cap]


def begin(where, grad, tokens, gates):
    count, width = grad.shape
    cap = tokens.shape[1]

    def kernel(w_ref, g_ref, t_ref, s_ref, block_ref, *outs):
        block_ref[:, :width] = g_ref[...]
        block_ref[:, width:] = jnp.zeros((count, LANES), BF)
        slot = lax.broadcasted_iota(jnp.int32, (1, cap), 1)
        for k in range(NX):
            lines = []
            for half in (0, 1):
                e = lax.rem(w_ref[0] + k, NX) * 2 + half
                live = slot < w_ref[2 + e]
                lines.append(jnp.where(live, t_ref[pl.ds(e, 1), :], -1).astype(F32))
                rest = jnp.where(live, s_ref[pl.ds(e, 1), :], F32(0.0))
                for _ in range(META - 1):
                    piece = rest.astype(BF).astype(F32)
                    lines.append(piece)
                    rest = rest - piece
            table = jnp.concatenate(lines, 0)
            table = jnp.concatenate([table, jnp.zeros((2 * META, LANES - cap), F32)], 1)
            table = jnp.concatenate([table, jnp.zeros((LANES - 2 * META, LANES), F32)], 0).T
            block_ref[k * cap : (k + 1) * cap, width:] = table[:cap].astype(BF)
        picked(w_ref, block_ref[:, width:], [g_ref], outs, 0)

    full = width + LANES
    return call(
        kernel,
        (1,),
        [whole(x.shape) for x in (grad, tokens, gates)],
        [whole((count, full))] + [whole((cap, full))] * NX,
        [jax.ShapeDtypeStruct((count, full), BF)] + [jax.ShapeDtypeStruct((cap, full), BF)] * NX,
        flops=2 * NX * cap * count * width,
        nbytes=6 * count * width,
    )(where, grad, tokens, gates)


def pick_rows(where, blocks, after):
    n = len(blocks)
    flat = [x for block in blocks for x in block]
    tokens = flat[0].shape[0]
    full = sum(x.shape[1] for x in blocks[0])
    cap = tokens // NX

    def kernel(w_ref, *refs):
        outs = refs[-NX:]
        for b in range(n):
            parts = list(refs[b * len(blocks[b]) : (b + 1) * len(blocks[b])])
            cut = parts[-1].shape[1] - LANES
            meta = parts[-1][:, cut:]
            parts[-1] = parts[-1].at[:, :cut]
            picked(w_ref, meta, parts, outs, b * cap)

    return call(
        kernel,
        (1,),
        [whole(x.shape) for x in flat] + [HBM] * len(after),
        [whole((n * cap, full))] * NX,
        [jax.ShapeDtypeStruct((n * cap, full), BF)] * NX,
        flops=2 * n * tokens * tokens * full,
        nbytes=4 * n * tokens * full,
    )(where, *flat, *after)


def hold(arrays, after):
    n = len(arrays)
    return pl.pallas_call(
        lambda *refs: None,
        in_specs=[HBM] * (n + len(after)),
        out_specs=[HBM] * n,
        out_shape=[jax.ShapeDtypeStruct(x.shape, x.dtype) for x in arrays],
        input_output_aliases={i: i for i in range(n)},
    )(*arrays, *after)


def project(where, got, weight, held, shifts, before):
    rows = got[0].shape[0]
    hid, width = weight.shape
    cap = rows // len(shifts)
    steps = width // 2 // TILE
    n = NX * len(shifts)

    def kernel(w_ref, *refs):
        lows, highs, metas = refs[:NX], refs[NX : 2 * NX], refs[2 * NX : 3 * NX]
        w_low, w_high, held_hbm = refs[3 * NX : 3 * NX + 3]
        hid_hbm, part_hbm, scaled_ref, acc, held_v, hid_v, part_v, sem_in, sem_hid, sem_part = refs[-10:]
        step = pl.program_id(0)

        def source(j):
            k, d = j // len(shifts), shifts[j % len(shifts)]
            return lax.rem(w_ref[0] + (NX - k), NX) * NZ + lax.rem(w_ref[1] + d, NZ)

        fetch = [pltpu.make_async_copy(held_hbm.at[source(j)], held_v.at[j], sem_in.at[j]) for j in range(n)]

        @pl.when(step == 0)
        def _():
            for copy in fetch:
                copy.start()

        contract = (((1,), (1,)), ((), ()))
        a = jnp.concatenate([r[...] for r in lows], 0)
        b = jnp.concatenate([r[...] for r in highs], 0)
        add = lax.dot_general(a, w_low[...], contract, preferred_element_type=F32)
        add += lax.dot_general(b, w_high[...], contract, preferred_element_type=F32)

        @pl.when(step == 0)
        def _():
            acc[...] = add

        @pl.when(step > 0)
        def _():
            acc[...] += add

        @pl.when(step == steps - 1)
        def _():
            half = w_ref[1] // (NZ // 2)
            lane = lax.broadcasted_iota(jnp.int32, (rows, LANES), 1) - META * half
            is_gate = (lane >= 1) & (lane < META)
            gate = jnp.concatenate(
                [
                    jnp.sum(jnp.where(is_gate, m[...].astype(F32), F32(0.0)), axis=1, keepdims=True)
                    for m in metas
                ],
                0,
            )
            proj = acc[...]
            hid_v[...] = (gate * proj).astype(BF).reshape(n, cap, hid)
            for copy in fetch:
                copy.wait()
            held_f = held_v[...].reshape(n * cap, hid).astype(F32)
            scaled_ref[...] = (held_f * gate).T.astype(BF)
            both = held_f * proj
            for j in range(n):
                part_v[j] = jnp.sum(both[j * cap : (j + 1) * cap].T, axis=0, keepdims=True)
            stores = []
            for j in range(n):
                stores.append(pltpu.make_async_copy(hid_v.at[j], hid_hbm.at[source(j)], sem_hid.at[j]))
                stores.append(pltpu.make_async_copy(part_v.at[j], part_hbm.at[source(j)], sem_part.at[j]))
            for copy in stores:
                copy.start()
            for copy in stores:
                copy.wait()

    extra = list(before) if before else []
    first = 1 + 3 * NX + 3
    sources = held.shape[0]
    return call(
        kernel,
        (steps,),
        [columns(rows, TILE, 0)] * NX
        + [columns(rows, TILE, width // 2)] * NX
        + [pl.BlockSpec((rows, LANES), lambda j, w: (0, width // LANES))] * NX
        + [columns(hid, TILE, 0), columns(hid, TILE, width // 2), HBM]
        + [HBM] * len(extra),
        [HBM, HBM, whole((hid, n * cap))],
        [
            jax.ShapeDtypeStruct(held.shape, BF),
            jax.ShapeDtypeStruct((sources, 1, cap), F32),
            jax.ShapeDtypeStruct((hid, n * cap), BF),
        ],
        [
            pltpu.VMEM((n * cap, hid), F32),
            pltpu.VMEM((n, cap, hid), BF),
            pltpu.VMEM((n, cap, hid), BF),
            pltpu.VMEM((n, 1, cap), F32),
            pltpu.SemaphoreType.DMA((n,)),
            pltpu.SemaphoreType.DMA((n,)),
            pltpu.SemaphoreType.DMA((n,)),
        ],
        {first: 0, first + 1: 1} if extra else {},
        flops=2 * n * cap * hid * width,
        nbytes=2 * width * (hid + n * cap),
    )(where, *got, *got, *got, weight, weight, held, *extra)


def weight_grad(where, rows, scaled, width):
    hid = scaled[0].shape[0]
    n, m = len(rows), len(scaled)
    total = sum(r.shape[0] for r in rows)

    def kernel(w_ref, *refs):
        b = jnp.concatenate([r[...] for r in refs[:n]], 0)
        a = jnp.concatenate([r[...] for r in refs[n : n + m]], 1)
        refs[-1][...] = jnp.dot(a, b, preferred_element_type=F32).astype(BF)

    return call(
        kernel,
        (width // WIDE,),
        [columns(r.shape[0], WIDE, 0) for r in rows] + [whole(x.shape) for x in scaled],
        columns(hid, WIDE, 0),
        jax.ShapeDtypeStruct((hid, width), BF),
        flops=2 * total * hid * width,
        nbytes=2 * width * (hid + total),
    )(where, *rows, *scaled)


def finish(where, grad, router, logit):
    rows, width = grad.shape

    def kernel(w_ref, g_ref, r_ref, l_ref, out_ref):
        piece = l_ref[...].astype(F32).T.astype(BF)
        add = jnp.dot(piece, r_ref[...], preferred_element_type=F32)
        out_ref[...] = (g_ref[...].astype(F32) + add).astype(BF)

    return call(
        kernel,
        (2,),
        [columns(rows, width // 2, 0), columns(router.shape[0], width // 2, 0), whole(logit.shape)],
        columns(rows, width // 2, 0),
        jax.ShapeDtypeStruct((rows, width), BF),
        flops=2 * rows * width * router.shape[0],
        nbytes=4 * rows * width,
        vmem=16,
    )(where, grad, router, logit)


def logits(returned, match, after):
    owners, _, cap = returned.shape
    experts = match.shape[0] // cap
    group = owners // experts

    def kernel(r_ref, m_ref, *refs):
        lines = []
        for e in range(experts):
            lines.append(sum(r_ref[e * group + q] for q in range(group)))
        gate = jnp.concatenate([jnp.concatenate(lines, 0)] * experts, 1)
        row = lax.broadcasted_iota(jnp.int32, gate.shape, 0)
        lane = lax.broadcasted_iota(jnp.int32, gate.shape, 1)
        rest = jnp.where(lane // cap == row, gate, F32(0.0))
        for i in range(3):
            piece = rest.astype(BF)
            rest = rest - piece.astype(F32)
            got = jnp.dot(piece, m_ref[...], preferred_element_type=F32)
            refs[-1][i * experts : (i + 1) * experts, :] = got.astype(BF)

    return pl.pallas_call(
        kernel,
        in_specs=[pl.BlockSpec(memory_space=pltpu.VMEM)] * 2 + [HBM] * len(after),
        out_specs=pl.BlockSpec(memory_space=pltpu.VMEM),
        out_shape=jax.ShapeDtypeStruct((3 * experts, match.shape[1]), BF),
    )(returned, match, *after)


def shards(out_grad, router_weight, down_weight, hidden_saved, slot_token, slot_count, slot_gate):
    grad = out_grad[0]
    tokens = slot_token[0, 0]
    counts = slot_count[0, 0]
    gates = slot_gate[0, 0]
    weight = down_weight[0]
    held = hidden_saved[0, 0]
    experts, capacity = tokens.shape
    tok_count, width = grad.shape
    mid = width // 2
    me = lax.axis_index("expert")
    mx, mz = me // NZ, me % NZ
    where = jnp.stack([mx, mz]).astype(jnp.int32)

    where = jnp.concatenate([jnp.stack([mx, mz]).astype(jnp.int32), counts])

    with jax.named_scope("next_section"):
        grad_next = passed_along(grad, "section", -1)
        router_next = passed_along(router_weight[0].T, "section", -1)
        router_next = jnp.concatenate([router_next] * 3, 0)

    def exchanged(rows):
        with jax.named_scope("exchange_x"):
            return [rows[0]] + [lax.ppermute(rows[k], "expert", shift_x(k)) for k in range(1, NX)]

    last = NZ // 2
    order = [[0]] + [[NZ - t, t] for t in range(1, last)] + [[last]]
    with jax.named_scope("pick"):
        block, *rows = begin(where, grad, tokens, gates)
    up = down = block
    arrived, scaled, written = [exchanged(rows)], [], None
    for t in range(1, last + 1):
        with jax.named_scope("ring_z"):
            if t == last:
                up, down = up[:, :mid], down[:, mid:]
            up = lax.ppermute(up, "expert", shift_z(1))
            down = lax.ppermute(down, "expert", shift_z(-1))
        with jax.named_scope("pick"):
            rows = pick_rows(where, [[up], [down]] if t < last else [[up, down]], scaled[t - 2 : t - 1])
            if t < last:
                up, down = hold([up, down], arrived[t - 1][1:] + [rows[0]])
            arrived.append(exchanged(rows))
        with jax.named_scope("project"):
            *written, piece = project(where, arrived[t - 1], weight, held, order[t - 1], written)
        scaled.append(piece)
    with jax.named_scope("project"):
        *written, piece = project(where, arrived[last], weight, held, order[last], written)
    scaled.append(piece)
    hidden_grad, partial = written

    with jax.named_scope("gate_return"):
        returned = lax.all_to_all(partial, "expert", split_axis=0, concat_axis=0, tiled=True)

    with jax.named_scope("weight_grad"):
        down_grad = weight_grad(where, [r for rows in arrived for r in rows], scaled, width)

    with jax.named_scope("input_grad"):
        slots = lax.broadcasted_iota(jnp.int32, (experts, capacity), 1)
        spot = jnp.where(slots < counts[:, None], tokens, -1).reshape(-1, 1)
        match = (spot == lax.broadcasted_iota(jnp.int32, (1, tok_count), 1)).astype(BF)
        logit_grad = logits(returned, match, [down_grad])
        logit_next = passed_along(logit_grad, "section", -1)
        passed = finish(where, grad_next, router_next, logit_next)
    return (down_grad[None], hidden_grad[None, None], passed[None])


def solution(mesh):
    return jax.shard_map(
        shards,
        mesh=mesh,
        in_specs=(
            P("section", "expert", None),
            P("section", None, None),
            P("section", "expert", None),
            P("section", "expert", None, None, None),
            P("section", "expert", None, None),
            P("section", "expert", None),
            P("section", "expert", None, None),
        ),
        out_specs=(
            P("section", "expert", None),
            P("section", "expert", None, None, None),
            P("section", "expert", None),
        ),
        check_vma=False,
    )
```

time: 465 us -> 264 us (0.57)
  waiting for transfers between devices: 335 us -> 118 us
  Pallas kernels: 0 us -> 73.9 us
  blocking collectives: 46.4 us -> 0 us
  starting transfers between devices: 25.2 us -> 60.3 us
  matrix products: 26.4 us -> 0 us
  local copies, waits for them, and re-layouts: 24.3 us -> 7.02 us
    all_to_all x2 -> x1, waiting for transfers between devices: 331 us -> 0.01 us  [shards(): lax.all_to_all(partial, 'expert', split_axis=0, concat_axis=0, tiled=True)]
    ppermute x0 -> x23, waiting for transfers between devices: none -> 117 us  [the longest x4 102 us: shards(): up = lax.ppermute(up, 'expert', shift_z(1))]
    pallas_call x0 -> x16, Pallas kernels: none -> 73.9 us  [the longest x5 32.3 us: project(): call(kernel, (steps,), [columns(rows, TILE, 0)] * NX + [columns(rows, TIL...]
    all_to_all x1 -> x0, blocking collectives: 46.4 us -> none  [shards(): lax.all_to_all(partial_value, 'expert', split_axis=0, concat_axis=0, tile...]
    ppermute x0 -> x23, starting transfers between devices: none -> 37.5 us  [the longest x15 23 us: exchanged(): lax.ppermute(rows[k], 'expert', shift_x(k))]
    dot_general x4 -> x0, matrix products: 26.4 us -> none  [the longest x1 12 us: shards(): jnp.einsum('sch,scd->hd', held, scaled, preferred_element_type=jnp.float32)]
    all_to_all x2 -> x1, starting transfers between devices: 21.3 us -> 7.58 us  [shards(): lax.all_to_all(partial, 'expert', split_axis=0, concat_axis=0, tiled=True)]
    ppermute x1 -> x3, starting transfers between devices: 3.87 us -> 15.2 us  [passed_along(): lax.ppermute(value, axis, [(source, source + steps) for source in range(i...]
  transfers between devices with their start and end apart: 3 -> 27, of which waited for: 2 -> 9; matrix products, arithmetic and copies ran while one was open for 7% -> 2% of each run, Pallas kernels for 0% -> 25%
where the time goes in v1:
time: 264 us
  waiting for transfers between devices  118 us (45%)
  Pallas kernels  73.9 us (28%)
  starting transfers between devices  60.3 us (23%)
  local copies, waits for them, and re-layouts  7.02 us (3%)
  other arithmetic  3.09 us (1%)
    ppermute x4, waiting for transfers between devices, shards(): up = lax.ppermute(up, 'expert', shift_z(1))  102 us
    pallas_call x5, Pallas kernels, project(): call(kernel, (steps,), [columns(rows, TILE, 0)] * NX + [columns(rows, TIL...  32.3 us
    ppermute x15, starting transfers between devices, exchanged(): lax.ppermute(rows[k], 'expert', shift_x(k))  23 us
    pallas_call x4, Pallas kernels, pick_rows(): call(kernel, (1,), [whole(x.shape) for x in flat] + [HBM] * len(after), [...  21.3 us
    ppermute x3, starting transfers between devices, passed_along(): lax.ppermute(value, axis, [(source, source + steps) for source in range(i...  15.2 us
    ppermute x15, waiting for transfers between devices, exchanged(): lax.ppermute(rows[k], 'expert', shift_x(k))  14.5 us
    ppermute x4, starting transfers between devices, shards(): down = lax.ppermute(down, 'expert', shift_z(-1))  10.6 us
    pallas_call x1, Pallas kernels, weight_grad(): call(kernel, (width // WIDE,), [columns(r.shape[0], WIDE, 0) for r in row...  10.3 us
  transfers between devices with their start and end apart: 27, of which 9 were waited for; matrix products, arithmetic and copies ran while one was open for 2% of the time, Pallas kernels for 25%

profile of v1, /device:TPU:1, one launch (start us, length us, event | category | flops | bytes accessed | tf_op | source)
XLA Modules:
  0.0 263.7 jit_solution(10361060511819823667)
XLA Ops:
  1.9 4.8 %pick.8 = (bf16[128,7296]{1,0:T(8,128)(2,1)}, bf16[32,7296]{1,0:T(8,128)(2,1)}, bf16[32,7296]{1,0:T(8,128)(2,1)}, bf16[32,7296]{1,0:T(8,128)(2,1)}, bf16[32,7296]{1,0:T(8,128)(2,1)}) custom-call(s32[10]{0:T(128)} %pad_add_fusion.w_ref, bf16[128,7168]{1,0:T(8,128)(2,1)} %bitcast.3.g_ref, s32[8,32]{1,0:T(8,128)} %bitcast.34, f32[8,32]{1,0:T(8,128)} %bitcast.35), custom_call_target="tpu_custom_call" | custom-call | flops 234881024 | bytes 5505024 | tf_op jit(solution)/shard_map/pick/pallas_call | solution.py:102
  6.7 2.5 collective-permute-start.3
  9.2 3.9 %collective-permute-start.4 = (bf16[128,7296]{1,0:T(8,128)(2,1)}, bf16[128,7296]{1,0:T(8,128)(2,1)}, u32[]{:S(2)}, u32[]{:S(2)}) collective-permute-start(bf16[128,7296]{1,0:T(8,128)(2,1)} %get-tuple-element.49), channel_id=1, source_target_pairs={{0,7},{1,0},{2,1},{3,2},{4,3},{5,4},{6,5},{7,6},{8,15},{9,8},{10,9... | collective-permute-start | bytes 5603336 | tf_op jit(solution)/shard_map/ring_z/ppermute | solution.py:355
  14.3 2.4 collective-permute-start.1
  17.9 35.9 %collective-permute-done.3.refs_0_ = bf16[128,7296]{1,0:T(8,128)(2,1)} collective-permute-done((bf16[128,7296]{1,0:T(8,128)(2,1)}, bf16[128,7296]{1,0:T(8,128)(2,1)}, u32[]{:S(2)}, u32[]{:S(2)}) %collective-permute-start.3) | collective-permute-done | bytes 1867808 | tf_op jit(solution)/shard_map/ring_z/ppermute | solution.py:354
  53.8 5.8 %pick.9 = (bf16[64,7296]{1,0:T(8,128)(2,1)}, bf16[64,7296]{1,0:T(8,128)(2,1)}, bf16[64,7296]{1,0:T(8,128)(2,1)}, bf16[64,7296]{1,0:T(8,128)(2,1)}) custom-call(s32[10]{0:T(128)} %pad_add_fusion.w_ref, bf16[128,7296]{1,0:T(8,128)(2,1)} %collective-permute-done.3.refs_0_, bf16[128,7296]{1,0:T(8,128)(2,1)} %collective-permute-done.4.refs_1_), custom_call_target="tpu_custom_call" | custom-call | flops 478150656 | bytes 7471104 | tf_op jit(solution)/shard_map/pick/pallas_call | solution.py:129
  60.6 2.7 %collective-permute-start.9 = (bf16[128,7296]{1,0:T(8,128)(2,1)}, bf16[128,7296]{1,0:T(8,128)(2,1)}, u32[]{:S(2)}, u32[]{:S(2)}) collective-permute-start(bf16[128,7296]{1,0:T(8,128)(2,1)} %get-tuple-element.55), channel_id=1, source_target_pairs={{0,7},{1,0},{2,1},{3,2},{4,3},{5,4},{6,5},{7,6},{8,15},{9,8},{10,9... | collective-permute-start | bytes 5603336 | tf_op jit(solution)/shard_map/ring_z/ppermute | solution.py:355
  64.5 2.5 collective-permute-start.6
  68.1 5.9 %project.5 = (bf16[32,32,256]{2,1,0:T(8,128)(2,1)}, f32[32,1,32]{2,1,0:T(1,128)}, bf16[256,128]{1,0:T(8,128)(2,1)}) custom-call(s32[10]{0:T(128)} %pad_add_fusion.w_ref, bf16[32,7296]{1,0:T(8,128)(2,1)} %get-tuple-element.45.refs_0_.refs_4_.refs_8_, bf16[32,7296]{1,0:T(8,128)(2,1)} %copy-done.4, bf16[32,7296]{1,0:T(8,128)(2,1)} %copy-done.5, ...), custom_call_target="tpu_custom_call" | custom-call | flops 469762048 | bytes 5505024 | tf_op jit(solution)/shard_map/project/pallas_call | solution.py:222
  74.0 29.1 %collective-permute-done.8.refs_0_ = bf16[128,7296]{1,0:T(8,128)(2,1)} collective-permute-done((bf16[128,7296]{1,0:T(8,128)(2,1)}, bf16[128,7296]{1,0:T(8,128)(2,1)}, u32[]{:S(2)}, u32[]{:S(2)}) %collective-permute-start.8) | collective-permute-done | bytes 1867808 | tf_op jit(solution)/shard_map/ring_z/ppermute | solution.py:354
  103.1 5.7 %pick.11 = (bf16[64,7296]{1,0:T(8,128)(2,1)}, bf16[64,7296]{1,0:T(8,128)(2,1)}, bf16[64,7296]{1,0:T(8,128)(2,1)}, bf16[64,7296]{1,0:T(8,128)(2,1)}) custom-call(s32[10]{0:T(128)} %pad_add_fusion.w_ref, bf16[128,7296]{1,0:T(8,128)(2,1)} %collective-permute-done.8.refs_0_, bf16[128,7296]{1,0:T(8,128)(2,1)} %collective-permute-done.9.refs_1_, ...), custom_call_target="tpu_custom_call" | custom-call | flops 478150656 | bytes 7471104 | tf_op jit(solution)/shard_map/pick/pallas_call | solution.py:129
  113.6 2.5 collective-permute-start.11
  117.2 6.8 %project.6 = (bf16[32,32,256]{2,1,0:T(8,128)(2,1)}, f32[32,1,32]{2,1,0:T(1,128)}, bf16[256,256]{1,0:T(8,128)(2,1)}) custom-call(s32[10]{0:T(128)} %pad_add_fusion.w_ref, bf16[64,7296]{1,0:T(8,128)(2,1)} %get-tuple-element.50.refs_5_.refs_0_.refs_4_.refs_8_, bf16[64,7296]{1,0:T(8,128)(2,1)} %copy-done.1, ...), custom_call_target="tpu_custom_call", output_to_operand_aliasing={{0}: (16, {}), {1}: (17, {})} | custom-call | flops 939524096 | bytes 7340032 | tf_op jit(solution)/shard_map/project/pallas_call | solution.py:222
  124.0 27.3 %collective-permute-done.13.refs_0_ = bf16[128,7296]{1,0:T(8,128)(2,1)} collective-permute-done((bf16[128,7296]{1,0:T(8,128)(2,1)}, bf16[128,7296]{1,0:T(8,128)(2,1)}, u32[]{:S(2)}, u32[]{:S(2)}) %collective-permute-start.13) | collective-permute-done | bytes 1867808 | tf_op jit(solution)/shard_map/ring_z/ppermute | solution.py:354
  151.3 5.7 %pick.13 = (bf16[64,7296]{1,0:T(8,128)(2,1)}, bf16[64,7296]{1,0:T(8,128)(2,1)}, bf16[64,7296]{1,0:T(8,128)(2,1)}, bf16[64,7296]{1,0:T(8,128)(2,1)}) custom-call(s32[10]{0:T(128)} %pad_add_fusion.w_ref, bf16[128,7296]{1,0:T(8,128)(2,1)} %collective-permute-done.13.refs_0_, bf16[128,7296]{1,0:T(8,128)(2,1)} %collective-permute-done.14.refs_1_, ...), custom_call_target="tpu_custom_call" | custom-call | flops 478150656 | bytes 7471104 | tf_op jit(solution)/shard_map/pick/pallas_call | solution.py:129
  159.8 2.2 slice.7
  162.0 2.2 collective-permute-start.19
  165.4 2.5 collective-permute-start.16
  169.3 10.1 %collective-permute-done.18.refs_0_ = bf16[128,3584]{1,0:T(8,128)(2,1)} collective-permute-done((bf16[128,3584]{1,0:T(8,128)(2,1)S(1)}, bf16[128,3584]{1,0:T(8,128)(2,1)}, u32[]{:S(2)}, u32[]{:S(2)}) %collective-permute-start.18) | collective-permute-done | bytes 917536 | tf_op jit(solution)/shard_map/ring_z/ppermute | solution.py:354
  179.4 5.9 %collective-permute-start.23 = (bf16[128,7168]{1,0:T(8,128)(2,1)}, bf16[128,7168]{1,0:T(8,128)(2,1)}, u32[]{:S(2)}, u32[]{:S(2)}) collective-permute-start(bf16[128,7168]{1,0:T(8,128)(2,1)} %bitcast.3.g_ref), channel_id=1, source_target_pairs={{32,0},{64,32},{96,64},{128,96},{160,128},{192,160},{224,192},{33,... | collective-permute-start | bytes 5505032 | tf_op jit(solution)/shard_map/next_section/ppermute | solution.py:27
  185.4 6.8 %project.7 = (bf16[32,32,256]{2,1,0:T(8,128)(2,1)}, f32[32,1,32]{2,1,0:T(1,128)}, bf16[256,256]{1,0:T(8,128)(2,1)}) custom-call(s32[10]{0:T(128)} %pad_add_fusion.w_ref, bf16[64,7296]{1,0:T(8,128)(2,1)} %get-tuple-element.57.refs_5_.refs_0_.refs_4_.refs_8_, bf16[64,7296]{1,0:T(8,128)(2,1)} %copy-done.2, ...), custom_call_target="tpu_custom_call", output_to_operand_aliasing={{0}: (16, {}), {1}: (17, {})} | custom-call | flops 939524096 | bytes 7340032 | tf_op jit(solution)/shard_map/project/pallas_call | solution.py:222
  192.2 4.1 %pick.15 = (bf16[32,7296]{1,0:T(8,128)(2,1)}, bf16[32,7296]{1,0:T(8,128)(2,1)}, bf16[32,7296]{1,0:T(8,128)(2,1)}, bf16[32,7296]{1,0:T(8,128)(2,1)}) custom-call(s32[10]{0:T(128)} %pad_add_fusion.w_ref, bf16[128,3584]{1,0:T(8,128)(2,1)} %collective-permute-done.18.refs_0_, bf16[128,3712]{1,0:T(8,128)(2,1)} %collective-permute-done.19.refs_1_, ...), custom_call_target="tpu_custom_call" | custom-call | flops 239075328 | bytes 3735552 | tf_op jit(solution)/shard_map/pick/pallas_call | solution.py:129
  197.5 2.5 collective-permute-start.21
  199.9 5.4 %collective-permute-done.16.refs_2_.refs_6_.refs_10_.refs_14_ = bf16[64,7296]{1,0:T(8,128)(2,1)} collective-permute-done((bf16[64,7296]{1,0:T(8,128)(2,1)}, bf16[64,7296]{1,0:T(8,128)(2,1)}, u32[]{:S(2)}, u32[]{:S(2)}) %collective-permute-start.16) | collective-permute-done | bytes 933920 | tf_op jit(solution)/shard_map/pick/exchange_x/ppermute | solution.py:342
  206.1 5.6 %collective-permute-done.17.refs_3_.refs_7_.refs_11_.refs_15_ = bf16[64,7296]{1,0:T(8,128)(2,1)} collective-permute-done((bf16[64,7296]{1,0:T(8,128)(2,1)}, bf16[64,7296]{1,0:T(8,128)(2,1)}, u32[]{:S(2)}, u32[]{:S(2)}) %collective-permute-start.17) | collective-permute-done | bytes 933920 | tf_op jit(solution)/shard_map/pick/exchange_x/ppermute | solution.py:342
  211.7 5.2 %collective-permute-start.24 = (bf16[8,7168]{1,0:T(8,128)(2,1)}, bf16[8,7168]{1,0:T(8,128)(2,1)}, u32[]{:S(2)}, u32[]{:S(2)}) collective-permute-start(bf16[8,7168]{1,0:T(8,128)(2,1)} %bitcast.38), channel_id=1, source_target_pairs={{32,0},{64,32},{96,64},{128,96},{160,128},{192,160},{224,192},{33,... | collective-permute-start | bytes 344072 | tf_op jit(solution)/shard_map/next_section/ppermute | solution.py:27
  217.0 6.8 %project.8 = (bf16[32,32,256]{2,1,0:T(8,128)(2,1)}, f32[32,1,32]{2,1,0:T(1,128)}, bf16[256,256]{1,0:T(8,128)(2,1)}) custom-call(s32[10]{0:T(128)} %pad_add_fusion.w_ref, bf16[64,7296]{1,0:T(8,128)(2,1)} %get-tuple-element.66.refs_5_.refs_0_.refs_4_.refs_8_.refs_12_, bf16[64,7296]{1,0:T(8,128)(2,1)} %copy-done.3, ...), custom_call_target="tpu_custom_call", output_to_operand_aliasing={{0}: (16, {}), {1}: (17, {})} | custom-call | flops 939524096 | bytes 7340032 | tf_op jit(solution)/shard_map/project/pallas_call | solution.py:222
  227.2 5.9 %project.9 = (bf16[32,32,256]{2,1,0:T(8,128)(2,1)}, f32[32,1,32]{2,1,0:T(1,128)}, bf16[256,128]{1,0:T(8,128)(2,1)}) custom-call(s32[10]{0:T(128)} %pad_add_fusion.w_ref, bf16[32,7296]{1,0:T(8,128)(2,1)} %get-tuple-element.75.refs_0_.refs_4_.refs_8_.refs_16_, ...), custom_call_target="tpu_custom_call", output_to_operand_aliasing={{0}: (16, {}), {1}: (17, {})} | custom-call | flops 469762048 | bytes 5505024 | tf_op jit(solution)/shard_map/project/pallas_call | solution.py:222
  233.2 7.6 %all-to-all-start = ((f32[32,1,32]{2,1,0:T(1,128)}), f32[32,1,32]{2,1,0:T(1,128)S(1)}, u32[]{:S(2)}, u32[]{:S(2)}) async-start(f32[32,1,32]{2,1,0:T(1,128)} %get-tuple-element.86), calls=%async_computation | async-start | bytes 32768 | tf_op jit(solution)/shard_map/gate_return/all_to_all | solution.py:370
  240.8 10.3 %weight_grad.1.refs_0_ = bf16[256,7168]{1,0:T(8,128)(2,1)} custom-call(s32[10]{0:T(128)} %pad_add_fusion.w_ref, bf16[32,7296]{1,0:T(8,128)(2,1)} %get-tuple-element.45.refs_0_.refs_4_.refs_8_, bf16[32,7296]{1,0:T(8,128)(2,1)} %copy-done.4, bf16[32,7296]{1,0:T(8,128)(2,1)} %copy-done.5, ...), custom_call_target="tpu_custom_call" | custom-call | flops 3758096384 | bytes 18350080 | tf_op jit(solution)/shard_map/weight_grad/pallas_call | solution.py:261
  253.3 4.1 %collective-permute-start.25 = (bf16[24,128]{1,0:T(8,128)(2,1)}, bf16[24,128]{1,0:T(8,128)(2,1)S(1)}, u32[]{:S(2)}, u32[]{:S(2)}) collective-permute-start(bf16[24,128]{1,0:T(8,128)(2,1)} %input_grad.2), channel_id=1, source_target_pairs={{32,0},{64,32},{96,64},{128,96},{160,128},{192,160},{224,192},{33,... | collective-permute-start | bytes 18440 | tf_op jit(solution)/shard_map/input_grad/ppermute | solution.py:27
  260.1 3.6 %input_grad.3 = bf16[128,7168]{1,0:T(8,128)(2,1)} custom-call(s32[10]{0:T(128)S(1)} %copy-done, bf16[128,7168]{1,0:T(8,128)(2,1)} %collective-permute-done.23.g_ref, bf16[24,7168]{1,0:T(8,128)(2,1)S(1)} %pad_maximum_fusion.r_ref, bf16[24,128]{1,0:T(8,128)(2,1)S(1)} %collective-permute-done.25.l_ref), custom_call_target="tpu_custom_call" | custom-call | flops 44040192 | bytes 3670016 | tf_op jit(solution)/shard_map/input_grad/pallas_call | solution.py:280
  (65 shorter events, 28.5 us)
Async XLA Ops:
  6.7 47.2 %collective-permute-start.3 = (bf16[128,7296]{1,0:T(8,128)(2,1)}, bf16[128,7296]{1,0:T(8,128)(2,1)}, u32[]{:S(2)}, u32[]{:S(2)}) collective-permute-start(bf16[128,7296]{1,0:T(8,128)(2,1)} %get-tuple-element.49), channel_id=1, source_target_pairs={{0,1},{1,2},{2,3},{3,4},{4,5},{5,6},{6,7},{7,0},{8,9},{9,10},{10,1... | collective-permute-start | bytes 5603336 | tf_op jit(solution)/shard_map/ring_z/ppermute | solution.py:354
  9.2 44.7 %collective-permute-start.4 = (bf16[128,7296]{1,0:T(8,128)(2,1)}, bf16[128,7296]{1,0:T(8,128)(2,1)}, u32[]{:S(2)}, u32[]{:S(2)}) collective-permute-start(bf16[128,7296]{1,0:T(8,128)(2,1)} %get-tuple-element.49), channel_id=1, source_target_pairs={{0,7},{1,0},{2,1},{3,2},{4,3},{5,4},{6,5},{7,6},{8,15},{9,8},{10,9... | collective-permute-start | bytes 5603336 | tf_op jit(solution)/shard_map/ring_z/ppermute | solution.py:355
  13.1 46.6 %collective-permute-start = (bf16[32,7296]{1,0:T(8,128)(2,1)}, bf16[32,7296]{1,0:T(8,128)(2,1)S(1)}, u32[]{:S(2)}, u32[]{:S(2)}) collective-permute-start(bf16[32,7296]{1,0:T(8,128)(2,1)} %get-tuple-element.46), channel_id=1, source_target_pairs={{0,8},{1,9},{2,10},{3,11},{4,12},{5,13},{6,14},{7,15},{8,16},{9,17... | collective-permute-start | bytes 1400840 | tf_op jit(solution)/shard_map/exchange_x/ppermute | solution.py:342
  14.3 45.3 %collective-permute-start.1 = (bf16[32,7296]{1,0:T(8,128)(2,1)}, bf16[32,7296]{1,0:T(8,128)(2,1)S(1)}, u32[]{:S(2)}, u32[]{:S(2)}) collective-permute-start(bf16[32,7296]{1,0:T(8,128)(2,1)} %get-tuple-element.47), channel_id=1, source_target_pairs={{0,16},{1,17},{2,18},{3,19},{4,20},{5,21},{6,22},{7,23},{8,24},{9,... | collective-permute-start | bytes 1400840 | tf_op jit(solution)/shard_map/exchange_x/ppermute | solution.py:342
  16.8 42.9 %collective-permute-start.2 = (bf16[32,7296]{1,0:T(8,128)(2,1)}, bf16[32,7296]{1,0:T(8,128)(2,1)}, u32[]{:S(2)}, u32[]{:S(2)}) collective-permute-start(bf16[32,7296]{1,0:T(8,128)(2,1)} %get-tuple-element.48), channel_id=1, source_target_pairs={{0,24},{1,25},{2,26},{3,27},{4,28},{5,29},{6,30},{7,31},{8,0},{9,1... | collective-permute-start | bytes 1400840 | tf_op jit(solution)/shard_map/exchange_x/ppermute | solution.py:342
  60.6 42.5 %collective-permute-start.8 = (bf16[128,7296]{1,0:T(8,128)(2,1)}, bf16[128,7296]{1,0:T(8,128)(2,1)}, u32[]{:S(2)}, u32[]{:S(2)}) collective-permute-start(bf16[128,7296]{1,0:T(8,128)(2,1)} %get-tuple-element.54), channel_id=1, source_target_pairs={{0,1},{1,2},{2,3},{3,4},{4,5},{5,6},{6,7},{7,0},{8,9},{9,10},{10,1... | collective-permute-start | bytes 5603336 | tf_op jit(solution)/shard_map/ring_z/ppermute | solution.py:354
  60.6 42.5 %collective-permute-start.9 = (bf16[128,7296]{1,0:T(8,128)(2,1)}, bf16[128,7296]{1,0:T(8,128)(2,1)}, u32[]{:S(2)}, u32[]{:S(2)}) collective-permute-start(bf16[128,7296]{1,0:T(8,128)(2,1)} %get-tuple-element.55), channel_id=1, source_target_pairs={{0,7},{1,0},{2,1},{3,2},{4,3},{5,4},{6,5},{7,6},{8,15},{9,8},{10,9... | collective-permute-start | bytes 5603336 | tf_op jit(solution)/shard_map/ring_z/ppermute | solution.py:355
  63.3 45.5 %collective-permute-start.5 = (bf16[64,7296]{1,0:T(8,128)(2,1)}, bf16[64,7296]{1,0:T(8,128)(2,1)S(1)}, u32[]{:S(2)}, u32[]{:S(2)}) collective-permute-start(bf16[64,7296]{1,0:T(8,128)(2,1)} %get-tuple-element.51), channel_id=1, source_target_pairs={{0,8},{1,9},{2,10},{3,11},{4,12},{5,13},{6,14},{7,15},{8,16},{9,17... | collective-permute-start | bytes 2801672 | tf_op jit(solution)/shard_map/pick/exchange_x/ppermute | solution.py:342
  64.5 44.3 %collective-permute-start.6 = (bf16[64,7296]{1,0:T(8,128)(2,1)}, bf16[64,7296]{1,0:T(8,128)(2,1)}, u32[]{:S(2)}, u32[]{:S(2)}) collective-permute-start(bf16[64,7296]{1,0:T(8,128)(2,1)} %get-tuple-element.52), channel_id=1, source_target_pairs={{0,16},{1,17},{2,18},{3,19},{4,20},{5,21},{6,22},{7,23},{8,24},{9,... | collective-permute-start | bytes 2801672 | tf_op jit(solution)/shard_map/pick/exchange_x/ppermute | solution.py:342
  66.9 41.9 %collective-permute-start.7 = (bf16[64,7296]{1,0:T(8,128)(2,1)}, bf16[64,7296]{1,0:T(8,128)(2,1)}, u32[]{:S(2)}, u32[]{:S(2)}) collective-permute-start(bf16[64,7296]{1,0:T(8,128)(2,1)} %get-tuple-element.53), channel_id=1, source_target_pairs={{0,24},{1,25},{2,26},{3,27},{4,28},{5,29},{6,30},{7,31},{8,0},{9,1... | collective-permute-start | bytes 2801672 | tf_op jit(solution)/shard_map/pick/exchange_x/ppermute | solution.py:342
  109.7 41.6 %collective-permute-start.13 = (bf16[128,7296]{1,0:T(8,128)(2,1)}, bf16[128,7296]{1,0:T(8,128)(2,1)}, u32[]{:S(2)}, u32[]{:S(2)}) collective-permute-start(bf16[128,7296]{1,0:T(8,128)(2,1)} %get-tuple-element.61), channel_id=1, source_target_pairs={{0,1},{1,2},{2,3},{3,4},{4,5},{5,6},{6,7},{7,0},{8,9},{9,10},{10,1... | collective-permute-start | bytes 5603336 | tf_op jit(solution)/shard_map/ring_z/ppermute | solution.py:354
  110.6 40.7 %collective-permute-start.14 = (bf16[128,7296]{1,0:T(8,128)(2,1)}, bf16[128,7296]{1,0:T(8,128)(2,1)}, u32[]{:S(2)}, u32[]{:S(2)}) collective-permute-start(bf16[128,7296]{1,0:T(8,128)(2,1)} %get-tuple-element.62), channel_id=1, source_target_pairs={{0,7},{1,0},{2,1},{3,2},{4,3},{5,4},{6,5},{7,6},{8,15},{9,8},{10,9... | collective-permute-start | bytes 5603336 | tf_op jit(solution)/shard_map/ring_z/ppermute | solution.py:355
  112.4 44.7 %collective-permute-start.10 = (bf16[64,7296]{1,0:T(8,128)(2,1)}, bf16[64,7296]{1,0:T(8,128)(2,1)S(1)}, u32[]{:S(2)}, u32[]{:S(2)}) collective-permute-start(bf16[64,7296]{1,0:T(8,128)(2,1)} %get-tuple-element.58), channel_id=1, source_target_pairs={{0,8},{1,9},{2,10},{3,11},{4,12},{5,13},{6,14},{7,15},{8,16},{9,17... | collective-permute-start | bytes 2801672 | tf_op jit(solution)/shard_map/pick/exchange_x/ppermute | solution.py:342
  113.6 43.5 %collective-permute-start.11 = (bf16[64,7296]{1,0:T(8,128)(2,1)}, bf16[64,7296]{1,0:T(8,128)(2,1)}, u32[]{:S(2)}, u32[]{:S(2)}) collective-permute-start(bf16[64,7296]{1,0:T(8,128)(2,1)} %get-tuple-element.59), channel_id=1, source_target_pairs={{0,16},{1,17},{2,18},{3,19},{4,20},{5,21},{6,22},{7,23},{8,24},{9,... | collective-permute-start | bytes 2801672 | tf_op jit(solution)/shard_map/pick/exchange_x/ppermute | solution.py:342
  116.1 41.0 %collective-permute-start.12 = (bf16[64,7296]{1,0:T(8,128)(2,1)}, bf16[64,7296]{1,0:T(8,128)(2,1)}, u32[]{:S(2)}, u32[]{:S(2)}) collective-permute-start(bf16[64,7296]{1,0:T(8,128)(2,1)} %get-tuple-element.60), channel_id=1, source_target_pairs={{0,24},{1,25},{2,26},{3,27},{4,28},{5,29},{6,30},{7,31},{8,0},{9,1... | collective-permute-start | bytes 2801672 | tf_op jit(solution)/shard_map/pick/exchange_x/ppermute | solution.py:342
  157.1 1.0 copy-start.2
  158.0 11.0 %copy-start.7 = (s32[1,1,8,32]{3,2,1,0:T(8,128)S(1)}, s32[1,1,8,32]{3,2,1,0:T(8,128)}, u32[]{:S(2)}) copy-start(s32[1,1,8,32]{3,2,1,0:T(8,128)} %param.11) | copy-start | bytes 3076
  158.0 11.1 %copy-start.8 = (s32[1,1,8]{2,1,0:T(1,128)S(1)}, s32[1,1,8]{2,1,0:T(1,128)}, u32[]{:S(2)}) copy-start(s32[1,1,8]{2,1,0:T(1,128)} %param.12) | copy-start | bytes 100
  159.3 20.1 %collective-permute-start.18 = (bf16[128,3584]{1,0:T(8,128)(2,1)S(1)}, bf16[128,3584]{1,0:T(8,128)(2,1)}, u32[]{:S(2)}, u32[]{:S(2)}) collective-permute-start(bf16[128,3584]{1,0:T(8,128)(2,1)S(1)} %slice.6), channel_id=1, source_target_pairs={{0,1},{1,2},{2,3},{3,4},{4,5},{5,6},{6,7},{7,0},{8,9},{9,10},{10,1... | collective-permute-start | bytes 2752520 | tf_op jit(solution)/shard_map/ring_z/ppermute | solution.py:354
  162.0 30.2 %collective-permute-start.19 = (bf16[128,3712]{1,0:T(8,128)(2,1)}, bf16[128,3712]{1,0:T(8,128)(2,1)}, u32[]{:S(2)}, u32[]{:S(2)}) collective-permute-start(bf16[128,3712]{1,0:T(8,128)(2,1)} %slice.7), channel_id=1, source_target_pairs={{0,7},{1,0},{2,1},{3,2},{4,3},{5,4},{6,5},{7,6},{8,15},{9,8},{10,9... | collective-permute-start | bytes 2850824 | tf_op jit(solution)/shard_map/ring_z/ppermute | solution.py:355
  164.2 33.2 %collective-permute-start.15 = (bf16[64,7296]{1,0:T(8,128)(2,1)}, bf16[64,7296]{1,0:T(8,128)(2,1)S(1)}, u32[]{:S(2)}, u32[]{:S(2)}) collective-permute-start(bf16[64,7296]{1,0:T(8,128)(2,1)} %get-tuple-element.67), channel_id=1, source_target_pairs={{0,8},{1,9},{2,10},{3,11},{4,12},{5,13},{6,14},{7,15},{8,16},{9,17... | collective-permute-start | bytes 2801672 | tf_op jit(solution)/shard_map/pick/exchange_x/ppermute | solution.py:342
  165.4 39.9 %collective-permute-start.16 = (bf16[64,7296]{1,0:T(8,128)(2,1)}, bf16[64,7296]{1,0:T(8,128)(2,1)}, u32[]{:S(2)}, u32[]{:S(2)}) collective-permute-start(bf16[64,7296]{1,0:T(8,128)(2,1)} %get-tuple-element.68), channel_id=1, source_target_pairs={{0,16},{1,17},{2,18},{3,19},{4,20},{5,21},{6,22},{7,23},{8,24},{9,... | collective-permute-start | bytes 2801672 | tf_op jit(solution)/shard_map/pick/exchange_x/ppermute | solution.py:342
  167.9 43.8 %collective-permute-start.17 = (bf16[64,7296]{1,0:T(8,128)(2,1)}, bf16[64,7296]{1,0:T(8,128)(2,1)}, u32[]{:S(2)}, u32[]{:S(2)}) collective-permute-start(bf16[64,7296]{1,0:T(8,128)(2,1)} %get-tuple-element.69), channel_id=1, source_target_pairs={{0,24},{1,25},{2,26},{3,27},{4,28},{5,29},{6,30},{7,31},{8,0},{9,1... | collective-permute-start | bytes 2801672 | tf_op jit(solution)/shard_map/pick/exchange_x/ppermute | solution.py:342
  179.4 79.1 %collective-permute-start.23 = (bf16[128,7168]{1,0:T(8,128)(2,1)}, bf16[128,7168]{1,0:T(8,128)(2,1)}, u32[]{:S(2)}, u32[]{:S(2)}) collective-permute-start(bf16[128,7168]{1,0:T(8,128)(2,1)} %bitcast.3.g_ref), channel_id=1, source_target_pairs={{32,0},{64,32},{96,64},{128,96},{160,128},{192,160},{224,192},{33,... | collective-permute-start | bytes 5505032 | tf_op jit(solution)/shard_map/next_section/ppermute | solution.py:27
  196.3 27.5 %collective-permute-start.20 = (bf16[32,7296]{1,0:T(8,128)(2,1)}, bf16[32,7296]{1,0:T(8,128)(2,1)}, u32[]{:S(2)}, u32[]{:S(2)}) collective-permute-start(bf16[32,7296]{1,0:T(8,128)(2,1)} %get-tuple-element.76), channel_id=1, source_target_pairs={{0,8},{1,9},{2,10},{3,11},{4,12},{5,13},{6,14},{7,15},{8,16},{9,17... | collective-permute-start | bytes 1400840 | tf_op jit(solution)/shard_map/pick/exchange_x/ppermute | solution.py:342
  197.5 19.5 %copy-start.3 = (bf16[64,7296]{1,0:T(8,128)(2,1)}, bf16[64,7296]{1,0:T(8,128)(2,1)S(1)}, u32[]{:S(2)}) copy-start(bf16[64,7296]{1,0:T(8,128)(2,1)S(1)} %collective-permute-done.15.refs_1_.refs_5_.refs_9_.refs_13_) | copy-start | bytes 2801668
  197.5 27.9 %collective-permute-start.21 = (bf16[32,7296]{1,0:T(8,128)(2,1)}, bf16[32,7296]{1,0:T(8,128)(2,1)}, u32[]{:S(2)}, u32[]{:S(2)}) collective-permute-start(bf16[32,7296]{1,0:T(8,128)(2,1)} %get-tuple-element.77), channel_id=1, source_target_pairs={{0,16},{1,17},{2,18},{3,19},{4,20},{5,21},{6,22},{7,23},{8,24},{9,... | collective-permute-start | bytes 1400840 | tf_op jit(solution)/shard_map/pick/exchange_x/ppermute | solution.py:342
  205.4 21.9 %collective-permute-start.22 = (bf16[32,7296]{1,0:T(8,128)(2,1)}, bf16[32,7296]{1,0:T(8,128)(2,1)}, u32[]{:S(2)}, u32[]{:S(2)}) collective-permute-start(bf16[32,7296]{1,0:T(8,128)(2,1)} %get-tuple-element.78), channel_id=1, source_target_pairs={{0,24},{1,25},{2,26},{3,27},{4,28},{5,29},{6,30},{7,31},{8,0},{9,1... | collective-permute-start | bytes 1400840 | tf_op jit(solution)/shard_map/pick/exchange_x/ppermute | solution.py:342
  211.7 45.7 %collective-permute-start.24 = (bf16[8,7168]{1,0:T(8,128)(2,1)}, bf16[8,7168]{1,0:T(8,128)(2,1)}, u32[]{:S(2)}, u32[]{:S(2)}) collective-permute-start(bf16[8,7168]{1,0:T(8,128)(2,1)} %bitcast.38), channel_id=1, source_target_pairs={{32,0},{64,32},{96,64},{128,96},{160,128},{192,160},{224,192},{33,... | collective-permute-start | bytes 344072 | tf_op jit(solution)/shard_map/next_section/ppermute | solution.py:27
  233.2 17.9 %all-to-all-start = ((f32[32,1,32]{2,1,0:T(1,128)}), f32[32,1,32]{2,1,0:T(1,128)S(1)}, u32[]{:S(2)}, u32[]{:S(2)}) async-start(f32[32,1,32]{2,1,0:T(1,128)} %get-tuple-element.86), calls=%async_computation | async-start | bytes 32768 | tf_op jit(solution)/shard_map/gate_return/all_to_all | solution.py:370
  251.1 9.0 %copy-start = (s32[10]{0:T(128)S(1)}, s32[10]{0:T(128)}, u32[]{:S(2)}) copy-start(s32[10]{0:T(128)} %pad_add_fusion.w_ref) | copy-start | bytes 124
  253.3 6.8 %collective-permute-start.25 = (bf16[24,128]{1,0:T(8,128)(2,1)}, bf16[24,128]{1,0:T(8,128)(2,1)S(1)}, u32[]{:S(2)}, u32[]{:S(2)}) collective-permute-start(bf16[24,128]{1,0:T(8,128)(2,1)} %input_grad.2), channel_id=1, source_target_pairs={{32,0},{64,32},{96,64},{128,96},{160,128},{192,160},{224,192},{33,... | collective-permute-start | bytes 18440 | tf_op jit(solution)/shard_map/input_grad/ppermute | solution.py:27
  (4 other events, 3.3 us)

commit v2 on v1

--- a/solution.py
+++ b/solution.py
@@ -77,9 +77,7 @@
     count, width = grad.shape
     cap = tokens.shape[1]
 
-    def kernel(w_ref, g_ref, t_ref, s_ref, block_ref, *outs):
-        block_ref[:, :width] = g_ref[...]
-        block_ref[:, width:] = jnp.zeros((count, LANES), BF)
+    def kernel(w_ref, g_ref, t_ref, s_ref, meta_ref, *outs):
         slot = lax.broadcasted_iota(jnp.int32, (1, cap), 1)
         for k in range(NX):
             lines = []
@@ -95,46 +93,53 @@
             table = jnp.concatenate(lines, 0)
             table = jnp.concatenate([table, jnp.zeros((2 * META, LANES - cap), F32)], 1)
             table = jnp.concatenate([table, jnp.zeros((LANES - 2 * META, LANES), F32)], 0).T
-            block_ref[k * cap : (k + 1) * cap, width:] = table[:cap].astype(BF)
-        picked(w_ref, block_ref[:, width:], [g_ref], outs, 0)
+            for z in range(NZ):
+                meta_ref[z, k * cap : (k + 1) * cap, :] = table[:cap].astype(BF)
+        picked(w_ref, meta_ref[0], [g_ref], outs, 0)
 
     full = width + LANES
     return call(
         kernel,
         (1,),
         [whole(x.shape) for x in (grad, tokens, gates)],
-        [whole((count, full))] + [whole((cap, full))] * NX,
-        [jax.ShapeDtypeStruct((count, full), BF)] + [jax.ShapeDtypeStruct((cap, full), BF)] * NX,
+        [whole((NZ, NX * cap, LANES))] + [whole((cap, full))] * NX,
+        [jax.ShapeDtypeStruct((NZ, NX * cap, LANES), BF)] + [jax.ShapeDtypeStruct((cap, full), BF)] * NX,
         flops=2 * NX * cap * count * width,
         nbytes=6 * count * width,
     )(where, grad, tokens, gates)
 
 
-def pick_rows(where, blocks, after):
+def pick_rows(where, blocks, metas, places, after, cut):
     n = len(blocks)
     flat = [x for block in blocks for x in block]
     tokens = flat[0].shape[0]
-    full = sum(x.shape[1] for x in blocks[0])
-    cap = tokens // NX
+    width = sum(x.shape[1] for x in blocks[0])
+    slots = metas.shape[1]
+    cap = slots // NX
+    mid = width // 2
+    cuts = 2 if cut else 0
 
     def kernel(w_ref, *refs):
-        outs = refs[-NX:]
+        outs = refs[len(refs) - NX - cuts :]
         for b in range(n):
-            parts = list(refs[b * len(blocks[b]) : (b + 1) * len(blocks[b])])
-            cut = parts[-1].shape[1] - LANES
-            meta = parts[-1][:, cut:]
-            parts[-1] = parts[-1].at[:, :cut]
-            picked(w_ref, meta, parts, outs, b * cap)
-
+            parts = refs[b * len(blocks[b]) : (b + 1) * len(blocks[b])]
+            picked(w_ref, refs[len(flat) + b][0], parts, outs[:NX], b * cap)
+        if cut:
+            outs[NX][...] = refs[0][:, :mid]
+            outs[NX + 1][...] = refs[1][:, mid:]
+
+    shapes = [(n * cap, width + LANES)] * NX + [(tokens, mid)] * cuts
     return call(
         kernel,
         (1,),
-        [whole(x.shape) for x in flat] + [HBM] * len(after),
-        [whole((n * cap, full))] * NX,
-        [jax.ShapeDtypeStruct((n * cap, full), BF)] * NX,
-        flops=2 * n * tokens * tokens * full,
-        nbytes=4 * n * tokens * full,
-    )(where, *flat, *after)
+        [whole(x.shape) for x in flat]
+        + [pl.BlockSpec((1, slots, LANES), lambda j, w, d=d: (lax.rem(w[1] + d, NZ), 0, 0)) for d in places]
+        + [HBM] * len(after),
+        [whole(x) for x in shapes],
+        [jax.ShapeDtypeStruct(x, BF) for x in shapes],
+        flops=2 * n * slots * tokens * width,
+        nbytes=4 * n * tokens * width,
+    )(where, *flat, *[metas] * n, *after)
 
 
 def hold(arrays, after):
@@ -325,7 +330,6 @@
     held = hidden_saved[0, 0]
     experts, capacity = tokens.shape
     tok_count, width = grad.shape
-    mid = width // 2
     me = lax.axis_index("expert")
     mx, mz = me // NZ, me % NZ
     where = jnp.stack([mx, mz]).astype(jnp.int32)
@@ -344,19 +348,23 @@
     last = NZ // 2
     order = [[0]] + [[NZ - t, t] for t in range(1, last)] + [[last]]
     with jax.named_scope("pick"):
-        block, *rows = begin(where, grad, tokens, gates)
-    up = down = block
+        spread, *rows = begin(where, grad, tokens, gates)
+        line = [[x * NZ + z for z in range(NZ)] for x in range(NX)]
+        metas = lax.all_to_all(
+            spread, "expert", split_axis=0, concat_axis=0, axis_index_groups=line, tiled=True
+        )
+    up = down = grad
     arrived, scaled, written = [exchanged(rows)], [], None
     for t in range(1, last + 1):
         with jax.named_scope("ring_z"):
-            if t == last:
-                up, down = up[:, :mid], down[:, mid:]
             up = lax.ppermute(up, "expert", shift_z(1))
             down = lax.ppermute(down, "expert", shift_z(-1))
         with jax.named_scope("pick"):
-            rows = pick_rows(where, [[up], [down]] if t < last else [[up, down]], scaled[t - 2 : t - 1])
+            blocks = [[up], [down]] if t < last else [[up, down]]
+            got = pick_rows(where, blocks, metas, order[t], scaled[t - 2 : t - 1], t == last - 1)
+            rows = got[:NX]
             if t < last:
-                up, down = hold([up, down], arrived[t - 1][1:] + [rows[0]])
+                up, down = hold(got[NX:] or [up, down], arrived[t - 1][1:] + [rows[0]])
             arrived.append(exchanged(rows))
         with jax.named_scope("project"):
             *written, piece = project(where, arrived[t - 1], weight, held, order[t - 1], written)

time: 264 us -> 260 us (0.985)
  waiting for transfers between devices: 118 us -> 108 us
  starting transfers between devices: 60.3 us -> 70.1 us
  local copies, waits for them, and re-layouts: 7.02 us -> 3.03 us
    ppermute x4, waiting for transfers between devices: 102 us -> 62.5 us  [shards(): up = lax.ppermute(up, 'expert', shift_z(1))]
    all_to_all x0 -> x1, waiting for transfers between devices: none -> 29.1 us  [shards(): lax.all_to_all(spread, 'expert', split_axis=0, concat_axis=0, axis_index_...]
    ppermute x4, starting transfers between devices: 3.92 us -> 10.2 us  [shards(): up = lax.ppermute(up, 'expert', shift_z(1))]
    all_to_all x0 -> x1, starting transfers between devices: none -> 5.19 us  [shards(): lax.all_to_all(spread, 'expert', split_axis=0, concat_axis=0, axis_index_...]
    ppermute x4, starting transfers between devices: 10.6 us -> 6.49 us  [shards(): down = lax.ppermute(down, 'expert', shift_z(-1))]
    slice x2 -> x0, local copies, waits for them, and re-layouts: 3.45 us -> none  [shards(): up, down = (up[:, :mid], down[:, mid:])]
  transfers between devices with their start and end apart: 27 -> 28, of which waited for: 9 -> 12; matrix products, arithmetic and copies ran while one was open for 2% -> 1% of each run, Pallas kernels for 25% -> 27%
where the time goes in v2:
time: 260 us; the launch traced here: 259 us
  waiting for transfers between devices  108 us (42%)
  Pallas kernels  73.9 us (28%)
  starting transfers between devices  70.1 us (27%)
  other arithmetic  3.17 us (1%)
  local copies, waits for them, and re-layouts  3.03 us (1%)
    ppermute x4, waiting for transfers between devices, shards(): up = lax.ppermute(up, 'expert', shift_z(1))  62.5 us
    pallas_call x5, Pallas kernels, project(): call(kernel, (steps,), [columns(rows, TILE, 0)] * NX + [columns(rows, TIL...  32.3 us
    all_to_all x1, waiting for transfers between devices, shards(): lax.all_to_all(spread, 'expert', split_axis=0, concat_axis=0, axis_index_...  29.1 us
    ppermute x15, starting transfers between devices, exchanged(): lax.ppermute(rows[k], 'expert', shift_x(k))  23 us
    pallas_call x4, Pallas kernels, pick_rows(): call(kernel, (1,), [whole(x.shape) for x in flat] + [pl.BlockSpec((1, slo...  21.9 us
    ppermute x3, starting transfers between devices, passed_along(): lax.ppermute(value, axis, [(source, source + steps) for source in range(i...  15.4 us
    ppermute x15, waiting for transfers between devices, exchanged(): lax.ppermute(rows[k], 'expert', shift_x(k))  13.9 us
    pallas_call x1, Pallas kernels, weight_grad(): call(kernel, (width // WIDE,), [columns(r.shape[0], WIDE, 0) for r in row...  10.3 us
  transfers between devices with their start and end apart: 28, of which 12 were waited for; matrix products, arithmetic and copies ran while one was open for 1% of the time, Pallas kernels for 27%

profile of v2, /device:TPU:1, one launch (start us, length us, event | category | flops | bytes accessed | tf_op | source)
XLA Modules:
  0.0 259.0 jit_solution(4855661721821944622)
XLA Ops:
  0.6 2.5 collective-permute-start.3
  3.2 4.0 %collective-permute-start.4 = (bf16[128,7168]{1,0:T(8,128)(2,1)}, bf16[128,7168]{1,0:T(8,128)(2,1)}, u32[]{:S(2)}, u32[]{:S(2)}) collective-permute-start(bf16[128,7168]{1,0:T(8,128)(2,1)} %bitcast.3.g_ref), channel_id=1, source_target_pairs={{0,7},{1,0},{2,1},{3,2},{4,3},{5,4},{6,5},{7,6},{8,15},{9,8},{10,9... | collective-permute-start | bytes 5505032 | tf_op jit(solution)/shard_map/ring_z/ppermute | solution.py:361
  8.5 4.2 %pick.8 = (bf16[8,128,128]{2,1,0:T(8,128)(2,1)}, bf16[32,7296]{1,0:T(8,128)(2,1)}, bf16[32,7296]{1,0:T(8,128)(2,1)}, bf16[32,7296]{1,0:T(8,128)(2,1)}, bf16[32,7296]{1,0:T(8,128)(2,1)}) custom-call(s32[10]{0:T(128)} %pad_add_fusion.w_ref, bf16[128,7168]{1,0:T(8,128)(2,1)} %bitcast.3.g_ref, s32[8,32]{1,0:T(8,128)} %bitcast.34, f32[8,32]{1,0:T(8,128)} %bitcast.35), custom_call_target="tpu_custom_call" | custom-call | flops 234881024 | bytes 5505024 | tf_op jit(solution)/shard_map/pick/pallas_call | solution.py:101
  12.7 5.2 %all-to-all-start = ((bf16[8,128,128]{2,1,0:T(8,128)(2,1)}), bf16[8,128,128]{2,1,0:T(8,128)(2,1)S(1)}, u32[]{:S(2)}, u32[]{:S(2)}) async-start(bf16[8,128,128]{2,1,0:T(8,128)(2,1)} %get-tuple-element.51), calls=%async_computation | async-start | bytes 524288 | tf_op jit(solution)/shard_map/pick/all_to_all | solution.py:353
  19.1 2.4 collective-permute-start.1
  22.7 29.1 %all-to-all-done.refs_2_.refs_3_ = bf16[8,128,128]{2,1,0:T(8,128)(2,1)S(1)} async-done(((bf16[8,128,128]{2,1,0:T(8,128)(2,1)}), bf16[8,128,128]{2,1,0:T(8,128)(2,1)S(1)}, u32[]{:S(2)}, u32[]{:S(2)}) %all-to-all-start) | async-done | bytes 262176 | tf_op jit(solution)/shard_map/pick/all_to_all | solution.py:353
  52.6 5.8 %pick.9 = (bf16[64,7296]{1,0:T(8,128)(2,1)}, bf16[64,7296]{1,0:T(8,128)(2,1)}, bf16[64,7296]{1,0:T(8,128)(2,1)}, bf16[64,7296]{1,0:T(8,128)(2,1)}) custom-call(s32[10]{0:T(128)} %pad_add_fusion.w_ref, bf16[128,7168]{1,0:T(8,128)(2,1)} %collective-permute-done.3.refs_0_, bf16[128,7168]{1,0:T(8,128)(2,1)} %collective-permute-done.4.refs_1_, ...), custom_call_target="tpu_custom_call" | custom-call | flops 469762048 | bytes 7340032 | tf_op jit(solution)/shard_map/pick/pallas_call | solution.py:132
  59.2 2.4 collective-permute-start.8
  63.0 2.4 collective-permute-start.6
  66.7 6.0 %project.5 = (bf16[32,32,256]{2,1,0:T(8,128)(2,1)}, f32[32,1,32]{2,1,0:T(1,128)}, bf16[256,128]{1,0:T(8,128)(2,1)}) custom-call(s32[10]{0:T(128)} %pad_add_fusion.w_ref, bf16[32,7296]{1,0:T(8,128)(2,1)} %get-tuple-element.47.refs_0_.refs_4_.refs_8_, bf16[32,7296]{1,0:T(8,128)(2,1)} %copy-done.5, ...), custom_call_target="tpu_custom_call" | custom-call | flops 469762048 | bytes 5505024 | tf_op jit(solution)/shard_map/project/pallas_call | solution.py:227
  72.6 27.1 %collective-permute-done.8.refs_0_ = bf16[128,7168]{1,0:T(8,128)(2,1)} collective-permute-done((bf16[128,7168]{1,0:T(8,128)(2,1)}, bf16[128,7168]{1,0:T(8,128)(2,1)}, u32[]{:S(2)}, u32[]{:S(2)}) %collective-permute-start.8) | collective-permute-done | bytes 1835040 | tf_op jit(solution)/shard_map/ring_z/ppermute | solution.py:360
  99.7 5.7 %pick.11 = (bf16[64,7296]{1,0:T(8,128)(2,1)}, bf16[64,7296]{1,0:T(8,128)(2,1)}, bf16[64,7296]{1,0:T(8,128)(2,1)}, bf16[64,7296]{1,0:T(8,128)(2,1)}) custom-call(s32[10]{0:T(128)} %pad_add_fusion.w_ref, bf16[128,7168]{1,0:T(8,128)(2,1)} %collective-permute-done.8.refs_0_, bf16[128,7168]{1,0:T(8,128)(2,1)} %collective-permute-done.9.refs_1_, ...), custom_call_target="tpu_custom_call" | custom-call | flops 469762048 | bytes 7340032 | tf_op jit(solution)/shard_map/pick/pallas_call | solution.py:132
  110.2 2.6 %collective-permute-start.11 = (bf16[64,7296]{1,0:T(8,128)(2,1)}, bf16[64,7296]{1,0:T(8,128)(2,1)}, u32[]{:S(2)}, u32[]{:S(2)}) collective-permute-start(bf16[64,7296]{1,0:T(8,128)(2,1)} %get-tuple-element.61), channel_id=1, source_target_pairs={{0,16},{1,17},{2,18},{3,19},{4,20},{5,21},{6,22},{7,23},{8,24},{9,... | collective-permute-start | bytes 2801672 | tf_op jit(solution)/shard_map/pick/exchange_x/ppermute | solution.py:346
  113.8 6.8 %project.6 = (bf16[32,32,256]{2,1,0:T(8,128)(2,1)}, f32[32,1,32]{2,1,0:T(1,128)}, bf16[256,256]{1,0:T(8,128)(2,1)}) custom-call(s32[10]{0:T(128)} %pad_add_fusion.w_ref, bf16[64,7296]{1,0:T(8,128)(2,1)} %get-tuple-element.52.refs_5_.refs_0_.refs_4_.refs_8_, bf16[64,7296]{1,0:T(8,128)(2,1)} %copy-done.1, ...), custom_call_target="tpu_custom_call", output_to_operand_aliasing={{0}: (16, {}), {1}: (17, {})} | custom-call | flops 939524096 | bytes 7340032 | tf_op jit(solution)/shard_map/project/pallas_call | solution.py:227
  120.6 24.1 %collective-permute-done.13.refs_0_ = bf16[128,7168]{1,0:T(8,128)(2,1)} collective-permute-done((bf16[128,7168]{1,0:T(8,128)(2,1)}, bf16[128,7168]{1,0:T(8,128)(2,1)}, u32[]{:S(2)}, u32[]{:S(2)}) %collective-permute-start.13) | collective-permute-done | bytes 1835040 | tf_op jit(solution)/shard_map/ring_z/ppermute | solution.py:360
  145.5 6.3 %pick.13 = (bf16[64,7296]{1,0:T(8,128)(2,1)}, bf16[64,7296]{1,0:T(8,128)(2,1)}, bf16[64,7296]{1,0:T(8,128)(2,1)}, bf16[64,7296]{1,0:T(8,128)(2,1)}, bf16[128,358...) custom-call(s32[10]{0:T(128)} %pad_add_fusion.w_ref, bf16[128,7168]{1,0:T(8,128)(2,1)} %collective-permute-done.13.refs_0_, ...), custom_call_target="tpu_custom_call" | custom-call | flops 469762048 | bytes 7340032 | tf_op jit(solution)/shard_map/pick/pallas_call | solution.py:132
  152.8 4.8 %collective-permute-start.18 = (bf16[128,3584]{1,0:T(8,128)(2,1)}, bf16[128,3584]{1,0:T(8,128)(2,1)}, u32[]{:S(2)}, u32[]{:S(2)}) collective-permute-start(bf16[128,3584]{1,0:T(8,128)(2,1)} %get-tuple-element.74), channel_id=1, source_target_pairs={{0,1},{1,2},{2,3},{3,4},{4,5},{5,6},{6,7},{7,0},{8,9},{9,10},{10,1... | collective-permute-start | bytes 2752520 | tf_op jit(solution)/shard_map/ring_z/ppermute | solution.py:360
  158.8 2.4 collective-permute-start.16
  162.6 11.3 %collective-permute-done.18.refs_0_ = bf16[128,3584]{1,0:T(8,128)(2,1)} collective-permute-done((bf16[128,3584]{1,0:T(8,128)(2,1)}, bf16[128,3584]{1,0:T(8,128)(2,1)}, u32[]{:S(2)}, u32[]{:S(2)}) %collective-permute-start.18) | collective-permute-done | bytes 917536 | tf_op jit(solution)/shard_map/ring_z/ppermute | solution.py:360
  173.9 6.4 %collective-permute-start.23 = (bf16[128,7168]{1,0:T(8,128)(2,1)}, bf16[128,7168]{1,0:T(8,128)(2,1)}, u32[]{:S(2)}, u32[]{:S(2)}) collective-permute-start(bf16[128,7168]{1,0:T(8,128)(2,1)} %bitcast.3.g_ref), channel_id=1, source_target_pairs={{32,0},{64,32},{96,64},{128,96},{160,128},{192,160},{224,192},{33,... | collective-permute-start | bytes 5505032 | tf_op jit(solution)/shard_map/next_section/ppermute | solution.py:27
  180.3 6.8 %project.7 = (bf16[32,32,256]{2,1,0:T(8,128)(2,1)}, f32[32,1,32]{2,1,0:T(1,128)}, bf16[256,256]{1,0:T(8,128)(2,1)}) custom-call(s32[10]{0:T(128)} %pad_add_fusion.w_ref, bf16[64,7296]{1,0:T(8,128)(2,1)} %get-tuple-element.59.refs_5_.refs_0_.refs_4_.refs_8_, bf16[64,7296]{1,0:T(8,128)(2,1)} %copy-done.2, ...), custom_call_target="tpu_custom_call", output_to_operand_aliasing={{0}: (16, {}), {1}: (17, {})} | custom-call | flops 939524096 | bytes 7340032 | tf_op jit(solution)/shard_map/project/pallas_call | solution.py:227
  187.1 4.1 %pick.15 = (bf16[32,7296]{1,0:T(8,128)(2,1)}, bf16[32,7296]{1,0:T(8,128)(2,1)}, bf16[32,7296]{1,0:T(8,128)(2,1)}, bf16[32,7296]{1,0:T(8,128)(2,1)}) custom-call(s32[10]{0:T(128)} %pad_add_fusion.w_ref, bf16[128,3584]{1,0:T(8,128)(2,1)} %collective-permute-done.18.refs_0_, bf16[128,3584]{1,0:T(8,128)(2,1)} %collective-permute-done.19.refs_1_, ...), custom_call_target="tpu_custom_call" | custom-call | flops 234881024 | bytes 3670016 | tf_op jit(solution)/shard_map/pick/pallas_call | solution.py:132
  192.4 2.4 collective-permute-start.21
  194.9 3.6 %collective-permute-done.16.refs_2_.refs_6_.refs_10_.refs_14_ = bf16[64,7296]{1,0:T(8,128)(2,1)} collective-permute-done((bf16[64,7296]{1,0:T(8,128)(2,1)}, bf16[64,7296]{1,0:T(8,128)(2,1)}, u32[]{:S(2)}, u32[]{:S(2)}) %collective-permute-start.16) | collective-permute-done | bytes 933920 | tf_op jit(solution)/shard_map/pick/exchange_x/ppermute | solution.py:346
  199.2 6.0 %collective-permute-done.17.refs_3_.refs_7_.refs_11_.refs_15_ = bf16[64,7296]{1,0:T(8,128)(2,1)} collective-permute-done((bf16[64,7296]{1,0:T(8,128)(2,1)}, bf16[64,7296]{1,0:T(8,128)(2,1)}, u32[]{:S(2)}, u32[]{:S(2)}) %collective-permute-start.17) | collective-permute-done | bytes 933920 | tf_op jit(solution)/shard_map/pick/exchange_x/ppermute | solution.py:346
  205.2 5.0 %collective-permute-start.24 = (bf16[8,7168]{1,0:T(8,128)(2,1)}, bf16[8,7168]{1,0:T(8,128)(2,1)}, u32[]{:S(2)}, u32[]{:S(2)}) collective-permute-start(bf16[8,7168]{1,0:T(8,128)(2,1)} %bitcast.38), channel_id=1, source_target_pairs={{32,0},{64,32},{96,64},{128,96},{160,128},{192,160},{224,192},{33,... | collective-permute-start | bytes 344072 | tf_op jit(solution)/shard_map/next_section/ppermute | solution.py:27
  210.2 6.8 %project.8 = (bf16[32,32,256]{2,1,0:T(8,128)(2,1)}, f32[32,1,32]{2,1,0:T(1,128)}, bf16[256,256]{1,0:T(8,128)(2,1)}) custom-call(s32[10]{0:T(128)} %pad_add_fusion.w_ref, bf16[64,7296]{1,0:T(8,128)(2,1)} %get-tuple-element.68.refs_5_.refs_0_.refs_4_.refs_8_.refs_12_, bf16[64,7296]{1,0:T(8,128)(2,1)} %copy-done.4, ...), custom_call_target="tpu_custom_call", output_to_operand_aliasing={{0}: (16, {}), {1}: (17, {})} | custom-call | flops 939524096 | bytes 7340032 | tf_op jit(solution)/shard_map/project/pallas_call | solution.py:227
  220.3 5.9 %project.9 = (bf16[32,32,256]{2,1,0:T(8,128)(2,1)}, f32[32,1,32]{2,1,0:T(1,128)}, bf16[256,128]{1,0:T(8,128)(2,1)}) custom-call(s32[10]{0:T(128)} %pad_add_fusion.w_ref, bf16[32,7296]{1,0:T(8,128)(2,1)} %get-tuple-element.79.refs_0_.refs_4_.refs_8_.refs_16_, ...), custom_call_target="tpu_custom_call", output_to_operand_aliasing={{0}: (16, {}), {1}: (17, {})} | custom-call | flops 469762048 | bytes 5505024 | tf_op jit(solution)/shard_map/project/pallas_call | solution.py:227
  226.3 9.9 %all-to-all-start.1 = ((f32[32,1,32]{2,1,0:T(1,128)}), f32[32,1,32]{2,1,0:T(1,128)S(1)}, u32[]{:S(2)}, u32[]{:S(2)}) async-start(f32[32,1,32]{2,1,0:T(1,128)} %get-tuple-element.90), calls=%async_computation.1 | async-start | bytes 32768 | tf_op jit(solution)/shard_map/gate_return/all_to_all | solution.py:378
  236.2 10.3 %weight_grad.1.refs_0_ = bf16[256,7168]{1,0:T(8,128)(2,1)} custom-call(s32[10]{0:T(128)} %pad_add_fusion.w_ref, bf16[32,7296]{1,0:T(8,128)(2,1)} %get-tuple-element.47.refs_0_.refs_4_.refs_8_, bf16[32,7296]{1,0:T(8,128)(2,1)} %copy-done.5, bf16[32,7296]{1,0:T(8,128)(2,1)} %collective-permute-done.1.refs_3_.refs_2_.refs_6_.refs_10_, ...), custom_call_target="tpu_custom_call" | custom-call | flops 3758096384 | bytes 18350080 | tf_op jit(solution)/shard_map/weight_grad/pallas_call | solution.py:266
  248.7 4.0 %collective-permute-start.25 = (bf16[24,128]{1,0:T(8,128)(2,1)}, bf16[24,128]{1,0:T(8,128)(2,1)S(1)}, u32[]{:S(2)}, u32[]{:S(2)}) collective-permute-start(bf16[24,128]{1,0:T(8,128)(2,1)} %input_grad.2), channel_id=1, source_target_pairs={{32,0},{64,32},{96,64},{128,96},{160,128},{192,160},{224,192},{33,... | collective-permute-start | bytes 18440 | tf_op jit(solution)/shard_map/input_grad/ppermute | solution.py:27
  255.5 3.6 %input_grad.3 = bf16[128,7168]{1,0:T(8,128)(2,1)} custom-call(s32[10]{0:T(128)S(1)} %copy-done, bf16[128,7168]{1,0:T(8,128)(2,1)} %collective-permute-done.23.g_ref, bf16[24,7168]{1,0:T(8,128)(2,1)S(1)} %pad_maximum_fusion.r_ref, bf16[24,128]{1,0:T(8,128)(2,1)S(1)} %collective-permute-done.25.l_ref), custom_call_target="tpu_custom_call" | custom-call | flops 44040192 | bytes 3670016 | tf_op jit(solution)/shard_map/input_grad/pallas_call | solution.py:285
  (65 shorter events, 28.1 us)
Async XLA Ops:
  0.6 51.3 %collective-permute-start.3 = (bf16[128,7168]{1,0:T(8,128)(2,1)}, bf16[128,7168]{1,0:T(8,128)(2,1)}, u32[]{:S(2)}, u32[]{:S(2)}) collective-permute-start(bf16[128,7168]{1,0:T(8,128)(2,1)} %bitcast.3.g_ref), channel_id=1, source_target_pairs={{0,1},{1,2},{2,3},{3,4},{4,5},{5,6},{6,7},{7,0},{8,9},{9,10},{10,1... | collective-permute-start | bytes 5505032 | tf_op jit(solution)/shard_map/ring_z/ppermute | solution.py:360
  3.2 48.7 %collective-permute-start.4 = (bf16[128,7168]{1,0:T(8,128)(2,1)}, bf16[128,7168]{1,0:T(8,128)(2,1)}, u32[]{:S(2)}, u32[]{:S(2)}) collective-permute-start(bf16[128,7168]{1,0:T(8,128)(2,1)} %bitcast.3.g_ref), channel_id=1, source_target_pairs={{0,7},{1,0},{2,1},{3,2},{4,3},{5,4},{6,5},{7,6},{8,15},{9,8},{10,9... | collective-permute-start | bytes 5505032 | tf_op jit(solution)/shard_map/ring_z/ppermute | solution.py:361
  12.7 39.2 %all-to-all-start = ((bf16[8,128,128]{2,1,0:T(8,128)(2,1)}), bf16[8,128,128]{2,1,0:T(8,128)(2,1)S(1)}, u32[]{:S(2)}, u32[]{:S(2)}) async-start(bf16[8,128,128]{2,1,0:T(8,128)(2,1)} %get-tuple-element.51), calls=%async_computation | async-start | bytes 524288 | tf_op jit(solution)/shard_map/pick/all_to_all | solution.py:353
  17.9 40.5 %collective-permute-start = (bf16[32,7296]{1,0:T(8,128)(2,1)}, bf16[32,7296]{1,0:T(8,128)(2,1)S(1)}, u32[]{:S(2)}, u32[]{:S(2)}) collective-permute-start(bf16[32,7296]{1,0:T(8,128)(2,1)} %get-tuple-element.48), channel_id=1, source_target_pairs={{0,8},{1,9},{2,10},{3,11},{4,12},{5,13},{6,14},{7,15},{8,16},{9,17... | collective-permute-start | bytes 1400840 | tf_op jit(solution)/shard_map/exchange_x/ppermute | solution.py:346
  19.1 39.3 %collective-permute-start.1 = (bf16[32,7296]{1,0:T(8,128)(2,1)}, bf16[32,7296]{1,0:T(8,128)(2,1)}, u32[]{:S(2)}, u32[]{:S(2)}) collective-permute-start(bf16[32,7296]{1,0:T(8,128)(2,1)} %get-tuple-element.49), channel_id=1, source_target_pairs={{0,16},{1,17},{2,18},{3,19},{4,20},{5,21},{6,22},{7,23},{8,24},{9,... | collective-permute-start | bytes 1400840 | tf_op jit(solution)/shard_map/exchange_x/ppermute | solution.py:346
  21.6 36.8 %collective-permute-start.2 = (bf16[32,7296]{1,0:T(8,128)(2,1)}, bf16[32,7296]{1,0:T(8,128)(2,1)}, u32[]{:S(2)}, u32[]{:S(2)}) collective-permute-start(bf16[32,7296]{1,0:T(8,128)(2,1)} %get-tuple-element.50), channel_id=1, source_target_pairs={{0,24},{1,25},{2,26},{3,27},{4,28},{5,29},{6,30},{7,31},{8,0},{9,1... | collective-permute-start | bytes 1400840 | tf_op jit(solution)/shard_map/exchange_x/ppermute | solution.py:346
  59.2 40.5 %collective-permute-start.8 = (bf16[128,7168]{1,0:T(8,128)(2,1)}, bf16[128,7168]{1,0:T(8,128)(2,1)}, u32[]{:S(2)}, u32[]{:S(2)}) collective-permute-start(bf16[128,7168]{1,0:T(8,128)(2,1)} %get-tuple-element.56), channel_id=1, source_target_pairs={{0,1},{1,2},{2,3},{3,4},{4,5},{5,6},{6,7},{7,0},{8,9},{9,10},{10,1... | collective-permute-start | bytes 5505032 | tf_op jit(solution)/shard_map/ring_z/ppermute | solution.py:360
  61.6 38.1 %collective-permute-start.9 = (bf16[128,7168]{1,0:T(8,128)(2,1)}, bf16[128,7168]{1,0:T(8,128)(2,1)}, u32[]{:S(2)}, u32[]{:S(2)}) collective-permute-start(bf16[128,7168]{1,0:T(8,128)(2,1)} %get-tuple-element.57), channel_id=1, source_target_pairs={{0,7},{1,0},{2,1},{3,2},{4,3},{5,4},{6,5},{7,6},{8,15},{9,8},{10,9... | collective-permute-start | bytes 5505032 | tf_op jit(solution)/shard_map/ring_z/ppermute | solution.py:361
  61.8 43.5 %collective-permute-start.5 = (bf16[64,7296]{1,0:T(8,128)(2,1)}, bf16[64,7296]{1,0:T(8,128)(2,1)S(1)}, u32[]{:S(2)}, u32[]{:S(2)}) collective-permute-start(bf16[64,7296]{1,0:T(8,128)(2,1)} %get-tuple-element.53), channel_id=1, source_target_pairs={{0,8},{1,9},{2,10},{3,11},{4,12},{5,13},{6,14},{7,15},{8,16},{9,17... | collective-permute-start | bytes 2801672 | tf_op jit(solution)/shard_map/pick/exchange_x/ppermute | solution.py:346
  63.0 42.3 %collective-permute-start.6 = (bf16[64,7296]{1,0:T(8,128)(2,1)}, bf16[64,7296]{1,0:T(8,128)(2,1)}, u32[]{:S(2)}, u32[]{:S(2)}) collective-permute-start(bf16[64,7296]{1,0:T(8,128)(2,1)} %get-tuple-element.54), channel_id=1, source_target_pairs={{0,16},{1,17},{2,18},{3,19},{4,20},{5,21},{6,22},{7,23},{8,24},{9,... | collective-permute-start | bytes 2801672 | tf_op jit(solution)/shard_map/pick/exchange_x/ppermute | solution.py:346
  65.5 40.1 %collective-permute-start.7 = (bf16[64,7296]{1,0:T(8,128)(2,1)}, bf16[64,7296]{1,0:T(8,128)(2,1)}, u32[]{:S(2)}, u32[]{:S(2)}) collective-permute-start(bf16[64,7296]{1,0:T(8,128)(2,1)} %get-tuple-element.55), channel_id=1, source_target_pairs={{0,24},{1,25},{2,26},{3,27},{4,28},{5,29},{6,30},{7,31},{8,0},{9,1... | collective-permute-start | bytes 2801672 | tf_op jit(solution)/shard_map/pick/exchange_x/ppermute | solution.py:346
  106.3 38.4 %collective-permute-start.13 = (bf16[128,7168]{1,0:T(8,128)(2,1)}, bf16[128,7168]{1,0:T(8,128)(2,1)}, u32[]{:S(2)}, u32[]{:S(2)}) collective-permute-start(bf16[128,7168]{1,0:T(8,128)(2,1)} %get-tuple-element.63), channel_id=1, source_target_pairs={{0,1},{1,2},{2,3},{3,4},{4,5},{5,6},{6,7},{7,0},{8,9},{9,10},{10,1... | collective-permute-start | bytes 5505032 | tf_op jit(solution)/shard_map/ring_z/ppermute | solution.py:360
  106.8 38.7 %collective-permute-start.14 = (bf16[128,7168]{1,0:T(8,128)(2,1)}, bf16[128,7168]{1,0:T(8,128)(2,1)}, u32[]{:S(2)}, u32[]{:S(2)}) collective-permute-start(bf16[128,7168]{1,0:T(8,128)(2,1)} %get-tuple-element.64), channel_id=1, source_target_pairs={{0,7},{1,0},{2,1},{3,2},{4,3},{5,4},{6,5},{7,6},{8,15},{9,8},{10,9... | collective-permute-start | bytes 5505032 | tf_op jit(solution)/shard_map/ring_z/ppermute | solution.py:361
  109.0 42.8 %collective-permute-start.10 = (bf16[64,7296]{1,0:T(8,128)(2,1)}, bf16[64,7296]{1,0:T(8,128)(2,1)S(1)}, u32[]{:S(2)}, u32[]{:S(2)}) collective-permute-start(bf16[64,7296]{1,0:T(8,128)(2,1)} %get-tuple-element.60), channel_id=1, source_target_pairs={{0,8},{1,9},{2,10},{3,11},{4,12},{5,13},{6,14},{7,15},{8,16},{9,17... | collective-permute-start | bytes 2801672 | tf_op jit(solution)/shard_map/pick/exchange_x/ppermute | solution.py:346
  110.2 41.6 %collective-permute-start.11 = (bf16[64,7296]{1,0:T(8,128)(2,1)}, bf16[64,7296]{1,0:T(8,128)(2,1)}, u32[]{:S(2)}, u32[]{:S(2)}) collective-permute-start(bf16[64,7296]{1,0:T(8,128)(2,1)} %get-tuple-element.61), channel_id=1, source_target_pairs={{0,16},{1,17},{2,18},{3,19},{4,20},{5,21},{6,22},{7,23},{8,24},{9,... | collective-permute-start | bytes 2801672 | tf_op jit(solution)/shard_map/pick/exchange_x/ppermute | solution.py:346
  112.8 39.9 %collective-permute-start.12 = (bf16[64,7296]{1,0:T(8,128)(2,1)}, bf16[64,7296]{1,0:T(8,128)(2,1)}, u32[]{:S(2)}, u32[]{:S(2)}) collective-permute-start(bf16[64,7296]{1,0:T(8,128)(2,1)} %get-tuple-element.62), channel_id=1, source_target_pairs={{0,24},{1,25},{2,26},{3,27},{4,28},{5,29},{6,30},{7,31},{8,0},{9,1... | collective-permute-start | bytes 2801672 | tf_op jit(solution)/shard_map/pick/exchange_x/ppermute | solution.py:346
  152.8 9.6 %copy-start.7 = (s32[1,1,8,32]{3,2,1,0:T(8,128)S(1)}, s32[1,1,8,32]{3,2,1,0:T(8,128)}, u32[]{:S(2)}) copy-start(s32[1,1,8,32]{3,2,1,0:T(8,128)} %param.11) | copy-start | bytes 3076
  152.8 9.7 %copy-start.8 = (s32[1,1,8]{2,1,0:T(1,128)S(1)}, s32[1,1,8]{2,1,0:T(1,128)}, u32[]{:S(2)}) copy-start(s32[1,1,8]{2,1,0:T(1,128)} %param.12) | copy-start | bytes 100
  152.8 21.1 %collective-permute-start.18 = (bf16[128,3584]{1,0:T(8,128)(2,1)}, bf16[128,3584]{1,0:T(8,128)(2,1)}, u32[]{:S(2)}, u32[]{:S(2)}) collective-permute-start(bf16[128,3584]{1,0:T(8,128)(2,1)} %get-tuple-element.74), channel_id=1, source_target_pairs={{0,1},{1,2},{2,3},{3,4},{4,5},{5,6},{6,7},{7,0},{8,9},{9,10},{10,1... | collective-permute-start | bytes 2752520 | tf_op jit(solution)/shard_map/ring_z/ppermute | solution.py:360
  157.5 29.6 %collective-permute-start.19 = (bf16[128,3584]{1,0:T(8,128)(2,1)}, bf16[128,3584]{1,0:T(8,128)(2,1)}, u32[]{:S(2)}, u32[]{:S(2)}) collective-permute-start(bf16[128,3584]{1,0:T(8,128)(2,1)} %get-tuple-element.75), channel_id=1, source_target_pairs={{0,7},{1,0},{2,1},{3,2},{4,3},{5,4},{6,5},{7,6},{8,15},{9,8},{10,9... | collective-permute-start | bytes 2752520 | tf_op jit(solution)/shard_map/ring_z/ppermute | solution.py:361
  157.5 34.9 %collective-permute-start.15 = (bf16[64,7296]{1,0:T(8,128)(2,1)}, bf16[64,7296]{1,0:T(8,128)(2,1)S(1)}, u32[]{:S(2)}, u32[]{:S(2)}) collective-permute-start(bf16[64,7296]{1,0:T(8,128)(2,1)} %get-tuple-element.69), channel_id=1, source_target_pairs={{0,8},{1,9},{2,10},{3,11},{4,12},{5,13},{6,14},{7,15},{8,16},{9,17... | collective-permute-start | bytes 2801672 | tf_op jit(solution)/shard_map/pick/exchange_x/ppermute | solution.py:346
  158.8 39.7 %collective-permute-start.16 = (bf16[64,7296]{1,0:T(8,128)(2,1)}, bf16[64,7296]{1,0:T(8,128)(2,1)}, u32[]{:S(2)}, u32[]{:S(2)}) collective-permute-start(bf16[64,7296]{1,0:T(8,128)(2,1)} %get-tuple-element.70), channel_id=1, source_target_pairs={{0,16},{1,17},{2,18},{3,19},{4,20},{5,21},{6,22},{7,23},{8,24},{9,... | collective-permute-start | bytes 2801672 | tf_op jit(solution)/shard_map/pick/exchange_x/ppermute | solution.py:346
  161.2 44.0 %collective-permute-start.17 = (bf16[64,7296]{1,0:T(8,128)(2,1)}, bf16[64,7296]{1,0:T(8,128)(2,1)}, u32[]{:S(2)}, u32[]{:S(2)}) collective-permute-start(bf16[64,7296]{1,0:T(8,128)(2,1)} %get-tuple-element.71), channel_id=1, source_target_pairs={{0,24},{1,25},{2,26},{3,27},{4,28},{5,29},{6,30},{7,31},{8,0},{9,1... | collective-permute-start | bytes 2801672 | tf_op jit(solution)/shard_map/pick/exchange_x/ppermute | solution.py:346
  173.9 79.9 %collective-permute-start.23 = (bf16[128,7168]{1,0:T(8,128)(2,1)}, bf16[128,7168]{1,0:T(8,128)(2,1)}, u32[]{:S(2)}, u32[]{:S(2)}) collective-permute-start(bf16[128,7168]{1,0:T(8,128)(2,1)} %bitcast.3.g_ref), channel_id=1, source_target_pairs={{32,0},{64,32},{96,64},{128,96},{160,128},{192,160},{224,192},{33,... | collective-permute-start | bytes 5505032 | tf_op jit(solution)/shard_map/next_section/ppermute | solution.py:27
  191.2 25.9 %collective-permute-start.20 = (bf16[32,7296]{1,0:T(8,128)(2,1)}, bf16[32,7296]{1,0:T(8,128)(2,1)}, u32[]{:S(2)}, u32[]{:S(2)}) collective-permute-start(bf16[32,7296]{1,0:T(8,128)(2,1)} %get-tuple-element.80), channel_id=1, source_target_pairs={{0,8},{1,9},{2,10},{3,11},{4,12},{5,13},{6,14},{7,15},{8,16},{9,17... | collective-permute-start | bytes 1400840 | tf_op jit(solution)/shard_map/pick/exchange_x/ppermute | solution.py:346
  192.4 17.8 %copy-start.4 = (bf16[64,7296]{1,0:T(8,128)(2,1)}, bf16[64,7296]{1,0:T(8,128)(2,1)S(1)}, u32[]{:S(2)}) copy-start(bf16[64,7296]{1,0:T(8,128)(2,1)S(1)} %collective-permute-done.15.refs_1_.refs_5_.refs_9_.refs_13_) | copy-start | bytes 2801668
  192.4 26.0 %collective-permute-start.21 = (bf16[32,7296]{1,0:T(8,128)(2,1)}, bf16[32,7296]{1,0:T(8,128)(2,1)}, u32[]{:S(2)}, u32[]{:S(2)}) collective-permute-start(bf16[32,7296]{1,0:T(8,128)(2,1)} %get-tuple-element.81), channel_id=1, source_target_pairs={{0,16},{1,17},{2,18},{3,19},{4,20},{5,21},{6,22},{7,23},{8,24},{9,... | collective-permute-start | bytes 1400840 | tf_op jit(solution)/shard_map/pick/exchange_x/ppermute | solution.py:346
  198.4 21.9 %collective-permute-start.22 = (bf16[32,7296]{1,0:T(8,128)(2,1)}, bf16[32,7296]{1,0:T(8,128)(2,1)}, u32[]{:S(2)}, u32[]{:S(2)}) collective-permute-start(bf16[32,7296]{1,0:T(8,128)(2,1)} %get-tuple-element.82), channel_id=1, source_target_pairs={{0,24},{1,25},{2,26},{3,27},{4,28},{5,29},{6,30},{7,31},{8,0},{9,1... | collective-permute-start | bytes 1400840 | tf_op jit(solution)/shard_map/pick/exchange_x/ppermute | solution.py:346
  205.2 47.5 %collective-permute-start.24 = (bf16[8,7168]{1,0:T(8,128)(2,1)}, bf16[8,7168]{1,0:T(8,128)(2,1)}, u32[]{:S(2)}, u32[]{:S(2)}) collective-permute-start(bf16[8,7168]{1,0:T(8,128)(2,1)} %bitcast.38), channel_id=1, source_target_pairs={{32,0},{64,32},{96,64},{128,96},{160,128},{192,160},{224,192},{33,... | collective-permute-start | bytes 344072 | tf_op jit(solution)/shard_map/next_section/ppermute | solution.py:27
  226.3 20.2 %all-to-all-start.1 = ((f32[32,1,32]{2,1,0:T(1,128)}), f32[32,1,32]{2,1,0:T(1,128)S(1)}, u32[]{:S(2)}, u32[]{:S(2)}) async-start(f32[32,1,32]{2,1,0:T(1,128)} %get-tuple-element.90), calls=%async_computation.1 | async-start | bytes 32768 | tf_op jit(solution)/shard_map/gate_return/all_to_all | solution.py:378
  246.4 9.0 %copy-start = (s32[10]{0:T(128)S(1)}, s32[10]{0:T(128)}, u32[]{:S(2)}) copy-start(s32[10]{0:T(128)} %pad_add_fusion.w_ref) | copy-start | bytes 124
  248.7 6.7 %collective-permute-start.25 = (bf16[24,128]{1,0:T(8,128)(2,1)}, bf16[24,128]{1,0:T(8,128)(2,1)S(1)}, u32[]{:S(2)}, u32[]{:S(2)}) collective-permute-start(bf16[24,128]{1,0:T(8,128)(2,1)} %input_grad.2), channel_id=1, source_target_pairs={{32,0},{64,32},{96,64},{128,96},{160,128},{192,160},{224,192},{33,... | collective-permute-start | bytes 18440 | tf_op jit(solution)/shard_map/input_grad/ppermute | solution.py:27
  (5 other events, 4.0 us)

commit v3 on v2

--- a/solution.py
+++ b/solution.py
@@ -77,7 +77,7 @@
     count, width = grad.shape
     cap = tokens.shape[1]
 
-    def kernel(w_ref, g_ref, t_ref, s_ref, meta_ref, *outs):
+    def kernel(w_ref, g_ref, t_ref, s_ref, own_ref, meta_ref, out_ref):
         slot = lax.broadcasted_iota(jnp.int32, (1, cap), 1)
         for k in range(NX):
             lines = []
@@ -93,17 +93,19 @@
             table = jnp.concatenate(lines, 0)
             table = jnp.concatenate([table, jnp.zeros((2 * META, LANES - cap), F32)], 1)
             table = jnp.concatenate([table, jnp.zeros((LANES - 2 * META, LANES), F32)], 0).T
+            own_ref[0, k * cap : (k + 1) * cap, :] = table[:cap].astype(BF)
             for z in range(NZ):
                 meta_ref[z, k * cap : (k + 1) * cap, :] = table[:cap].astype(BF)
-        picked(w_ref, meta_ref[0], [g_ref], outs, 0)
+        picked(w_ref, own_ref[0], [g_ref], [out_ref.at[lax.rem(w_ref[0] + k, NX)] for k in range(NX)], 0)
 
     full = width + LANES
     return call(
         kernel,
         (1,),
         [whole(x.shape) for x in (grad, tokens, gates)],
-        [whole((NZ, NX * cap, LANES))] + [whole((cap, full))] * NX,
-        [jax.ShapeDtypeStruct((NZ, NX * cap, LANES), BF)] + [jax.ShapeDtypeStruct((cap, full), BF)] * NX,
+        [whole((n, NX * cap, LANES)) for n in (1, NZ)] + [whole((NX, cap, full))],
+        [jax.ShapeDtypeStruct((n, NX * cap, LANES), BF) for n in (1, NZ)]
+        + [jax.ShapeDtypeStruct((NX, cap, full), BF)],
         flops=2 * NX * cap * count * width,
         nbytes=6 * count * width,
     )(where, grad, tokens, gates)
@@ -114,7 +116,7 @@
     flat = [x for block in blocks for x in block]
     tokens = flat[0].shape[0]
     width = sum(x.shape[1] for x in blocks[0])
-    slots = metas.shape[1]
+    slots = metas[0].shape[1]
     cap = slots // NX
     mid = width // 2
     cuts = 2 if cut else 0
@@ -133,13 +135,16 @@
         kernel,
         (1,),
         [whole(x.shape) for x in flat]
-        + [pl.BlockSpec((1, slots, LANES), lambda j, w, d=d: (lax.rem(w[1] + d, NZ), 0, 0)) for d in places]
+        + [
+            pl.BlockSpec((1, slots, LANES), lambda j, w, d=d: (0 if d is None else lax.rem(w[1] + d, NZ), 0, 0))
+            for d in places
+        ]
         + [HBM] * len(after),
         [whole(x) for x in shapes],
         [jax.ShapeDtypeStruct(x, BF) for x in shapes],
         flops=2 * n * slots * tokens * width,
         nbytes=4 * n * tokens * width,
-    )(where, *flat, *[metas] * n, *after)
+    )(where, *flat, *metas, *after)
 
 
 def hold(arrays, after):
@@ -156,17 +161,20 @@
 def project(where, got, weight, held, shifts, before):
     rows = got[0].shape[0]
     hid, width = weight.shape
-    cap = rows // len(shifts)
+    arrays = len(got)
+    cap = rows * arrays // NX // len(shifts)
     steps = width // 2 // TILE
     n = NX * len(shifts)
 
     def kernel(w_ref, *refs):
-        lows, highs, metas = refs[:NX], refs[NX : 2 * NX], refs[2 * NX : 3 * NX]
-        w_low, w_high, held_hbm = refs[3 * NX : 3 * NX + 3]
+        lows, highs, metas = refs[:arrays], refs[arrays : 2 * arrays], refs[2 * arrays : 3 * arrays]
+        w_low, w_high, held_hbm = refs[3 * arrays : 3 * arrays + 3]
         hid_hbm, part_hbm, scaled_ref, acc, held_v, hid_v, part_v, sem_in, sem_hid, sem_part = refs[-10:]
         step = pl.program_id(0)
 
         def source(j):
+            if arrays == 1:
+                return j * NZ + w_ref[1]
             k, d = j // len(shifts), shifts[j % len(shifts)]
             return lax.rem(w_ref[0] + (NX - k), NX) * NZ + lax.rem(w_ref[1] + d, NZ)
 
@@ -222,14 +230,14 @@
                 copy.wait()
 
     extra = list(before) if before else []
-    first = 1 + 3 * NX + 3
+    first = 1 + 3 * arrays + 3
     sources = held.shape[0]
     return call(
         kernel,
         (steps,),
-        [columns(rows, TILE, 0)] * NX
-        + [columns(rows, TILE, width // 2)] * NX
-        + [pl.BlockSpec((rows, LANES), lambda j, w: (0, width // LANES))] * NX
+        [columns(rows, TILE, 0)] * arrays
+        + [columns(rows, TILE, width // 2)] * arrays
+        + [pl.BlockSpec((rows, LANES), lambda j, w: (0, width // LANES))] * arrays
         + [columns(hid, TILE, 0), columns(hid, TILE, width // 2), HBM]
         + [HBM] * len(extra),
         [HBM, HBM, whole((hid, n * cap))],
@@ -348,23 +356,30 @@
     last = NZ // 2
     order = [[0]] + [[NZ - t, t] for t in range(1, last)] + [[last]]
     with jax.named_scope("pick"):
-        spread, *rows = begin(where, grad, tokens, gates)
+        own, spread, rows = begin(where, grad, tokens, gates)
+        near = [lax.ppermute(own, "expert", shift_z(k)) for k in (1, -1)]
         line = [[x * NZ + z for z in range(NZ)] for x in range(NX)]
         metas = lax.all_to_all(
             spread, "expert", split_axis=0, concat_axis=0, axis_index_groups=line, tiled=True
         )
     up = down = grad
-    arrived, scaled, written = [exchanged(rows)], [], None
+    with jax.named_scope("exchange_x"):
+        across = [[x * NZ + z for x in range(NX)] for z in range(NZ)]
+        rows = lax.all_to_all(
+            rows, "expert", split_axis=0, concat_axis=0, axis_index_groups=across, tiled=True
+        )
+    arrived, scaled, written = [[rows.reshape(-1, rows.shape[2])]], [], None
     for t in range(1, last + 1):
         with jax.named_scope("ring_z"):
             up = lax.ppermute(up, "expert", shift_z(1))
             down = lax.ppermute(down, "expert", shift_z(-1))
         with jax.named_scope("pick"):
             blocks = [[up], [down]] if t < last else [[up, down]]
-            got = pick_rows(where, blocks, metas, order[t], scaled[t - 2 : t - 1], t == last - 1)
+            tables, places = (near, [None, None]) if t == 1 else ([metas] * len(blocks), order[t])
+            got = pick_rows(where, blocks, tables, places, scaled[t - 2 : t - 1], t == last - 1)
             rows = got[:NX]
             if t < last:
-                up, down = hold(got[NX:] or [up, down], arrived[t - 1][1:] + [rows[0]])
+                up, down = hold(got[NX:] or [up, down], arrived[t - 1][-3:] + [rows[0]])
             arrived.append(exchanged(rows))
         with jax.named_scope("project"):
             *written, piece = project(where, arrived[t - 1], weight, held, order[t - 1], written)

time: 260 us -> 259 us (level)
  waiting for transfers between devices: 108 us -> 103 us
  starting transfers between devices: 70.1 us -> 74.7 us
    ppermute x0 -> x2, waiting for transfers between devices: none -> 27.8 us  [shards(): near = [lax.ppermute(own, 'expert', shift_z(k)) for k in (1, -1)]]
    ppermute x4, waiting for transfers between devices: 62.5 us -> 35.3 us  [shards(): up = lax.ppermute(up, 'expert', shift_z(1))]
    ppermute x15 -> x12, starting transfers between devices: 23 us -> 18.1 us  [exchanged(): lax.ppermute(rows[k], 'expert', shift_x(k))]
    all_to_all x0 -> x1, starting transfers between devices: none -> 4.55 us  [shards(): lax.all_to_all(rows, 'expert', split_axis=0, concat_axis=0, axis_index_gr...]
    ppermute x3, starting transfers between devices: 15.4 us -> 18.5 us  [passed_along(): lax.ppermute(value, axis, [(source, source + steps) for source in range(i...]
    ppermute x15 -> x12, waiting for transfers between devices: 13.9 us -> 10.9 us  [exchanged(): lax.ppermute(rows[k], 'expert', shift_x(k))]
    ppermute x0 -> x2, starting transfers between devices: none -> 2.75 us  [shards(): near = [lax.ppermute(own, 'expert', shift_z(k)) for k in (1, -1)]]
    ppermute x4, starting transfers between devices: 10.2 us -> 7.55 us  [shards(): up = lax.ppermute(up, 'expert', shift_z(1))]
  transfers between devices with their start and end apart: 28 -> 28, of which waited for: 12 -> 10; matrix products, arithmetic and copies ran while one was open for 1% -> 1% of each run, Pallas kernels for 27% -> 27%
where the time goes in v3:
time: 259 us; the launch traced here: 258 us
  waiting for transfers between devices  103 us (40%)
  starting transfers between devices  74.7 us (29%)
  Pallas kernels  73.4 us (28%)
  other arithmetic  3.17 us (1%)
    ppermute x4, waiting for transfers between devices, shards(): up = lax.ppermute(up, 'expert', shift_z(1))  35.3 us
    pallas_call x5, Pallas kernels, project(): call(kernel, (steps,), [columns(rows, TILE, 0)] * arrays + [columns(rows,...  32.1 us
    ppermute x2, waiting for transfers between devices, shards(): near = [lax.ppermute(own, 'expert', shift_z(k)) for k in (1, -1)]  27.8 us
    all_to_all x1, waiting for transfers between devices, shards(): lax.all_to_all(spread, 'expert', split_axis=0, concat_axis=0, axis_index_...  27.5 us
    pallas_call x4, Pallas kernels, pick_rows(): call(kernel, (1,), [whole(x.shape) for x in flat] + [pl.BlockSpec((1, slo...  21.8 us
    ppermute x3, starting transfers between devices, passed_along(): lax.ppermute(value, axis, [(source, source + steps) for source in range(i...  18.5 us
    ppermute x12, starting transfers between devices, exchanged(): lax.ppermute(rows[k], 'expert', shift_x(k))  18.1 us
    ppermute x12, waiting for transfers between devices, exchanged(): lax.ppermute(rows[k], 'expert', shift_x(k))  10.9 us
  transfers between devices with their start and end apart: 28, of which 10 were waited for; matrix products, arithmetic and copies ran while one was open for 1% of the time, Pallas kernels for 27%

profile of v3, /device:TPU:1, one launch (start us, length us, event | category | flops | bytes accessed | tf_op | source)
XLA Modules:
  0.0 257.9 jit_solution(6650430069578341798)
XLA Ops:
  0.6 2.5 collective-permute-start
  3.2 4.0 %collective-permute-start.1 = (bf16[128,7168]{1,0:T(8,128)(2,1)}, bf16[128,7168]{1,0:T(8,128)(2,1)}, u32[]{:S(2)}, u32[]{:S(2)}) collective-permute-start(bf16[128,7168]{1,0:T(8,128)(2,1)} %bitcast.3.g_ref), channel_id=1, source_target_pairs={{0,7},{1,0},{2,1},{3,2},{4,3},{5,4},{6,5},{7,6},{8,15},{9,8},{10,9... | collective-permute-start | bytes 5505032 | tf_op jit(solution)/shard_map/ring_z/ppermute | solution.py:375
  8.5 4.2 %pick.8 = (bf16[1,128,128]{2,1,0:T(8,128)(2,1)}, bf16[8,128,128]{2,1,0:T(8,128)(2,1)}, bf16[4,32,7296]{2,1,0:T(8,128)(2,1)}) custom-call(s32[10]{0:T(128)} %pad_add_fusion.w_ref, bf16[128,7168]{1,0:T(8,128)(2,1)} %bitcast.3.g_ref, s32[8,32]{1,0:T(8,128)} %bitcast.35, f32[8,32]{1,0:T(8,128)} %bitcast.36), custom_call_target="tpu_custom_call" | custom-call | flops 234881024 | bytes 5505024 | tf_op jit(solution)/shard_map/pick/pallas_call | solution.py:102
  12.7 4.5 %all-to-all-start = ((bf16[4,32,7296]{2,1,0:T(8,128)(2,1)}), bf16[4,32,7296]{2,1,0:T(8,128)(2,1)}, u32[]{:S(2)}, u32[]{:S(2)}) async-start(bf16[4,32,7296]{2,1,0:T(8,128)(2,1)} %get-tuple-element.45), calls=%async_computation | async-start | bytes 3735552 | tf_op jit(solution)/shard_map/exchange_x/all_to_all | solution.py:368
  17.4 2.7 %collective-permute-start.3 = (bf16[1,128,128]{2,1,0:T(8,128)(2,1)S(1)}, bf16[1,128,128]{2,1,0:T(8,128)(2,1)S(1)}, u32[]{:S(2)}, u32[]{:S(2)}) collective-permute-start(bf16[1,128,128]{2,1,0:T(8,128)(2,1)S(1)} %copy-done.9), channel_id=1, source_target_pairs={{0,7},{1,0},{2,1},{3,2},{4,3},{5,4},{6,5},{7,6},{8,15},{9,8},{10,9... | collective-permute-start | bytes 98312 | tf_op jit(solution)/shard_map/pick/ppermute | solution.py:360
  20.1 27.8 %collective-permute-done.2.refs_2_ = bf16[1,128,128]{2,1,0:T(8,128)(2,1)S(1)} collective-permute-done((bf16[1,128,128]{2,1,0:T(8,128)(2,1)S(1)}, bf16[1,128,128]{2,1,0:T(8,128)(2,1)S(1)}, u32[]{:S(2)}, u32[]{:S(2)}) %collective-permute-start.2) | collective-permute-done | bytes 32800 | tf_op jit(solution)/shard_map/pick/ppermute | solution.py:360
  48.5 5.7 %pick.9 = (bf16[64,7296]{1,0:T(8,128)(2,1)}, bf16[64,7296]{1,0:T(8,128)(2,1)}, bf16[64,7296]{1,0:T(8,128)(2,1)}, bf16[64,7296]{1,0:T(8,128)(2,1)}) custom-call(s32[10]{0:T(128)} %pad_add_fusion.w_ref, bf16[128,7168]{1,0:T(8,128)(2,1)} %collective-permute-done.refs_0_, bf16[128,7168]{1,0:T(8,128)(2,1)} %collective-permute-done.1.refs_1_, ...), custom_call_target="tpu_custom_call" | custom-call | flops 469762048 | bytes 7340032 | tf_op jit(solution)/shard_map/pick/pallas_call | solution.py:134
  54.2 2.7 %collective-permute-start.8 = (bf16[128,7168]{1,0:T(8,128)(2,1)}, bf16[128,7168]{1,0:T(8,128)(2,1)}, u32[]{:S(2)}, u32[]{:S(2)}) collective-permute-start(bf16[128,7168]{1,0:T(8,128)(2,1)} %get-tuple-element.52), channel_id=1, source_target_pairs={{0,7},{1,0},{2,1},{3,2},{4,3},{5,4},{6,5},{7,6},{8,15},{9,8},{10,9... | collective-permute-start | bytes 5505032 | tf_op jit(solution)/shard_map/ring_z/ppermute | solution.py:375
  58.1 2.5 collective-permute-start.5
  61.7 5.0 %all-to-all-start.1 = ((bf16[8,128,128]{2,1,0:T(8,128)(2,1)}), bf16[8,128,128]{2,1,0:T(8,128)(2,1)}, u32[]{:S(2)}, u32[]{:S(2)}) async-start(bf16[8,128,128]{2,1,0:T(8,128)(2,1)} %get-tuple-element.53), calls=%async_computation.1 | async-start | bytes 524288 | tf_op jit(solution)/shard_map/pick/all_to_all | solution.py:362
  66.7 5.7 %project.5 = (bf16[32,32,256]{2,1,0:T(8,128)(2,1)}, f32[32,1,32]{2,1,0:T(1,128)}, bf16[256,128]{1,0:T(8,128)(2,1)}) custom-call(s32[10]{0:T(128)} %pad_add_fusion.w_ref, bf16[128,7296]{1,0:T(8,128)(2,1)} %bitcast.6.refs_2_.refs_0_.refs_1_, bf16[128,7296]{1,0:T(8,128)(2,1)} %bitcast.6.refs_2_.refs_0_.refs_1_, ...), custom_call_target="tpu_custom_call" | custom-call | flops 469762048 | bytes 5505024 | tf_op jit(solution)/shard_map/project/pallas_call | solution.py:235
  72.4 27.5 %all-to-all-done.1.refs_2_.refs_3_ = bf16[8,128,128]{2,1,0:T(8,128)(2,1)} async-done(((bf16[8,128,128]{2,1,0:T(8,128)(2,1)}), bf16[8,128,128]{2,1,0:T(8,128)(2,1)}, u32[]{:S(2)}, u32[]{:S(2)}) %all-to-all-start.1) | async-done | bytes 262176 | tf_op jit(solution)/shard_map/pick/all_to_all | solution.py:362
  99.9 5.8 %pick.11 = (bf16[64,7296]{1,0:T(8,128)(2,1)}, bf16[64,7296]{1,0:T(8,128)(2,1)}, bf16[64,7296]{1,0:T(8,128)(2,1)}, bf16[64,7296]{1,0:T(8,128)(2,1)}) custom-call(s32[10]{0:T(128)} %pad_add_fusion.w_ref, bf16[128,7168]{1,0:T(8,128)(2,1)} %collective-permute-done.7.refs_0_, bf16[128,7168]{1,0:T(8,128)(2,1)} %collective-permute-done.8.refs_1_, ...), custom_call_target="tpu_custom_call" | custom-call | flops 469762048 | bytes 7340032 | tf_op jit(solution)/shard_map/pick/pallas_call | solution.py:134
  106.7 3.1 %collective-permute-start.12 = (bf16[128,7168]{1,0:T(8,128)(2,1)}, bf16[128,7168]{1,0:T(8,128)(2,1)}, u32[]{:S(2)}, u32[]{:S(2)}) collective-permute-start(bf16[128,7168]{1,0:T(8,128)(2,1)} %get-tuple-element.59), channel_id=1, source_target_pairs={{0,1},{1,2},{2,3},{3,4},{4,5},{5,6},{6,7},{7,0},{8,9},{9,10},{10,1... | collective-permute-start | bytes 5505032 | tf_op jit(solution)/shard_map/ring_z/ppermute | solution.py:374
  111.2 2.5 collective-permute-start.10
  114.8 6.8 %project.6 = (bf16[32,32,256]{2,1,0:T(8,128)(2,1)}, f32[32,1,32]{2,1,0:T(1,128)}, bf16[256,256]{1,0:T(8,128)(2,1)}) custom-call(s32[10]{0:T(128)} %pad_add_fusion.w_ref, bf16[64,7296]{1,0:T(8,128)(2,1)} %get-tuple-element.47.refs_3_.refs_0_.refs_4_.refs_8_.refs_1_, bf16[64,7296]{1,0:T(8,128)(2,1)} %copy-done.1, ...), custom_call_target="tpu_custom_call", output_to_operand_aliasing={{0}: (16, {}), {1}: (17, {})} | custom-call | flops 939524096 | bytes 7340032 | tf_op jit(solution)/shard_map/project/pallas_call | solution.py:235
  121.6 24.8 %collective-permute-done.12.refs_0_ = bf16[128,7168]{1,0:T(8,128)(2,1)} collective-permute-done((bf16[128,7168]{1,0:T(8,128)(2,1)}, bf16[128,7168]{1,0:T(8,128)(2,1)}, u32[]{:S(2)}, u32[]{:S(2)}) %collective-permute-start.12) | collective-permute-done | bytes 1835040 | tf_op jit(solution)/shard_map/ring_z/ppermute | solution.py:374
  146.6 6.3 %pick.13 = (bf16[64,7296]{1,0:T(8,128)(2,1)}, bf16[64,7296]{1,0:T(8,128)(2,1)}, bf16[64,7296]{1,0:T(8,128)(2,1)}, bf16[64,7296]{1,0:T(8,128)(2,1)}, bf16[128,358...) custom-call(s32[10]{0:T(128)} %pad_add_fusion.w_ref, bf16[128,7168]{1,0:T(8,128)(2,1)} %collective-permute-done.12.refs_0_, ...), custom_call_target="tpu_custom_call" | custom-call | flops 469762048 | bytes 7340032 | tf_op jit(solution)/shard_map/pick/pallas_call | solution.py:134
  158.2 2.8 %collective-permute-start.15 = (bf16[64,7296]{1,0:T(8,128)(2,1)}, bf16[64,7296]{1,0:T(8,128)(2,1)}, u32[]{:S(2)}, u32[]{:S(2)}) collective-permute-start(bf16[64,7296]{1,0:T(8,128)(2,1)} %get-tuple-element.66), channel_id=1, source_target_pairs={{0,16},{1,17},{2,18},{3,19},{4,20},{5,21},{6,22},{7,23},{8,24},{9,... | collective-permute-start | bytes 2801672 | tf_op jit(solution)/shard_map/pick/exchange_x/ppermute | solution.py:354
  161.6 10.5 %collective-permute-done.17.refs_0_ = bf16[128,3584]{1,0:T(8,128)(2,1)} collective-permute-done((bf16[128,3584]{1,0:T(8,128)(2,1)}, bf16[128,3584]{1,0:T(8,128)(2,1)}, u32[]{:S(2)}, u32[]{:S(2)}) %collective-permute-start.17) | collective-permute-done | bytes 917536 | tf_op jit(solution)/shard_map/ring_z/ppermute | solution.py:374
  172.1 8.3 %collective-permute-start.22 = (bf16[128,7168]{1,0:T(8,128)(2,1)}, bf16[128,7168]{1,0:T(8,128)(2,1)}, u32[]{:S(2)}, u32[]{:S(2)}) collective-permute-start(bf16[128,7168]{1,0:T(8,128)(2,1)} %bitcast.3.g_ref), channel_id=1, source_target_pairs={{32,0},{64,32},{96,64},{128,96},{160,128},{192,160},{224,192},{33,... | collective-permute-start | bytes 5505032 | tf_op jit(solution)/shard_map/next_section/ppermute | solution.py:27
  180.5 6.8 %project.7 = (bf16[32,32,256]{2,1,0:T(8,128)(2,1)}, f32[32,1,32]{2,1,0:T(1,128)}, bf16[256,256]{1,0:T(8,128)(2,1)}) custom-call(s32[10]{0:T(128)} %pad_add_fusion.w_ref, bf16[64,7296]{1,0:T(8,128)(2,1)} %get-tuple-element.55.refs_5_.refs_0_.refs_4_.refs_8_, bf16[64,7296]{1,0:T(8,128)(2,1)} %copy-done.2, ...), custom_call_target="tpu_custom_call", output_to_operand_aliasing={{0}: (16, {}), {1}: (17, {})} | custom-call | flops 939524096 | bytes 7340032 | tf_op jit(solution)/shard_map/project/pallas_call | solution.py:235
  187.3 4.0 %pick.15 = (bf16[32,7296]{1,0:T(8,128)(2,1)}, bf16[32,7296]{1,0:T(8,128)(2,1)}, bf16[32,7296]{1,0:T(8,128)(2,1)}, bf16[32,7296]{1,0:T(8,128)(2,1)}) custom-call(s32[10]{0:T(128)} %pad_add_fusion.w_ref, bf16[128,3584]{1,0:T(8,128)(2,1)} %collective-permute-done.17.refs_0_, bf16[128,3584]{1,0:T(8,128)(2,1)} %collective-permute-done.18.refs_1_, ...), custom_call_target="tpu_custom_call" | custom-call | flops 234881024 | bytes 3670016 | tf_op jit(solution)/shard_map/pick/pallas_call | solution.py:134
  192.6 2.8 %collective-permute-start.20 = (bf16[32,7296]{1,0:T(8,128)(2,1)}, bf16[32,7296]{1,0:T(8,128)(2,1)}, u32[]{:S(2)}, u32[]{:S(2)}) collective-permute-start(bf16[32,7296]{1,0:T(8,128)(2,1)} %get-tuple-element.77), channel_id=1, source_target_pairs={{0,16},{1,17},{2,18},{3,19},{4,20},{5,21},{6,22},{7,23},{8,24},{9,... | collective-permute-start | bytes 1400840 | tf_op jit(solution)/shard_map/pick/exchange_x/ppermute | solution.py:354
  197.3 8.5 %collective-permute-done.16.refs_3_.refs_7_.refs_11_.refs_12_ = bf16[64,7296]{1,0:T(8,128)(2,1)} collective-permute-done((bf16[64,7296]{1,0:T(8,128)(2,1)}, bf16[64,7296]{1,0:T(8,128)(2,1)}, u32[]{:S(2)}, u32[]{:S(2)}) %collective-permute-start.16) | collective-permute-done | bytes 933920 | tf_op jit(solution)/shard_map/pick/exchange_x/ppermute | solution.py:354
  205.8 5.8 %collective-permute-start.23 = (bf16[8,7168]{1,0:T(8,128)(2,1)}, bf16[8,7168]{1,0:T(8,128)(2,1)}, u32[]{:S(2)}, u32[]{:S(2)}) collective-permute-start(bf16[8,7168]{1,0:T(8,128)(2,1)} %bitcast.39), channel_id=1, source_target_pairs={{32,0},{64,32},{96,64},{128,96},{160,128},{192,160},{224,192},{33,... | collective-permute-start | bytes 344072 | tf_op jit(solution)/shard_map/next_section/ppermute | solution.py:27
  211.6 6.8 %project.8 = (bf16[32,32,256]{2,1,0:T(8,128)(2,1)}, f32[32,1,32]{2,1,0:T(1,128)}, bf16[256,256]{1,0:T(8,128)(2,1)}) custom-call(s32[10]{0:T(128)} %pad_add_fusion.w_ref, bf16[64,7296]{1,0:T(8,128)(2,1)} %get-tuple-element.64.refs_5_.refs_0_.refs_4_.refs_8_.refs_9_, bf16[64,7296]{1,0:T(8,128)(2,1)} %copy-done.3, ...), custom_call_target="tpu_custom_call", output_to_operand_aliasing={{0}: (16, {}), {1}: (17, {})} | custom-call | flops 939524096 | bytes 7340032 | tf_op jit(solution)/shard_map/project/pallas_call | solution.py:235
  218.9 5.9 %project.9 = (bf16[32,32,256]{2,1,0:T(8,128)(2,1)}, f32[32,1,32]{2,1,0:T(1,128)}, bf16[256,128]{1,0:T(8,128)(2,1)}) custom-call(s32[10]{0:T(128)} %pad_add_fusion.w_ref, bf16[32,7296]{1,0:T(8,128)(2,1)} %get-tuple-element.75.refs_0_.refs_4_.refs_8_.refs_13_, ...), custom_call_target="tpu_custom_call", output_to_operand_aliasing={{0}: (16, {}), {1}: (17, {})} | custom-call | flops 469762048 | bytes 5505024 | tf_op jit(solution)/shard_map/project/pallas_call | solution.py:235
  224.8 10.0 %all-to-all-start.2 = ((f32[32,1,32]{2,1,0:T(1,128)}), f32[32,1,32]{2,1,0:T(1,128)S(1)}, u32[]{:S(2)}, u32[]{:S(2)}) async-start(f32[32,1,32]{2,1,0:T(1,128)} %get-tuple-element.86), calls=%async_computation.2 | async-start | bytes 32768 | tf_op jit(solution)/shard_map/gate_return/all_to_all | solution.py:393
  234.9 10.1 %weight_grad.1.refs_0_ = bf16[256,7168]{1,0:T(8,128)(2,1)} custom-call(s32[10]{0:T(128)} %pad_add_fusion.w_ref, bf16[128,7296]{1,0:T(8,128)(2,1)} %bitcast.6.refs_2_.refs_0_.refs_1_, bf16[64,7296]{1,0:T(8,128)(2,1)} %get-tuple-element.47.refs_3_.refs_0_.refs_4_.refs_8_.refs_1_, bf16[64,7296]{1,0:T(8,128)(2,1)} %copy-done.1, ...), custom_call_target="tpu_custom_call" | custom-call | flops 3758096384 | bytes 18350080 | tf_op jit(solution)/shard_map/weight_grad/pallas_call | solution.py:274
  247.3 4.4 %collective-permute-start.24 = (bf16[24,128]{1,0:T(8,128)(2,1)}, bf16[24,128]{1,0:T(8,128)(2,1)S(1)}, u32[]{:S(2)}, u32[]{:S(2)}) collective-permute-start(bf16[24,128]{1,0:T(8,128)(2,1)} %input_grad.2), channel_id=1, source_target_pairs={{32,0},{64,32},{96,64},{128,96},{160,128},{192,160},{224,192},{33,... | collective-permute-start | bytes 18440 | tf_op jit(solution)/shard_map/input_grad/ppermute | solution.py:27
  254.4 3.5 %input_grad.3 = bf16[128,7168]{1,0:T(8,128)(2,1)} custom-call(s32[10]{0:T(128)S(1)} %copy-done, bf16[128,7168]{1,0:T(8,128)(2,1)} %collective-permute-done.22.g_ref, bf16[24,7168]{1,0:T(8,128)(2,1)S(1)} %pad_maximum_fusion.r_ref, bf16[24,128]{1,0:T(8,128)(2,1)S(1)} %collective-permute-done.24.l_ref), custom_call_target="tpu_custom_call" | custom-call | flops 44040192 | bytes 3670016 | tf_op jit(solution)/shard_map/input_grad/pallas_call | solution.py:293
  (67 shorter events, 22.4 us)
Async XLA Ops:
  0.6 47.3 %collective-permute-start = (bf16[128,7168]{1,0:T(8,128)(2,1)}, bf16[128,7168]{1,0:T(8,128)(2,1)}, u32[]{:S(2)}, u32[]{:S(2)}) collective-permute-start(bf16[128,7168]{1,0:T(8,128)(2,1)} %bitcast.3.g_ref), channel_id=1, source_target_pairs={{0,1},{1,2},{2,3},{3,4},{4,5},{5,6},{6,7},{7,0},{8,9},{9,10},{10,1... | collective-permute-start | bytes 5505032 | tf_op jit(solution)/shard_map/ring_z/ppermute | solution.py:374
  3.2 44.7 %collective-permute-start.1 = (bf16[128,7168]{1,0:T(8,128)(2,1)}, bf16[128,7168]{1,0:T(8,128)(2,1)}, u32[]{:S(2)}, u32[]{:S(2)}) collective-permute-start(bf16[128,7168]{1,0:T(8,128)(2,1)} %bitcast.3.g_ref), channel_id=1, source_target_pairs={{0,7},{1,0},{2,1},{3,2},{4,3},{5,4},{6,5},{7,6},{8,15},{9,8},{10,9... | collective-permute-start | bytes 5505032 | tf_op jit(solution)/shard_map/ring_z/ppermute | solution.py:375
  12.7 41.5 %all-to-all-start = ((bf16[4,32,7296]{2,1,0:T(8,128)(2,1)}), bf16[4,32,7296]{2,1,0:T(8,128)(2,1)}, u32[]{:S(2)}, u32[]{:S(2)}) async-start(bf16[4,32,7296]{2,1,0:T(8,128)(2,1)} %get-tuple-element.45), calls=%async_computation | async-start | bytes 3735552 | tf_op jit(solution)/shard_map/exchange_x/all_to_all | solution.py:368
  17.3 30.6 %collective-permute-start.2 = (bf16[1,128,128]{2,1,0:T(8,128)(2,1)S(1)}, bf16[1,128,128]{2,1,0:T(8,128)(2,1)S(1)}, u32[]{:S(2)}, u32[]{:S(2)}) collective-permute-start(bf16[1,128,128]{2,1,0:T(8,128)(2,1)S(1)} %copy-done.9), channel_id=1, source_target_pairs={{0,1},{1,2},{2,3},{3,4},{4,5},{5,6},{6,7},{7,0},{8,9},{9,10},{10,1... | collective-permute-start | bytes 98312 | tf_op jit(solution)/shard_map/pick/ppermute | solution.py:360
  17.4 30.5 %collective-permute-start.3 = (bf16[1,128,128]{2,1,0:T(8,128)(2,1)S(1)}, bf16[1,128,128]{2,1,0:T(8,128)(2,1)S(1)}, u32[]{:S(2)}, u32[]{:S(2)}) collective-permute-start(bf16[1,128,128]{2,1,0:T(8,128)(2,1)S(1)} %copy-done.9), channel_id=1, source_target_pairs={{0,7},{1,0},{2,1},{3,2},{4,3},{5,4},{6,5},{7,6},{8,15},{9,8},{10,9... | collective-permute-start | bytes 98312 | tf_op jit(solution)/shard_map/pick/ppermute | solution.py:360
  54.2 45.7 %collective-permute-start.7 = (bf16[128,7168]{1,0:T(8,128)(2,1)}, bf16[128,7168]{1,0:T(8,128)(2,1)}, u32[]{:S(2)}, u32[]{:S(2)}) collective-permute-start(bf16[128,7168]{1,0:T(8,128)(2,1)} %get-tuple-element.51), channel_id=1, source_target_pairs={{0,1},{1,2},{2,3},{3,4},{4,5},{5,6},{6,7},{7,0},{8,9},{9,10},{10,1... | collective-permute-start | bytes 5505032 | tf_op jit(solution)/shard_map/ring_z/ppermute | solution.py:374
  54.2 45.7 %collective-permute-start.8 = (bf16[128,7168]{1,0:T(8,128)(2,1)}, bf16[128,7168]{1,0:T(8,128)(2,1)}, u32[]{:S(2)}, u32[]{:S(2)}) collective-permute-start(bf16[128,7168]{1,0:T(8,128)(2,1)} %get-tuple-element.52), channel_id=1, source_target_pairs={{0,7},{1,0},{2,1},{3,2},{4,3},{5,4},{6,5},{7,6},{8,15},{9,8},{10,9... | collective-permute-start | bytes 5505032 | tf_op jit(solution)/shard_map/ring_z/ppermute | solution.py:375
  56.9 48.8 %collective-permute-start.4 = (bf16[64,7296]{1,0:T(8,128)(2,1)}, bf16[64,7296]{1,0:T(8,128)(2,1)S(1)}, u32[]{:S(2)}, u32[]{:S(2)}) collective-permute-start(bf16[64,7296]{1,0:T(8,128)(2,1)} %get-tuple-element.48), channel_id=1, source_target_pairs={{0,8},{1,9},{2,10},{3,11},{4,12},{5,13},{6,14},{7,15},{8,16},{9,17... | collective-permute-start | bytes 2801672 | tf_op jit(solution)/shard_map/pick/exchange_x/ppermute | solution.py:354
  58.1 47.6 %collective-permute-start.5 = (bf16[64,7296]{1,0:T(8,128)(2,1)}, bf16[64,7296]{1,0:T(8,128)(2,1)}, u32[]{:S(2)}, u32[]{:S(2)}) collective-permute-start(bf16[64,7296]{1,0:T(8,128)(2,1)} %get-tuple-element.49), channel_id=1, source_target_pairs={{0,16},{1,17},{2,18},{3,19},{4,20},{5,21},{6,22},{7,23},{8,24},{9,... | collective-permute-start | bytes 2801672 | tf_op jit(solution)/shard_map/pick/exchange_x/ppermute | solution.py:354
  60.6 45.1 %collective-permute-start.6 = (bf16[64,7296]{1,0:T(8,128)(2,1)}, bf16[64,7296]{1,0:T(8,128)(2,1)}, u32[]{:S(2)}, u32[]{:S(2)}) collective-permute-start(bf16[64,7296]{1,0:T(8,128)(2,1)} %get-tuple-element.50), channel_id=1, source_target_pairs={{0,24},{1,25},{2,26},{3,27},{4,28},{5,29},{6,30},{7,31},{8,0},{9,1... | collective-permute-start | bytes 2801672 | tf_op jit(solution)/shard_map/pick/exchange_x/ppermute | solution.py:354
  61.7 38.2 %all-to-all-start.1 = ((bf16[8,128,128]{2,1,0:T(8,128)(2,1)}), bf16[8,128,128]{2,1,0:T(8,128)(2,1)}, u32[]{:S(2)}, u32[]{:S(2)}) async-start(bf16[8,128,128]{2,1,0:T(8,128)(2,1)} %get-tuple-element.53), calls=%async_computation.1 | async-start | bytes 524288 | tf_op jit(solution)/shard_map/pick/all_to_all | solution.py:362
  106.7 39.7 %collective-permute-start.12 = (bf16[128,7168]{1,0:T(8,128)(2,1)}, bf16[128,7168]{1,0:T(8,128)(2,1)}, u32[]{:S(2)}, u32[]{:S(2)}) collective-permute-start(bf16[128,7168]{1,0:T(8,128)(2,1)} %get-tuple-element.59), channel_id=1, source_target_pairs={{0,1},{1,2},{2,3},{3,4},{4,5},{5,6},{6,7},{7,0},{8,9},{9,10},{10,1... | collective-permute-start | bytes 5505032 | tf_op jit(solution)/shard_map/ring_z/ppermute | solution.py:374
  109.8 36.8 %collective-permute-start.13 = (bf16[128,7168]{1,0:T(8,128)(2,1)}, bf16[128,7168]{1,0:T(8,128)(2,1)}, u32[]{:S(2)}, u32[]{:S(2)}) collective-permute-start(bf16[128,7168]{1,0:T(8,128)(2,1)} %get-tuple-element.60), channel_id=1, source_target_pairs={{0,7},{1,0},{2,1},{3,2},{4,3},{5,4},{6,5},{7,6},{8,15},{9,8},{10,9... | collective-permute-start | bytes 5505032 | tf_op jit(solution)/shard_map/ring_z/ppermute | solution.py:375
  110.0 42.9 %collective-permute-start.9 = (bf16[64,7296]{1,0:T(8,128)(2,1)}, bf16[64,7296]{1,0:T(8,128)(2,1)S(1)}, u32[]{:S(2)}, u32[]{:S(2)}) collective-permute-start(bf16[64,7296]{1,0:T(8,128)(2,1)} %get-tuple-element.56), channel_id=1, source_target_pairs={{0,8},{1,9},{2,10},{3,11},{4,12},{5,13},{6,14},{7,15},{8,16},{9,17... | collective-permute-start | bytes 2801672 | tf_op jit(solution)/shard_map/pick/exchange_x/ppermute | solution.py:354
  111.2 41.7 %collective-permute-start.10 = (bf16[64,7296]{1,0:T(8,128)(2,1)}, bf16[64,7296]{1,0:T(8,128)(2,1)}, u32[]{:S(2)}, u32[]{:S(2)}) collective-permute-start(bf16[64,7296]{1,0:T(8,128)(2,1)} %get-tuple-element.57), channel_id=1, source_target_pairs={{0,16},{1,17},{2,18},{3,19},{4,20},{5,21},{6,22},{7,23},{8,24},{9,... | collective-permute-start | bytes 2801672 | tf_op jit(solution)/shard_map/pick/exchange_x/ppermute | solution.py:354
  113.7 40.1 %collective-permute-start.11 = (bf16[64,7296]{1,0:T(8,128)(2,1)}, bf16[64,7296]{1,0:T(8,128)(2,1)}, u32[]{:S(2)}, u32[]{:S(2)}) collective-permute-start(bf16[64,7296]{1,0:T(8,128)(2,1)} %get-tuple-element.58), channel_id=1, source_target_pairs={{0,24},{1,25},{2,26},{3,27},{4,28},{5,29},{6,30},{7,31},{8,0},{9,1... | collective-permute-start | bytes 2801672 | tf_op jit(solution)/shard_map/pick/exchange_x/ppermute | solution.py:354
  153.8 7.5 %copy-start.7 = (s32[1,1,8,32]{3,2,1,0:T(8,128)S(1)}, s32[1,1,8,32]{3,2,1,0:T(8,128)}, u32[]{:S(2)}) copy-start(s32[1,1,8,32]{3,2,1,0:T(8,128)} %param.11) | copy-start | bytes 3076
  153.8 7.6 %copy-start.8 = (s32[1,1,8]{2,1,0:T(1,128)S(1)}, s32[1,1,8]{2,1,0:T(1,128)}, u32[]{:S(2)}) copy-start(s32[1,1,8]{2,1,0:T(1,128)} %param.12) | copy-start | bytes 100
  153.8 18.3 %collective-permute-start.17 = (bf16[128,3584]{1,0:T(8,128)(2,1)}, bf16[128,3584]{1,0:T(8,128)(2,1)}, u32[]{:S(2)}, u32[]{:S(2)}) collective-permute-start(bf16[128,3584]{1,0:T(8,128)(2,1)} %get-tuple-element.70), channel_id=1, source_target_pairs={{0,1},{1,2},{2,3},{3,4},{4,5},{5,6},{6,7},{7,0},{8,9},{9,10},{10,1... | collective-permute-start | bytes 2752520 | tf_op jit(solution)/shard_map/ring_z/ppermute | solution.py:374
  155.7 31.6 %collective-permute-start.18 = (bf16[128,3584]{1,0:T(8,128)(2,1)}, bf16[128,3584]{1,0:T(8,128)(2,1)}, u32[]{:S(2)}, u32[]{:S(2)}) collective-permute-start(bf16[128,3584]{1,0:T(8,128)(2,1)} %get-tuple-element.71), channel_id=1, source_target_pairs={{0,7},{1,0},{2,1},{3,2},{4,3},{5,4},{6,5},{7,6},{8,15},{9,8},{10,9... | collective-permute-start | bytes 2752520 | tf_op jit(solution)/shard_map/ring_z/ppermute | solution.py:375
  157.0 35.6 %collective-permute-start.14 = (bf16[64,7296]{1,0:T(8,128)(2,1)}, bf16[64,7296]{1,0:T(8,128)(2,1)S(1)}, u32[]{:S(2)}, u32[]{:S(2)}) collective-permute-start(bf16[64,7296]{1,0:T(8,128)(2,1)} %get-tuple-element.65), channel_id=1, source_target_pairs={{0,8},{1,9},{2,10},{3,11},{4,12},{5,13},{6,14},{7,15},{8,16},{9,17... | collective-permute-start | bytes 2801672 | tf_op jit(solution)/shard_map/pick/exchange_x/ppermute | solution.py:354
  158.2 38.3 %collective-permute-start.15 = (bf16[64,7296]{1,0:T(8,128)(2,1)}, bf16[64,7296]{1,0:T(8,128)(2,1)}, u32[]{:S(2)}, u32[]{:S(2)}) collective-permute-start(bf16[64,7296]{1,0:T(8,128)(2,1)} %get-tuple-element.66), channel_id=1, source_target_pairs={{0,16},{1,17},{2,18},{3,19},{4,20},{5,21},{6,22},{7,23},{8,24},{9,... | collective-permute-start | bytes 2801672 | tf_op jit(solution)/shard_map/pick/exchange_x/ppermute | solution.py:354
  161.1 44.7 %collective-permute-start.16 = (bf16[64,7296]{1,0:T(8,128)(2,1)}, bf16[64,7296]{1,0:T(8,128)(2,1)}, u32[]{:S(2)}, u32[]{:S(2)}) collective-permute-start(bf16[64,7296]{1,0:T(8,128)(2,1)} %get-tuple-element.67), channel_id=1, source_target_pairs={{0,24},{1,25},{2,26},{3,27},{4,28},{5,29},{6,30},{7,31},{8,0},{9,1... | collective-permute-start | bytes 2801672 | tf_op jit(solution)/shard_map/pick/exchange_x/ppermute | solution.py:354
  172.1 80.6 %collective-permute-start.22 = (bf16[128,7168]{1,0:T(8,128)(2,1)}, bf16[128,7168]{1,0:T(8,128)(2,1)}, u32[]{:S(2)}, u32[]{:S(2)}) collective-permute-start(bf16[128,7168]{1,0:T(8,128)(2,1)} %bitcast.3.g_ref), channel_id=1, source_target_pairs={{32,0},{64,32},{96,64},{128,96},{160,128},{192,160},{224,192},{33,... | collective-permute-start | bytes 5505032 | tf_op jit(solution)/shard_map/next_section/ppermute | solution.py:27
  191.3 27.1 %collective-permute-start.19 = (bf16[32,7296]{1,0:T(8,128)(2,1)}, bf16[32,7296]{1,0:T(8,128)(2,1)}, u32[]{:S(2)}, u32[]{:S(2)}) collective-permute-start(bf16[32,7296]{1,0:T(8,128)(2,1)} %get-tuple-element.76), channel_id=1, source_target_pairs={{0,8},{1,9},{2,10},{3,11},{4,12},{5,13},{6,14},{7,15},{8,16},{9,17... | collective-permute-start | bytes 1400840 | tf_op jit(solution)/shard_map/pick/exchange_x/ppermute | solution.py:354
  192.6 19.0 %copy-start.3 = (bf16[64,7296]{1,0:T(8,128)(2,1)}, bf16[64,7296]{1,0:T(8,128)(2,1)S(1)}, u32[]{:S(2)}) copy-start(bf16[64,7296]{1,0:T(8,128)(2,1)S(1)} %collective-permute-done.14.refs_1_.refs_5_.refs_9_.refs_10_) | copy-start | bytes 2801668
  192.6 25.8 %collective-permute-start.20 = (bf16[32,7296]{1,0:T(8,128)(2,1)}, bf16[32,7296]{1,0:T(8,128)(2,1)}, u32[]{:S(2)}, u32[]{:S(2)}) collective-permute-start(bf16[32,7296]{1,0:T(8,128)(2,1)} %get-tuple-element.77), channel_id=1, source_target_pairs={{0,16},{1,17},{2,18},{3,19},{4,20},{5,21},{6,22},{7,23},{8,24},{9,... | collective-permute-start | bytes 1400840 | tf_op jit(solution)/shard_map/pick/exchange_x/ppermute | solution.py:354
  196.5 22.3 %collective-permute-start.21 = (bf16[32,7296]{1,0:T(8,128)(2,1)}, bf16[32,7296]{1,0:T(8,128)(2,1)}, u32[]{:S(2)}, u32[]{:S(2)}) collective-permute-start(bf16[32,7296]{1,0:T(8,128)(2,1)} %get-tuple-element.78), channel_id=1, source_target_pairs={{0,24},{1,25},{2,26},{3,27},{4,28},{5,29},{6,30},{7,31},{8,0},{9,1... | collective-permute-start | bytes 1400840 | tf_op jit(solution)/shard_map/pick/exchange_x/ppermute | solution.py:354
  205.8 45.9 %collective-permute-start.23 = (bf16[8,7168]{1,0:T(8,128)(2,1)}, bf16[8,7168]{1,0:T(8,128)(2,1)}, u32[]{:S(2)}, u32[]{:S(2)}) collective-permute-start(bf16[8,7168]{1,0:T(8,128)(2,1)} %bitcast.39), channel_id=1, source_target_pairs={{32,0},{64,32},{96,64},{128,96},{160,128},{192,160},{224,192},{33,... | collective-permute-start | bytes 344072 | tf_op jit(solution)/shard_map/next_section/ppermute | solution.py:27
  224.8 20.1 %all-to-all-start.2 = ((f32[32,1,32]{2,1,0:T(1,128)}), f32[32,1,32]{2,1,0:T(1,128)S(1)}, u32[]{:S(2)}, u32[]{:S(2)}) async-start(f32[32,1,32]{2,1,0:T(1,128)} %get-tuple-element.86), calls=%async_computation.2 | async-start | bytes 32768 | tf_op jit(solution)/shard_map/gate_return/all_to_all | solution.py:393
  245.0 9.4 %copy-start = (s32[10]{0:T(128)S(1)}, s32[10]{0:T(128)}, u32[]{:S(2)}) copy-start(s32[10]{0:T(128)} %pad_add_fusion.w_ref) | copy-start | bytes 124
  247.3 7.1 %collective-permute-start.24 = (bf16[24,128]{1,0:T(8,128)(2,1)}, bf16[24,128]{1,0:T(8,128)(2,1)S(1)}, u32[]{:S(2)}, u32[]{:S(2)}) collective-permute-start(bf16[24,128]{1,0:T(8,128)(2,1)} %input_grad.2), channel_id=1, source_target_pairs={{32,0},{64,32},{96,64},{128,96},{160,128},{192,160},{224,192},{33,... | collective-permute-start | bytes 18440 | tf_op jit(solution)/shard_map/input_grad/ppermute | solution.py:27
  (6 other events, 8.4 us)

commit v4 on v3

--- a/solution.py
+++ b/solution.py
@@ -77,7 +77,7 @@
     count, width = grad.shape
     cap = tokens.shape[1]
 
-    def kernel(w_ref, g_ref, t_ref, s_ref, own_ref, meta_ref, out_ref):
+    def kernel(w_ref, g_ref, t_ref, s_ref, own_ref, out_ref):
         slot = lax.broadcasted_iota(jnp.int32, (1, cap), 1)
         for k in range(NX):
             lines = []
@@ -94,8 +94,6 @@
             table = jnp.concatenate([table, jnp.zeros((2 * META, LANES - cap), F32)], 1)
             table = jnp.concatenate([table, jnp.zeros((LANES - 2 * META, LANES), F32)], 0).T
             own_ref[0, k * cap : (k + 1) * cap, :] = table[:cap].astype(BF)
-            for z in range(NZ):
-                meta_ref[z, k * cap : (k + 1) * cap, :] = table[:cap].astype(BF)
         picked(w_ref, own_ref[0], [g_ref], [out_ref.at[lax.rem(w_ref[0] + k, NX)] for k in range(NX)], 0)
 
     full = width + LANES
@@ -103,48 +101,53 @@
         kernel,
         (1,),
         [whole(x.shape) for x in (grad, tokens, gates)],
-        [whole((n, NX * cap, LANES)) for n in (1, NZ)] + [whole((NX, cap, full))],
-        [jax.ShapeDtypeStruct((n, NX * cap, LANES), BF) for n in (1, NZ)]
-        + [jax.ShapeDtypeStruct((NX, cap, full), BF)],
+        [whole((1, NX * cap, LANES)), whole((NX, cap, full))],
+        [jax.ShapeDtypeStruct((1, NX * cap, LANES), BF), jax.ShapeDtypeStruct((NX, cap, full), BF)],
         flops=2 * NX * cap * count * width,
         nbytes=6 * count * width,
     )(where, grad, tokens, gates)
 
 
-def pick_rows(where, blocks, metas, places, after, cut):
+def pick_rows(where, blocks, tables, after, cut):
     n = len(blocks)
     flat = [x for block in blocks for x in block]
     tokens = flat[0].shape[0]
-    width = sum(x.shape[1] for x in blocks[0])
-    slots = metas[0].shape[1]
-    cap = slots // NX
+    full = sum(x.shape[1] for x in blocks[0]) + (LANES if tables else 0)
+    width = full - LANES
+    cap = tokens // NX
     mid = width // 2
-    cuts = 2 if cut else 0
 
     def kernel(w_ref, *refs):
-        outs = refs[len(refs) - NX - cuts :]
+        outs = refs[len(refs) - len(shapes) :]
         for b in range(n):
-            parts = refs[b * len(blocks[b]) : (b + 1) * len(blocks[b])]
-            picked(w_ref, refs[len(flat) + b][0], parts, outs[:NX], b * cap)
+            parts = list(refs[b * len(blocks[b]) : (b + 1) * len(blocks[b])])
+            if tables:
+                meta = refs[len(flat) + b][0]
+                outs[NX + b][:, :width] = parts[0][...]
+                outs[NX + b][:, width:] = meta
+            else:
+                own = parts[-1].shape[1] - LANES
+                meta = parts[-1][:, own:]
+                parts[-1] = parts[-1].at[:, :own]
+            picked(w_ref, meta, parts, outs[:NX], b * cap)
         if cut:
             outs[NX][...] = refs[0][:, :mid]
             outs[NX + 1][...] = refs[1][:, mid:]
 
-    shapes = [(n * cap, width + LANES)] * NX + [(tokens, mid)] * cuts
+    shapes = [(n * cap, full)] * NX
+    if tables:
+        shapes += [(tokens, full)] * n
+    if cut:
+        shapes += [(tokens, mid), (tokens, full - mid)]
     return call(
         kernel,
         (1,),
-        [whole(x.shape) for x in flat]
-        + [
-            pl.BlockSpec((1, slots, LANES), lambda j, w, d=d: (0 if d is None else lax.rem(w[1] + d, NZ), 0, 0))
-            for d in places
-        ]
-        + [HBM] * len(after),
+        [whole(x.shape) for x in flat + tables] + [HBM] * len(after),
         [whole(x) for x in shapes],
         [jax.ShapeDtypeStruct(x, BF) for x in shapes],
-        flops=2 * n * slots * tokens * width,
+        flops=2 * n * tokens * tokens * width,
         nbytes=4 * n * tokens * width,
-    )(where, *flat, *metas, *after)
+    )(where, *flat, *tables, *after)
 
 
 def hold(arrays, after):
@@ -356,12 +359,8 @@
     last = NZ // 2
     order = [[0]] + [[NZ - t, t] for t in range(1, last)] + [[last]]
     with jax.named_scope("pick"):
-        own, spread, rows = begin(where, grad, tokens, gates)
+        own, rows = begin(where, grad, tokens, gates)
         near = [lax.ppermute(own, "expert", shift_z(k)) for k in (1, -1)]
-        line = [[x * NZ + z for z in range(NZ)] for x in range(NX)]
-        metas = lax.all_to_all(
-            spread, "expert", split_axis=0, concat_axis=0, axis_index_groups=line, tiled=True
-        )
     up = down = grad
     with jax.named_scope("exchange_x"):
         across = [[x * NZ + z for x in range(NX)] for z in range(NZ)]
@@ -375,8 +374,7 @@
             down = lax.ppermute(down, "expert", shift_z(-1))
         with jax.named_scope("pick"):
             blocks = [[up], [down]] if t < last else [[up, down]]
-            tables, places = (near, [None, None]) if t == 1 else ([metas] * len(blocks), order[t])
-            got = pick_rows(where, blocks, tables, places, scaled[t - 2 : t - 1], t == last - 1)
+            got = pick_rows(where, blocks, near if t == 1 else [], scaled[t - 2 : t - 1], t == last - 1)
             rows = got[:NX]
             if t < last:
                 up, down = hold(got[NX:] or [up, down], arrived[t - 1][-3:] + [rows[0]])

time: 259 us -> 256 us (0.988)
  starting transfers between devices: 74.7 us -> 62.1 us
  waiting for transfers between devices: 103 us -> 112 us
    ppermute x4, waiting for transfers between devices: 35.3 us -> 70 us  [shards(): up = lax.ppermute(up, 'expert', shift_z(1))]
    all_to_all x1 -> x0, waiting for transfers between devices: 27.5 us -> none  [shards(): lax.all_to_all(spread, 'expert', split_axis=0, concat_axis=0, axis_index_...]
    all_to_all x1 -> x0, starting transfers between devices: 4.96 us -> none  [shards(): lax.all_to_all(spread, 'expert', split_axis=0, concat_axis=0, axis_index_...]
    ppermute x3, starting transfers between devices: 18.5 us -> 14.9 us  [passed_along(): lax.ppermute(value, axis, [(source, source + steps) for source in range(i...]
    ppermute x4, starting transfers between devices: 7.55 us -> 3.98 us  [shards(): up = lax.ppermute(up, 'expert', shift_z(1))]
  transfers between devices with their start and end apart: 28 -> 27, of which waited for: 10 -> 9; matrix products, arithmetic and copies ran while one was open for 1% -> 1% of each run, Pallas kernels for 27% -> 28%
where the time goes in v4:
time: 256 us
  waiting for transfers between devices  112 us (44%)
  Pallas kernels  74.8 us (29%)
  starting transfers between devices  62.1 us (24%)
  local copies, waits for them, and re-layouts  3.29 us (1%)
  other arithmetic  3.14 us (1%)
    ppermute x4, waiting for transfers between devices, shards(): up = lax.ppermute(up, 'expert', shift_z(1))  70 us
    pallas_call x5, Pallas kernels, project(): call(kernel, (steps,), [columns(rows, TILE, 0)] * arrays + [columns(rows,...  32.1 us
    ppermute x2, waiting for transfers between devices, shards(): near = [lax.ppermute(own, 'expert', shift_z(k)) for k in (1, -1)]  27.9 us
    pallas_call x4, Pallas kernels, pick_rows(): call(kernel, (1,), [whole(x.shape) for x in flat + tables] + [HBM] * len(...  23.2 us
    ppermute x12, starting transfers between devices, exchanged(): lax.ppermute(rows[k], 'expert', shift_x(k))  17.6 us
    ppermute x3, starting transfers between devices, passed_along(): lax.ppermute(value, axis, [(source, source + steps) for source in range(i...  14.9 us
    ppermute x12, waiting for transfers between devices, exchanged(): lax.ppermute(rows[k], 'expert', shift_x(k))  12.2 us
    ppermute x4, starting transfers between devices, shards(): down = lax.ppermute(down, 'expert', shift_z(-1))  10.6 us
  transfers between devices with their start and end apart: 27, of which 9 were waited for; matrix products, arithmetic and copies ran while one was open for 1% of the time, Pallas kernels for 28%

profile of v4, /device:TPU:1, one launch (start us, length us, event | category | flops | bytes accessed | tf_op | source)
XLA Modules:
  0.0 255.8 jit_solution(14497092539055230514)
XLA Ops:
  0.6 2.5 collective-permute-start
  3.2 4.0 %collective-permute-start.1 = (bf16[128,7168]{1,0:T(8,128)(2,1)}, bf16[128,7168]{1,0:T(8,128)(2,1)}, u32[]{:S(2)}, u32[]{:S(2)}) collective-permute-start(bf16[128,7168]{1,0:T(8,128)(2,1)} %bitcast.3.g_ref), channel_id=1, source_target_pairs={{0,7},{1,0},{2,1},{3,2},{4,3},{5,4},{6,5},{7,6},{8,15},{9,8},{10,9... | collective-permute-start | bytes 5505032 | tf_op jit(solution)/shard_map/ring_z/ppermute | solution.py:374
  8.5 4.2 %pick.8 = (bf16[1,128,128]{2,1,0:T(8,128)(2,1)}, bf16[4,32,7296]{2,1,0:T(8,128)(2,1)}) custom-call(s32[10]{0:T(128)} %pad_add_fusion.w_ref, bf16[128,7168]{1,0:T(8,128)(2,1)} %bitcast.3.g_ref, s32[8,32]{1,0:T(8,128)} %bitcast.35, f32[8,32]{1,0:T(8,128)} %bitcast.36), custom_call_target="tpu_custom_call" | custom-call | flops 234881024 | bytes 5505024 | tf_op jit(solution)/shard_map/pick/pallas_call | solution.py:100
  12.7 4.5 %all-to-all-start = ((bf16[4,32,7296]{2,1,0:T(8,128)(2,1)}), bf16[4,32,7296]{2,1,0:T(8,128)(2,1)}, u32[]{:S(2)}, u32[]{:S(2)}) async-start(bf16[4,32,7296]{2,1,0:T(8,128)(2,1)} %get-tuple-element.46), calls=%async_computation | async-start | bytes 3735552 | tf_op jit(solution)/shard_map/exchange_x/all_to_all | solution.py:367
  17.3 2.7 %collective-permute-start.3 = (bf16[1,128,128]{2,1,0:T(8,128)(2,1)S(1)}, bf16[1,128,128]{2,1,0:T(8,128)(2,1)S(1)}, u32[]{:S(2)}, u32[]{:S(2)}) collective-permute-start(bf16[1,128,128]{2,1,0:T(8,128)(2,1)S(1)} %copy-done.9), channel_id=1, source_target_pairs={{0,7},{1,0},{2,1},{3,2},{4,3},{5,4},{6,5},{7,6},{8,15},{9,8},{10,9... | collective-permute-start | bytes 98312 | tf_op jit(solution)/shard_map/pick/ppermute | solution.py:363
  20.0 27.9 %collective-permute-done.2.refs_2_ = bf16[1,128,128]{2,1,0:T(8,128)(2,1)S(1)} collective-permute-done((bf16[1,128,128]{2,1,0:T(8,128)(2,1)S(1)}, bf16[1,128,128]{2,1,0:T(8,128)(2,1)S(1)}, u32[]{:S(2)}, u32[]{:S(2)}) %collective-permute-start.2) | collective-permute-done | bytes 32800 | tf_op jit(solution)/shard_map/pick/ppermute | solution.py:363
  48.5 7.0 %pick.9 = (bf16[64,7296]{1,0:T(8,128)(2,1)}, bf16[64,7296]{1,0:T(8,128)(2,1)}, bf16[64,7296]{1,0:T(8,128)(2,1)}, bf16[64,7296]{1,0:T(8,128)(2,1)}, bf16[128,7296]{1,0:T(8,128)(2,1)}, /*index=5*/bf16[128,7296]{1,0:T(8,128)(2,1)}) custom-call(s32[10]{0:T(128)} %pad_add_fusion.w_ref, bf16[128,7168]{1,0:T(8,128)(2,1)} %collective-permute-done.refs_0_, ...), custom_call_target="tpu_custom_call" | custom-call | flops 469762048 | bytes 7340032 | tf_op jit(solution)/shard_map/pick/pallas_call | solution.py:142
  55.5 2.7 %collective-permute-start.8 = (bf16[128,7296]{1,0:T(8,128)(2,1)}, bf16[128,7296]{1,0:T(8,128)(2,1)}, u32[]{:S(2)}, u32[]{:S(2)}) collective-permute-start(bf16[128,7296]{1,0:T(8,128)(2,1)} %get-tuple-element.55), channel_id=1, source_target_pairs={{0,7},{1,0},{2,1},{3,2},{4,3},{5,4},{6,5},{7,6},{8,15},{9,8},{10,9... | collective-permute-start | bytes 5603336 | tf_op jit(solution)/shard_map/ring_z/ppermute | solution.py:374
  59.4 2.4 collective-permute-start.5
  63.0 5.7 %project.5 = (bf16[32,32,256]{2,1,0:T(8,128)(2,1)}, f32[32,1,32]{2,1,0:T(1,128)}, bf16[256,128]{1,0:T(8,128)(2,1)}) custom-call(s32[10]{0:T(128)} %pad_add_fusion.w_ref, bf16[128,7296]{1,0:T(8,128)(2,1)} %bitcast.6.refs_2_.refs_0_.refs_1_, bf16[128,7296]{1,0:T(8,128)(2,1)} %bitcast.6.refs_2_.refs_0_.refs_1_, ...), custom_call_target="tpu_custom_call" | custom-call | flops 469762048 | bytes 5505024 | tf_op jit(solution)/shard_map/project/pallas_call | solution.py:238
  68.7 29.4 %collective-permute-done.7.refs_0_ = bf16[128,7296]{1,0:T(8,128)(2,1)} collective-permute-done((bf16[128,7296]{1,0:T(8,128)(2,1)}, bf16[128,7296]{1,0:T(8,128)(2,1)}, u32[]{:S(2)}, u32[]{:S(2)}) %collective-permute-start.7) | collective-permute-done | bytes 1867808 | tf_op jit(solution)/shard_map/ring_z/ppermute | solution.py:373
  98.1 5.8 %pick.11 = (bf16[64,7296]{1,0:T(8,128)(2,1)}, bf16[64,7296]{1,0:T(8,128)(2,1)}, bf16[64,7296]{1,0:T(8,128)(2,1)}, bf16[64,7296]{1,0:T(8,128)(2,1)}) custom-call(s32[10]{0:T(128)} %pad_add_fusion.w_ref, bf16[128,7296]{1,0:T(8,128)(2,1)} %collective-permute-done.7.refs_0_, bf16[128,7296]{1,0:T(8,128)(2,1)} %collective-permute-done.8.refs_1_, ...), custom_call_target="tpu_custom_call" | custom-call | flops 469762048 | bytes 7340032 | tf_op jit(solution)/shard_map/pick/pallas_call | solution.py:142
  107.6 2.8 %collective-permute-start.10 = (bf16[64,7296]{1,0:T(8,128)(2,1)}, bf16[64,7296]{1,0:T(8,128)(2,1)S(1)}, u32[]{:S(2)}, u32[]{:S(2)}) collective-permute-start(bf16[64,7296]{1,0:T(8,128)(2,1)} %get-tuple-element.59), channel_id=1, source_target_pairs={{0,16},{1,17},{2,18},{3,19},{4,20},{5,21},{6,22},{7,23},{8,24},{9,... | collective-permute-start | bytes 2801672 | tf_op jit(solution)/shard_map/pick/exchange_x/ppermute | solution.py:357
  111.8 6.8 %project.6 = (bf16[32,32,256]{2,1,0:T(8,128)(2,1)}, f32[32,1,32]{2,1,0:T(1,128)}, bf16[256,256]{1,0:T(8,128)(2,1)}) custom-call(s32[10]{0:T(128)} %pad_add_fusion.w_ref, bf16[64,7296]{1,0:T(8,128)(2,1)} %get-tuple-element.48.refs_3_.refs_0_.refs_4_.refs_8_.refs_1_, bf16[64,7296]{1,0:T(8,128)(2,1)} %copy-done.1, ...), custom_call_target="tpu_custom_call", output_to_operand_aliasing={{0}: (16, {}), {1}: (17, {})} | custom-call | flops 939524096 | bytes 7340032 | tf_op jit(solution)/shard_map/project/pallas_call | solution.py:238
  118.6 28.0 %collective-permute-done.12.refs_0_ = bf16[128,7296]{1,0:T(8,128)(2,1)} collective-permute-done((bf16[128,7296]{1,0:T(8,128)(2,1)}, bf16[128,7296]{1,0:T(8,128)(2,1)}, u32[]{:S(2)}, u32[]{:S(2)}) %collective-permute-start.12) | collective-permute-done | bytes 1867808 | tf_op jit(solution)/shard_map/ring_z/ppermute | solution.py:373
  146.6 6.4 %pick.13 = (bf16[64,7296]{1,0:T(8,128)(2,1)}, bf16[64,7296]{1,0:T(8,128)(2,1)}, bf16[64,7296]{1,0:T(8,128)(2,1)}, bf16[64,7296]{1,0:T(8,128)(2,1)}, bf16[128,358...) custom-call(s32[10]{0:T(128)} %pad_add_fusion.w_ref, bf16[128,7296]{1,0:T(8,128)(2,1)} %collective-permute-done.12.refs_0_, ...), custom_call_target="tpu_custom_call" | custom-call | flops 469762048 | bytes 7340032 | tf_op jit(solution)/shard_map/pick/pallas_call | solution.py:142
  154.4 2.2 collective-permute-start.18
  157.9 2.4 collective-permute-start.15
  161.7 12.6 %collective-permute-done.17.refs_0_ = bf16[128,3584]{1,0:T(8,128)(2,1)} collective-permute-done((bf16[128,3584]{1,0:T(8,128)(2,1)}, bf16[128,3584]{1,0:T(8,128)(2,1)}, u32[]{:S(2)}, u32[]{:S(2)}) %collective-permute-start.17) | collective-permute-done | bytes 917536 | tf_op jit(solution)/shard_map/ring_z/ppermute | solution.py:373
  174.3 5.8 %collective-permute-start.22 = (bf16[128,7168]{1,0:T(8,128)(2,1)}, bf16[128,7168]{1,0:T(8,128)(2,1)}, u32[]{:S(2)}, u32[]{:S(2)}) collective-permute-start(bf16[128,7168]{1,0:T(8,128)(2,1)} %bitcast.3.g_ref), channel_id=1, source_target_pairs={{32,0},{64,32},{96,64},{128,96},{160,128},{192,160},{224,192},{33,... | collective-permute-start | bytes 5505032 | tf_op jit(solution)/shard_map/next_section/ppermute | solution.py:27
  180.1 6.8 %project.7 = (bf16[32,32,256]{2,1,0:T(8,128)(2,1)}, f32[32,1,32]{2,1,0:T(1,128)}, bf16[256,256]{1,0:T(8,128)(2,1)}) custom-call(s32[10]{0:T(128)} %pad_add_fusion.w_ref, bf16[64,7296]{1,0:T(8,128)(2,1)} %get-tuple-element.57.refs_5_.refs_0_.refs_4_.refs_8_, ...), custom_call_target="tpu_custom_call", output_to_operand_aliasing={{0}: (16, {}), {1}: (17, {})} | custom-call | flops 939524096 | bytes 7340032 | tf_op jit(solution)/shard_map/project/pallas_call | solution.py:238
  187.0 4.1 %pick.15 = (bf16[32,7296]{1,0:T(8,128)(2,1)}, bf16[32,7296]{1,0:T(8,128)(2,1)}, bf16[32,7296]{1,0:T(8,128)(2,1)}, bf16[32,7296]{1,0:T(8,128)(2,1)}) custom-call(s32[10]{0:T(128)} %pad_add_fusion.w_ref, bf16[128,3584]{1,0:T(8,128)(2,1)} %collective-permute-done.17.refs_0_, bf16[128,3712]{1,0:T(8,128)(2,1)} %collective-permute-done.18.refs_1_, ...), custom_call_target="tpu_custom_call" | custom-call | flops 234881024 | bytes 3670016 | tf_op jit(solution)/shard_map/pick/pallas_call | solution.py:142
  192.3 2.4 collective-permute-start.20
  194.7 3.1 %collective-permute-done.15.refs_2_.refs_6_.refs_10_.refs_11_ = bf16[64,7296]{1,0:T(8,128)(2,1)} collective-permute-done((bf16[64,7296]{1,0:T(8,128)(2,1)}, bf16[64,7296]{1,0:T(8,128)(2,1)}, u32[]{:S(2)}, u32[]{:S(2)}) %collective-permute-start.15) | collective-permute-done | bytes 933920 | tf_op jit(solution)/shard_map/pick/exchange_x/ppermute | solution.py:357
  198.6 5.4 %collective-permute-done.16.refs_3_.refs_7_.refs_11_.refs_12_ = bf16[64,7296]{1,0:T(8,128)(2,1)} collective-permute-done((bf16[64,7296]{1,0:T(8,128)(2,1)}, bf16[64,7296]{1,0:T(8,128)(2,1)}, u32[]{:S(2)}, u32[]{:S(2)}) %collective-permute-start.16) | collective-permute-done | bytes 933920 | tf_op jit(solution)/shard_map/pick/exchange_x/ppermute | solution.py:357
  204.0 5.2 %collective-permute-start.23 = (bf16[8,7168]{1,0:T(8,128)(2,1)}, bf16[8,7168]{1,0:T(8,128)(2,1)}, u32[]{:S(2)}, u32[]{:S(2)}) collective-permute-start(bf16[8,7168]{1,0:T(8,128)(2,1)} %bitcast.39), channel_id=1, source_target_pairs={{32,0},{64,32},{96,64},{128,96},{160,128},{192,160},{224,192},{33,... | collective-permute-start | bytes 344072 | tf_op jit(solution)/shard_map/next_section/ppermute | solution.py:27
  209.2 6.8 %project.8 = (bf16[32,32,256]{2,1,0:T(8,128)(2,1)}, f32[32,1,32]{2,1,0:T(1,128)}, bf16[256,256]{1,0:T(8,128)(2,1)}) custom-call(s32[10]{0:T(128)} %pad_add_fusion.w_ref, bf16[64,7296]{1,0:T(8,128)(2,1)} %get-tuple-element.66.refs_5_.refs_0_.refs_4_.refs_8_.refs_9_, bf16[64,7296]{1,0:T(8,128)(2,1)} %copy-done.3, ...), custom_call_target="tpu_custom_call", output_to_operand_aliasing={{0}: (16, {}), {1}: (17, {})} | custom-call | flops 939524096 | bytes 7340032 | tf_op jit(solution)/shard_map/project/pallas_call | solution.py:238
  219.7 6.0 %project.9 = (bf16[32,32,256]{2,1,0:T(8,128)(2,1)}, f32[32,1,32]{2,1,0:T(1,128)}, bf16[256,128]{1,0:T(8,128)(2,1)}) custom-call(s32[10]{0:T(128)} %pad_add_fusion.w_ref, bf16[32,7296]{1,0:T(8,128)(2,1)} %get-tuple-element.77.refs_0_.refs_4_.refs_8_.refs_13_, ...), custom_call_target="tpu_custom_call", output_to_operand_aliasing={{0}: (16, {}), {1}: (17, {})} | custom-call | flops 469762048 | bytes 5505024 | tf_op jit(solution)/shard_map/project/pallas_call | solution.py:238
  225.7 7.7 %all-to-all-start.1 = ((f32[32,1,32]{2,1,0:T(1,128)}), f32[32,1,32]{2,1,0:T(1,128)S(1)}, u32[]{:S(2)}, u32[]{:S(2)}) async-start(f32[32,1,32]{2,1,0:T(1,128)} %get-tuple-element.88), calls=%async_computation.1 | async-start | bytes 32768 | tf_op jit(solution)/shard_map/gate_return/all_to_all | solution.py:391
  233.3 10.1 %weight_grad.1.refs_0_ = bf16[256,7168]{1,0:T(8,128)(2,1)} custom-call(s32[10]{0:T(128)} %pad_add_fusion.w_ref, bf16[128,7296]{1,0:T(8,128)(2,1)} %bitcast.6.refs_2_.refs_0_.refs_1_, bf16[64,7296]{1,0:T(8,128)(2,1)} %get-tuple-element.48.refs_3_.refs_0_.refs_4_.refs_8_.refs_1_, bf16[64,7296]{1,0:T(8,128)(2,1)} %copy-done.1, ...), custom_call_target="tpu_custom_call" | custom-call | flops 3758096384 | bytes 18350080 | tf_op jit(solution)/shard_map/weight_grad/pallas_call | solution.py:277
  245.7 3.9 %collective-permute-start.24 = (bf16[24,128]{1,0:T(8,128)(2,1)}, bf16[24,128]{1,0:T(8,128)(2,1)S(1)}, u32[]{:S(2)}, u32[]{:S(2)}) collective-permute-start(bf16[24,128]{1,0:T(8,128)(2,1)} %input_grad.2), channel_id=1, source_target_pairs={{32,0},{64,32},{96,64},{128,96},{160,128},{192,160},{224,192},{33,... | collective-permute-start | bytes 18440 | tf_op jit(solution)/shard_map/input_grad/ppermute | solution.py:27
  252.3 3.6 %input_grad.3 = bf16[128,7168]{1,0:T(8,128)(2,1)} custom-call(s32[10]{0:T(128)S(1)} %copy-done, bf16[128,7168]{1,0:T(8,128)(2,1)} %collective-permute-done.22.g_ref, bf16[24,7168]{1,0:T(8,128)(2,1)S(1)} %pad_maximum_fusion.r_ref, bf16[24,128]{1,0:T(8,128)(2,1)S(1)} %collective-permute-done.24.l_ref), custom_call_target="tpu_custom_call" | custom-call | flops 44040192 | bytes 3670016 | tf_op jit(solution)/shard_map/input_grad/pallas_call | solution.py:296
  (65 shorter events, 24.1 us)
Async XLA Ops:
  0.6 47.3 %collective-permute-start = (bf16[128,7168]{1,0:T(8,128)(2,1)}, bf16[128,7168]{1,0:T(8,128)(2,1)}, u32[]{:S(2)}, u32[]{:S(2)}) collective-permute-start(bf16[128,7168]{1,0:T(8,128)(2,1)} %bitcast.3.g_ref), channel_id=1, source_target_pairs={{0,1},{1,2},{2,3},{3,4},{4,5},{5,6},{6,7},{7,0},{8,9},{9,10},{10,1... | collective-permute-start | bytes 5505032 | tf_op jit(solution)/shard_map/ring_z/ppermute | solution.py:373
  3.2 44.7 %collective-permute-start.1 = (bf16[128,7168]{1,0:T(8,128)(2,1)}, bf16[128,7168]{1,0:T(8,128)(2,1)}, u32[]{:S(2)}, u32[]{:S(2)}) collective-permute-start(bf16[128,7168]{1,0:T(8,128)(2,1)} %bitcast.3.g_ref), channel_id=1, source_target_pairs={{0,7},{1,0},{2,1},{3,2},{4,3},{5,4},{6,5},{7,6},{8,15},{9,8},{10,9... | collective-permute-start | bytes 5505032 | tf_op jit(solution)/shard_map/ring_z/ppermute | solution.py:374
  12.7 4.6 %copy-start.9 = (bf16[1,128,128]{2,1,0:T(8,128)(2,1)S(1)}, bf16[1,128,128]{2,1,0:T(8,128)(2,1)}, u32[]{:S(2)}) copy-start(bf16[1,128,128]{2,1,0:T(8,128)(2,1)} %get-tuple-element.47) | copy-start | bytes 98308
  12.7 42.9 %all-to-all-start = ((bf16[4,32,7296]{2,1,0:T(8,128)(2,1)}), bf16[4,32,7296]{2,1,0:T(8,128)(2,1)}, u32[]{:S(2)}, u32[]{:S(2)}) async-start(bf16[4,32,7296]{2,1,0:T(8,128)(2,1)} %get-tuple-element.46), calls=%async_computation | async-start | bytes 3735552 | tf_op jit(solution)/shard_map/exchange_x/all_to_all | solution.py:367
  17.2 30.6 %collective-permute-start.2 = (bf16[1,128,128]{2,1,0:T(8,128)(2,1)S(1)}, bf16[1,128,128]{2,1,0:T(8,128)(2,1)S(1)}, u32[]{:S(2)}, u32[]{:S(2)}) collective-permute-start(bf16[1,128,128]{2,1,0:T(8,128)(2,1)S(1)} %copy-done.9), channel_id=1, source_target_pairs={{0,1},{1,2},{2,3},{3,4},{4,5},{5,6},{6,7},{7,0},{8,9},{9,10},{10,1... | collective-permute-start | bytes 98312 | tf_op jit(solution)/shard_map/pick/ppermute | solution.py:363
  17.3 30.5 %collective-permute-start.3 = (bf16[1,128,128]{2,1,0:T(8,128)(2,1)S(1)}, bf16[1,128,128]{2,1,0:T(8,128)(2,1)S(1)}, u32[]{:S(2)}, u32[]{:S(2)}) collective-permute-start(bf16[1,128,128]{2,1,0:T(8,128)(2,1)S(1)} %copy-done.9), channel_id=1, source_target_pairs={{0,7},{1,0},{2,1},{3,2},{4,3},{5,4},{6,5},{7,6},{8,15},{9,8},{10,9... | collective-permute-start | bytes 98312 | tf_op jit(solution)/shard_map/pick/ppermute | solution.py:363
  55.5 42.6 %collective-permute-start.7 = (bf16[128,7296]{1,0:T(8,128)(2,1)}, bf16[128,7296]{1,0:T(8,128)(2,1)}, u32[]{:S(2)}, u32[]{:S(2)}) collective-permute-start(bf16[128,7296]{1,0:T(8,128)(2,1)} %get-tuple-element.54), channel_id=1, source_target_pairs={{0,1},{1,2},{2,3},{3,4},{4,5},{5,6},{6,7},{7,0},{8,9},{9,10},{10,1... | collective-permute-start | bytes 5603336 | tf_op jit(solution)/shard_map/ring_z/ppermute | solution.py:373
  55.5 42.6 %collective-permute-start.8 = (bf16[128,7296]{1,0:T(8,128)(2,1)}, bf16[128,7296]{1,0:T(8,128)(2,1)}, u32[]{:S(2)}, u32[]{:S(2)}) collective-permute-start(bf16[128,7296]{1,0:T(8,128)(2,1)} %get-tuple-element.55), channel_id=1, source_target_pairs={{0,7},{1,0},{2,1},{3,2},{4,3},{5,4},{6,5},{7,6},{8,15},{9,8},{10,9... | collective-permute-start | bytes 5603336 | tf_op jit(solution)/shard_map/ring_z/ppermute | solution.py:374
  58.2 45.7 %collective-permute-start.4 = (bf16[64,7296]{1,0:T(8,128)(2,1)}, bf16[64,7296]{1,0:T(8,128)(2,1)S(1)}, u32[]{:S(2)}, u32[]{:S(2)}) collective-permute-start(bf16[64,7296]{1,0:T(8,128)(2,1)} %get-tuple-element.49), channel_id=1, source_target_pairs={{0,8},{1,9},{2,10},{3,11},{4,12},{5,13},{6,14},{7,15},{8,16},{9,17... | collective-permute-start | bytes 2801672 | tf_op jit(solution)/shard_map/pick/exchange_x/ppermute | solution.py:357
  59.4 44.5 %collective-permute-start.5 = (bf16[64,7296]{1,0:T(8,128)(2,1)}, bf16[64,7296]{1,0:T(8,128)(2,1)}, u32[]{:S(2)}, u32[]{:S(2)}) collective-permute-start(bf16[64,7296]{1,0:T(8,128)(2,1)} %get-tuple-element.50), channel_id=1, source_target_pairs={{0,16},{1,17},{2,18},{3,19},{4,20},{5,21},{6,22},{7,23},{8,24},{9,... | collective-permute-start | bytes 2801672 | tf_op jit(solution)/shard_map/pick/exchange_x/ppermute | solution.py:357
  61.9 42.1 %collective-permute-start.6 = (bf16[64,7296]{1,0:T(8,128)(2,1)}, bf16[64,7296]{1,0:T(8,128)(2,1)}, u32[]{:S(2)}, u32[]{:S(2)}) collective-permute-start(bf16[64,7296]{1,0:T(8,128)(2,1)} %get-tuple-element.51), channel_id=1, source_target_pairs={{0,24},{1,25},{2,26},{3,27},{4,28},{5,29},{6,30},{7,31},{8,0},{9,1... | collective-permute-start | bytes 2801672 | tf_op jit(solution)/shard_map/pick/exchange_x/ppermute | solution.py:357
  104.9 41.7 %collective-permute-start.12 = (bf16[128,7296]{1,0:T(8,128)(2,1)}, bf16[128,7296]{1,0:T(8,128)(2,1)}, u32[]{:S(2)}, u32[]{:S(2)}) collective-permute-start(bf16[128,7296]{1,0:T(8,128)(2,1)} %get-tuple-element.61), channel_id=1, source_target_pairs={{0,1},{1,2},{2,3},{3,4},{4,5},{5,6},{6,7},{7,0},{8,9},{9,10},{10,1... | collective-permute-start | bytes 5603336 | tf_op jit(solution)/shard_map/ring_z/ppermute | solution.py:373
  105.8 40.8 %collective-permute-start.13 = (bf16[128,7296]{1,0:T(8,128)(2,1)}, bf16[128,7296]{1,0:T(8,128)(2,1)}, u32[]{:S(2)}, u32[]{:S(2)}) collective-permute-start(bf16[128,7296]{1,0:T(8,128)(2,1)} %get-tuple-element.62), channel_id=1, source_target_pairs={{0,7},{1,0},{2,1},{3,2},{4,3},{5,4},{6,5},{7,6},{8,15},{9,8},{10,9... | collective-permute-start | bytes 5603336 | tf_op jit(solution)/shard_map/ring_z/ppermute | solution.py:374
  107.6 45.4 %collective-permute-start.10 = (bf16[64,7296]{1,0:T(8,128)(2,1)}, bf16[64,7296]{1,0:T(8,128)(2,1)S(1)}, u32[]{:S(2)}, u32[]{:S(2)}) collective-permute-start(bf16[64,7296]{1,0:T(8,128)(2,1)} %get-tuple-element.59), channel_id=1, source_target_pairs={{0,16},{1,17},{2,18},{3,19},{4,20},{5,21},{6,22},{7,23},{8,24},{9,... | collective-permute-start | bytes 2801672 | tf_op jit(solution)/shard_map/pick/exchange_x/ppermute | solution.py:357
  110.3 42.6 %collective-permute-start.11 = (bf16[64,7296]{1,0:T(8,128)(2,1)}, bf16[64,7296]{1,0:T(8,128)(2,1)}, u32[]{:S(2)}, u32[]{:S(2)}) collective-permute-start(bf16[64,7296]{1,0:T(8,128)(2,1)} %get-tuple-element.60), channel_id=1, source_target_pairs={{0,24},{1,25},{2,26},{3,27},{4,28},{5,29},{6,30},{7,31},{8,0},{9,1... | collective-permute-start | bytes 2801672 | tf_op jit(solution)/shard_map/pick/exchange_x/ppermute | solution.py:357
  111.2 41.8 %collective-permute-start.9 = (bf16[64,7296]{1,0:T(8,128)(2,1)}, bf16[64,7296]{1,0:T(8,128)(2,1)}, u32[]{:S(2)}, u32[]{:S(2)}) collective-permute-start(bf16[64,7296]{1,0:T(8,128)(2,1)} %get-tuple-element.58), channel_id=1, source_target_pairs={{0,8},{1,9},{2,10},{3,11},{4,12},{5,13},{6,14},{7,15},{8,16},{9,17... | collective-permute-start | bytes 2801672 | tf_op jit(solution)/shard_map/pick/exchange_x/ppermute | solution.py:357
  153.9 7.5 %copy-start.7 = (s32[1,1,8,32]{3,2,1,0:T(8,128)S(1)}, s32[1,1,8,32]{3,2,1,0:T(8,128)}, u32[]{:S(2)}) copy-start(s32[1,1,8,32]{3,2,1,0:T(8,128)} %param.11) | copy-start | bytes 3076
  153.9 7.6 %copy-start.8 = (s32[1,1,8]{2,1,0:T(1,128)S(1)}, s32[1,1,8]{2,1,0:T(1,128)}, u32[]{:S(2)}) copy-start(s32[1,1,8]{2,1,0:T(1,128)} %param.12) | copy-start | bytes 100
  153.9 20.4 %collective-permute-start.17 = (bf16[128,3584]{1,0:T(8,128)(2,1)}, bf16[128,3584]{1,0:T(8,128)(2,1)}, u32[]{:S(2)}, u32[]{:S(2)}) collective-permute-start(bf16[128,3584]{1,0:T(8,128)(2,1)} %get-tuple-element.72), channel_id=1, source_target_pairs={{0,1},{1,2},{2,3},{3,4},{4,5},{5,6},{6,7},{7,0},{8,9},{9,10},{10,1... | collective-permute-start | bytes 2752520 | tf_op jit(solution)/shard_map/ring_z/ppermute | solution.py:373
  154.4 32.5 %collective-permute-start.18 = (bf16[128,3712]{1,0:T(8,128)(2,1)}, bf16[128,3712]{1,0:T(8,128)(2,1)}, u32[]{:S(2)}, u32[]{:S(2)}) collective-permute-start(bf16[128,3712]{1,0:T(8,128)(2,1)} %get-tuple-element.73), channel_id=1, source_target_pairs={{0,7},{1,0},{2,1},{3,2},{4,3},{5,4},{6,5},{7,6},{8,15},{9,8},{10,9... | collective-permute-start | bytes 2850824 | tf_op jit(solution)/shard_map/ring_z/ppermute | solution.py:374
  156.6 35.7 %collective-permute-start.14 = (bf16[64,7296]{1,0:T(8,128)(2,1)}, bf16[64,7296]{1,0:T(8,128)(2,1)S(1)}, u32[]{:S(2)}, u32[]{:S(2)}) collective-permute-start(bf16[64,7296]{1,0:T(8,128)(2,1)} %get-tuple-element.67), channel_id=1, source_target_pairs={{0,8},{1,9},{2,10},{3,11},{4,12},{5,13},{6,14},{7,15},{8,16},{9,17... | collective-permute-start | bytes 2801672 | tf_op jit(solution)/shard_map/pick/exchange_x/ppermute | solution.py:357
  157.9 40.0 %collective-permute-start.15 = (bf16[64,7296]{1,0:T(8,128)(2,1)}, bf16[64,7296]{1,0:T(8,128)(2,1)}, u32[]{:S(2)}, u32[]{:S(2)}) collective-permute-start(bf16[64,7296]{1,0:T(8,128)(2,1)} %get-tuple-element.68), channel_id=1, source_target_pairs={{0,16},{1,17},{2,18},{3,19},{4,20},{5,21},{6,22},{7,23},{8,24},{9,... | collective-permute-start | bytes 2801672 | tf_op jit(solution)/shard_map/pick/exchange_x/ppermute | solution.py:357
  160.3 43.7 %collective-permute-start.16 = (bf16[64,7296]{1,0:T(8,128)(2,1)}, bf16[64,7296]{1,0:T(8,128)(2,1)}, u32[]{:S(2)}, u32[]{:S(2)}) collective-permute-start(bf16[64,7296]{1,0:T(8,128)(2,1)} %get-tuple-element.69), channel_id=1, source_target_pairs={{0,24},{1,25},{2,26},{3,27},{4,28},{5,29},{6,30},{7,31},{8,0},{9,1... | collective-permute-start | bytes 2801672 | tf_op jit(solution)/shard_map/pick/exchange_x/ppermute | solution.py:357
  174.3 76.4 %collective-permute-start.22 = (bf16[128,7168]{1,0:T(8,128)(2,1)}, bf16[128,7168]{1,0:T(8,128)(2,1)}, u32[]{:S(2)}, u32[]{:S(2)}) collective-permute-start(bf16[128,7168]{1,0:T(8,128)(2,1)} %bitcast.3.g_ref), channel_id=1, source_target_pairs={{32,0},{64,32},{96,64},{128,96},{160,128},{192,160},{224,192},{33,... | collective-permute-start | bytes 5505032 | tf_op jit(solution)/shard_map/next_section/ppermute | solution.py:27
  191.0 25.0 %collective-permute-start.19 = (bf16[32,7296]{1,0:T(8,128)(2,1)}, bf16[32,7296]{1,0:T(8,128)(2,1)}, u32[]{:S(2)}, u32[]{:S(2)}) collective-permute-start(bf16[32,7296]{1,0:T(8,128)(2,1)} %get-tuple-element.78), channel_id=1, source_target_pairs={{0,8},{1,9},{2,10},{3,11},{4,12},{5,13},{6,14},{7,15},{8,16},{9,17... | collective-permute-start | bytes 1400840 | tf_op jit(solution)/shard_map/pick/exchange_x/ppermute | solution.py:357
  192.3 17.0 %copy-start.3 = (bf16[64,7296]{1,0:T(8,128)(2,1)}, bf16[64,7296]{1,0:T(8,128)(2,1)S(1)}, u32[]{:S(2)}) copy-start(bf16[64,7296]{1,0:T(8,128)(2,1)S(1)} %collective-permute-done.14.refs_1_.refs_5_.refs_9_.refs_10_) | copy-start | bytes 2801668
  192.3 25.6 %collective-permute-start.20 = (bf16[32,7296]{1,0:T(8,128)(2,1)}, bf16[32,7296]{1,0:T(8,128)(2,1)}, u32[]{:S(2)}, u32[]{:S(2)}) collective-permute-start(bf16[32,7296]{1,0:T(8,128)(2,1)} %get-tuple-element.79), channel_id=1, source_target_pairs={{0,16},{1,17},{2,18},{3,19},{4,20},{5,21},{6,22},{7,23},{8,24},{9,... | collective-permute-start | bytes 1400840 | tf_op jit(solution)/shard_map/pick/exchange_x/ppermute | solution.py:357
  197.9 21.8 %collective-permute-start.21 = (bf16[32,7296]{1,0:T(8,128)(2,1)}, bf16[32,7296]{1,0:T(8,128)(2,1)}, u32[]{:S(2)}, u32[]{:S(2)}) collective-permute-start(bf16[32,7296]{1,0:T(8,128)(2,1)} %get-tuple-element.80), channel_id=1, source_target_pairs={{0,24},{1,25},{2,26},{3,27},{4,28},{5,29},{6,30},{7,31},{8,0},{9,1... | collective-permute-start | bytes 1400840 | tf_op jit(solution)/shard_map/pick/exchange_x/ppermute | solution.py:357
  204.0 45.6 %collective-permute-start.23 = (bf16[8,7168]{1,0:T(8,128)(2,1)}, bf16[8,7168]{1,0:T(8,128)(2,1)}, u32[]{:S(2)}, u32[]{:S(2)}) collective-permute-start(bf16[8,7168]{1,0:T(8,128)(2,1)} %bitcast.39), channel_id=1, source_target_pairs={{32,0},{64,32},{96,64},{128,96},{160,128},{192,160},{224,192},{33,... | collective-permute-start | bytes 344072 | tf_op jit(solution)/shard_map/next_section/ppermute | solution.py:27
  225.7 17.7 %all-to-all-start.1 = ((f32[32,1,32]{2,1,0:T(1,128)}), f32[32,1,32]{2,1,0:T(1,128)S(1)}, u32[]{:S(2)}, u32[]{:S(2)}) async-start(f32[32,1,32]{2,1,0:T(1,128)} %get-tuple-element.88), calls=%async_computation.1 | async-start | bytes 32768 | tf_op jit(solution)/shard_map/gate_return/all_to_all | solution.py:391
  243.4 8.9 %copy-start = (s32[10]{0:T(128)S(1)}, s32[10]{0:T(128)}, u32[]{:S(2)}) copy-start(s32[10]{0:T(128)} %pad_add_fusion.w_ref) | copy-start | bytes 124
  245.7 6.6 %collective-permute-start.24 = (bf16[24,128]{1,0:T(8,128)(2,1)}, bf16[24,128]{1,0:T(8,128)(2,1)S(1)}, u32[]{:S(2)}, u32[]{:S(2)}) collective-permute-start(bf16[24,128]{1,0:T(8,128)(2,1)} %input_grad.2), channel_id=1, source_target_pairs={{32,0},{64,32},{96,64},{128,96},{160,128},{192,160},{224,192},{33,... | collective-permute-start | bytes 18440 | tf_op jit(solution)/shard_map/input_grad/ppermute | solution.py:27
  (5 other events, 3.8 us)

commit v5 on v4

--- a/solution.py
+++ b/solution.py
@@ -27,7 +27,7 @@
     return lax.ppermute(value, axis, [(source, source + steps) for source in range(initial, last)])
 
 
-def call(kernel, grid, in_specs, out_specs, out_shape, scratch=(), aliases=None, flops=0, nbytes=0, vmem=63):
+def call(kernel, grid, in_specs, out_specs, out_shape, scratch=(), aliases=None, flops=0, nbytes=0, vmem=64):
     return pl.pallas_call(
         kernel,
         grid_spec=pltpu.PrefetchScalarGridSpec(

time: 256 us -> 253 us (0.988)
  waiting for transfers between devices: 112 us -> 109 us
    unnamed x20 -> x8, local copies, waits for them, and re-layouts: 3.13 us -> 0.02 us
  transfers between devices with their start and end apart: 27 -> 27, of which waited for: 9 -> 9; matrix products, arithmetic and copies ran while one was open for 1% -> 2% of each run, Pallas kernels for 28% -> 28%
where the time goes in v5:
time: 253 us
  waiting for transfers between devices  109 us (43%)
  Pallas kernels  74.8 us (30%)
  starting transfers between devices  63.1 us (25%)
  other arithmetic  3.75 us (1%)
    ppermute x4, waiting for transfers between devices, shards(): up = lax.ppermute(up, 'expert', shift_z(1))  68.6 us
    pallas_call x5, Pallas kernels, project(): call(kernel, (steps,), [columns(rows, TILE, 0)] * arrays + [columns(rows,...  32.1 us
    ppermute x2, waiting for transfers between devices, shards(): near = [lax.ppermute(own, 'expert', shift_z(k)) for k in (1, -1)]  27.9 us
    pallas_call x4, Pallas kernels, pick_rows(): call(kernel, (1,), [whole(x.shape) for x in flat + tables] + [HBM] * len(...  23.2 us
    ppermute x12, starting transfers between devices, exchanged(): lax.ppermute(rows[k], 'expert', shift_x(k))  17.5 us
    ppermute x3, starting transfers between devices, passed_along(): lax.ppermute(value, axis, [(source, source + steps) for source in range(i...  15.9 us
    ppermute x12, waiting for transfers between devices, exchanged(): lax.ppermute(rows[k], 'expert', shift_x(k))  10.9 us
    ppermute x4, starting transfers between devices, shards(): down = lax.ppermute(down, 'expert', shift_z(-1))  10.7 us
  transfers between devices with their start and end apart: 27, of which 9 were waited for; matrix products, arithmetic and copies ran while one was open for 2% of the time, Pallas kernels for 28%

profile of v5, /device:TPU:1, one launch (start us, length us, event | category | flops | bytes accessed | tf_op | source)
XLA Modules:
  0.0 252.8 jit_solution(1278627048225270903)
XLA Ops:
  0.6 2.5 %collective-permute-start = (bf16[128,7168]{1,0:T(8,128)(2,1)}, bf16[128,7168]{1,0:T(8,128)(2,1)}, u32[]{:S(2)}, u32[]{:S(2)}) collective-permute-start(bf16[128,7168]{1,0:T(8,128)(2,1)} %bitcast.3.g_ref), channel_id=1, source_target_pairs={{0,1},{1,2},{2,3},{3,4},{4,5},{5,6},{6,7},{7,0},{8,9},{9,10},{10,1... | collective-permute-start | bytes 5505032 | tf_op jit(solution)/shard_map/ring_z/ppermute | solution.py:373
  3.2 4.0 %collective-permute-start.1 = (bf16[128,7168]{1,0:T(8,128)(2,1)}, bf16[128,7168]{1,0:T(8,128)(2,1)}, u32[]{:S(2)}, u32[]{:S(2)}) collective-permute-start(bf16[128,7168]{1,0:T(8,128)(2,1)} %bitcast.3.g_ref), channel_id=1, source_target_pairs={{0,7},{1,0},{2,1},{3,2},{4,3},{5,4},{6,5},{7,6},{8,15},{9,8},{10,9... | collective-permute-start | bytes 5505032 | tf_op jit(solution)/shard_map/ring_z/ppermute | solution.py:374
  8.5 4.2 %pick.8 = (bf16[1,128,128]{2,1,0:T(8,128)(2,1)}, bf16[4,32,7296]{2,1,0:T(8,128)(2,1)}) custom-call(s32[10]{0:T(128)} %pad_add_fusion.w_ref, bf16[128,7168]{1,0:T(8,128)(2,1)} %bitcast.3.g_ref, s32[8,32]{1,0:T(8,128)} %bitcast.35, f32[8,32]{1,0:T(8,128)} %bitcast.36), custom_call_target="tpu_custom_call" | custom-call | flops 234881024 | bytes 5505024 | tf_op jit(solution)/shard_map/pick/pallas_call | solution.py:100
  12.7 4.5 %all-to-all-start = ((bf16[4,32,7296]{2,1,0:T(8,128)(2,1)}), bf16[4,32,7296]{2,1,0:T(8,128)(2,1)}, u32[]{:S(2)}, u32[]{:S(2)}) async-start(bf16[4,32,7296]{2,1,0:T(8,128)(2,1)} %get-tuple-element.46), calls=%async_computation | async-start | bytes 3735552 | tf_op jit(solution)/shard_map/exchange_x/all_to_all | solution.py:367
  17.3 2.7 %collective-permute-start.3 = (bf16[1,128,128]{2,1,0:T(8,128)(2,1)S(1)}, bf16[1,128,128]{2,1,0:T(8,128)(2,1)}, u32[]{:S(2)}, u32[]{:S(2)}) collective-permute-start(bf16[1,128,128]{2,1,0:T(8,128)(2,1)S(1)} %copy-done.3), channel_id=1, source_target_pairs={{0,7},{1,0},{2,1},{3,2},{4,3},{5,4},{6,5},{7,6},{8,15},{9,8},{10,9... | collective-permute-start | bytes 98312 | tf_op jit(solution)/shard_map/pick/ppermute | solution.py:363
  20.0 27.9 %collective-permute-done.2.refs_2_ = bf16[1,128,128]{2,1,0:T(8,128)(2,1)} collective-permute-done((bf16[1,128,128]{2,1,0:T(8,128)(2,1)S(1)}, bf16[1,128,128]{2,1,0:T(8,128)(2,1)}, u32[]{:S(2)}, u32[]{:S(2)}) %collective-permute-start.2) | collective-permute-done | bytes 32800 | tf_op jit(solution)/shard_map/pick/ppermute | solution.py:363
  47.9 7.1 %pick.9 = (bf16[64,7296]{1,0:T(8,128)(2,1)}, bf16[64,7296]{1,0:T(8,128)(2,1)}, bf16[64,7296]{1,0:T(8,128)(2,1)}, bf16[64,7296]{1,0:T(8,128)(2,1)}, bf16[128,7296]{1,0:T(8,128)(2,1)}, /*index=5*/bf16[128,7296]{1,0:T(8,128)(2,1)}) custom-call(s32[10]{0:T(128)} %pad_add_fusion.w_ref, bf16[128,7168]{1,0:T(8,128)(2,1)} %collective-permute-done.refs_0_, ...), custom_call_target="tpu_custom_call" | custom-call | flops 469762048 | bytes 7340032 | tf_op jit(solution)/shard_map/pick/pallas_call | solution.py:142
  55.0 2.7 %collective-permute-start.8 = (bf16[128,7296]{1,0:T(8,128)(2,1)}, bf16[128,7296]{1,0:T(8,128)(2,1)}, u32[]{:S(2)}, u32[]{:S(2)}) collective-permute-start(bf16[128,7296]{1,0:T(8,128)(2,1)} %get-tuple-element.55), channel_id=1, source_target_pairs={{0,7},{1,0},{2,1},{3,2},{4,3},{5,4},{6,5},{7,6},{8,15},{9,8},{10,9... | collective-permute-start | bytes 5603336 | tf_op jit(solution)/shard_map/ring_z/ppermute | solution.py:374
  58.8 2.5 collective-permute-start.5
  62.4 5.7 %project.5 = (bf16[32,32,256]{2,1,0:T(8,128)(2,1)}, f32[32,1,32]{2,1,0:T(1,128)}, bf16[256,128]{1,0:T(8,128)(2,1)}) custom-call(s32[10]{0:T(128)} %pad_add_fusion.w_ref, bf16[128,7296]{1,0:T(8,128)(2,1)} %bitcast.6.refs_2_.refs_0_.refs_1_, bf16[128,7296]{1,0:T(8,128)(2,1)} %bitcast.6.refs_2_.refs_0_.refs_1_, ...), custom_call_target="tpu_custom_call" | custom-call | flops 469762048 | bytes 5505024 | tf_op jit(solution)/shard_map/project/pallas_call | solution.py:238
  68.2 29.3 %collective-permute-done.7.refs_0_ = bf16[128,7296]{1,0:T(8,128)(2,1)} collective-permute-done((bf16[128,7296]{1,0:T(8,128)(2,1)}, bf16[128,7296]{1,0:T(8,128)(2,1)}, u32[]{:S(2)}, u32[]{:S(2)}) %collective-permute-start.7) | collective-permute-done | bytes 1867808 | tf_op jit(solution)/shard_map/ring_z/ppermute | solution.py:373
  97.4 5.7 %pick.11 = (bf16[64,7296]{1,0:T(8,128)(2,1)}, bf16[64,7296]{1,0:T(8,128)(2,1)}, bf16[64,7296]{1,0:T(8,128)(2,1)}, bf16[64,7296]{1,0:T(8,128)(2,1)}) custom-call(s32[10]{0:T(128)} %pad_add_fusion.w_ref, bf16[128,7296]{1,0:T(8,128)(2,1)} %collective-permute-done.7.refs_0_, bf16[128,7296]{1,0:T(8,128)(2,1)} %collective-permute-done.8.refs_1_, ...), custom_call_target="tpu_custom_call" | custom-call | flops 469762048 | bytes 7340032 | tf_op jit(solution)/shard_map/pick/pallas_call | solution.py:142
  106.0 2.8 %collective-permute-start.10 = (bf16[64,7296]{1,0:T(8,128)(2,1)}, bf16[64,7296]{1,0:T(8,128)(2,1)}, u32[]{:S(2)}, u32[]{:S(2)}) collective-permute-start(bf16[64,7296]{1,0:T(8,128)(2,1)} %get-tuple-element.59), channel_id=1, source_target_pairs={{0,16},{1,17},{2,18},{3,19},{4,20},{5,21},{6,22},{7,23},{8,24},{9,... | collective-permute-start | bytes 2801672 | tf_op jit(solution)/shard_map/pick/exchange_x/ppermute | solution.py:357
  110.2 6.8 %project.6 = (bf16[32,32,256]{2,1,0:T(8,128)(2,1)}, f32[32,1,32]{2,1,0:T(1,128)}, bf16[256,256]{1,0:T(8,128)(2,1)}) custom-call(s32[10]{0:T(128)} %pad_add_fusion.w_ref, bf16[64,7296]{1,0:T(8,128)(2,1)} %get-tuple-element.48.refs_3_.refs_0_.refs_4_.refs_8_.refs_1_, ...), custom_call_target="tpu_custom_call", output_to_operand_aliasing={{0}: (16, {}), {1}: (17, {})} | custom-call | flops 939524096 | bytes 7340032 | tf_op jit(solution)/shard_map/project/pallas_call | solution.py:238
  117.0 27.9 %collective-permute-done.12.refs_0_ = bf16[128,7296]{1,0:T(8,128)(2,1)} collective-permute-done((bf16[128,7296]{1,0:T(8,128)(2,1)}, bf16[128,7296]{1,0:T(8,128)(2,1)}, u32[]{:S(2)}, u32[]{:S(2)}) %collective-permute-start.12) | collective-permute-done | bytes 1867808 | tf_op jit(solution)/shard_map/ring_z/ppermute | solution.py:373
  144.9 6.4 %pick.13 = (bf16[64,7296]{1,0:T(8,128)(2,1)}, bf16[64,7296]{1,0:T(8,128)(2,1)}, bf16[64,7296]{1,0:T(8,128)(2,1)}, bf16[64,7296]{1,0:T(8,128)(2,1)}, bf16[128,358...) custom-call(s32[10]{0:T(128)} %pad_add_fusion.w_ref, bf16[128,7296]{1,0:T(8,128)(2,1)} %collective-permute-done.12.refs_0_, ...), custom_call_target="tpu_custom_call" | custom-call | flops 469762048 | bytes 7340032 | tf_op jit(solution)/shard_map/pick/pallas_call | solution.py:142
  151.9 2.2 collective-permute-start.18
  155.3 2.4 collective-permute-start.15
  160.2 11.5 %collective-permute-done.17.refs_0_ = bf16[128,3584]{1,0:T(8,128)(2,1)} collective-permute-done((bf16[128,3584]{1,0:T(8,128)(2,1)}, bf16[128,3584]{1,0:T(8,128)(2,1)}, u32[]{:S(2)}, u32[]{:S(2)}) %collective-permute-start.17) | collective-permute-done | bytes 917536 | tf_op jit(solution)/shard_map/ring_z/ppermute | solution.py:373
  171.7 5.9 %collective-permute-start.22 = (bf16[128,7168]{1,0:T(8,128)(2,1)}, bf16[128,7168]{1,0:T(8,128)(2,1)}, u32[]{:S(2)}, u32[]{:S(2)}) collective-permute-start(bf16[128,7168]{1,0:T(8,128)(2,1)} %bitcast.3.g_ref), channel_id=1, source_target_pairs={{32,0},{64,32},{96,64},{128,96},{160,128},{192,160},{224,192},{33,... | collective-permute-start | bytes 5505032 | tf_op jit(solution)/shard_map/next_section/ppermute | solution.py:27
  177.6 6.8 %project.7 = (bf16[32,32,256]{2,1,0:T(8,128)(2,1)}, f32[32,1,32]{2,1,0:T(1,128)}, bf16[256,256]{1,0:T(8,128)(2,1)}) custom-call(s32[10]{0:T(128)} %pad_add_fusion.w_ref, bf16[64,7296]{1,0:T(8,128)(2,1)} %get-tuple-element.57.refs_5_.refs_0_.refs_4_.refs_8_, ...), custom_call_target="tpu_custom_call", output_to_operand_aliasing={{0}: (16, {}), {1}: (17, {})} | custom-call | flops 939524096 | bytes 7340032 | tf_op jit(solution)/shard_map/project/pallas_call | solution.py:238
  184.4 4.0 %pick.15 = (bf16[32,7296]{1,0:T(8,128)(2,1)}, bf16[32,7296]{1,0:T(8,128)(2,1)}, bf16[32,7296]{1,0:T(8,128)(2,1)}, bf16[32,7296]{1,0:T(8,128)(2,1)}) custom-call(s32[10]{0:T(128)} %pad_add_fusion.w_ref, bf16[128,3584]{1,0:T(8,128)(2,1)} %collective-permute-done.17.refs_0_, bf16[128,3712]{1,0:T(8,128)(2,1)} %collective-permute-done.18.refs_1_, ...), custom_call_target="tpu_custom_call" | custom-call | flops 234881024 | bytes 3670016 | tf_op jit(solution)/shard_map/pick/pallas_call | solution.py:142
  189.7 2.4 collective-permute-start.20
  192.1 3.1 %collective-permute-done.15.refs_2_.refs_6_.refs_10_.refs_11_ = bf16[64,7296]{1,0:T(8,128)(2,1)} collective-permute-done((bf16[64,7296]{1,0:T(8,128)(2,1)}, bf16[64,7296]{1,0:T(8,128)(2,1)}, u32[]{:S(2)}, u32[]{:S(2)}) %collective-permute-start.15) | collective-permute-done | bytes 933920 | tf_op jit(solution)/shard_map/pick/exchange_x/ppermute | solution.py:357
  196.5 5.0 %collective-permute-done.16.refs_3_.refs_7_.refs_11_.refs_12_ = bf16[64,7296]{1,0:T(8,128)(2,1)} collective-permute-done((bf16[64,7296]{1,0:T(8,128)(2,1)}, bf16[64,7296]{1,0:T(8,128)(2,1)}, u32[]{:S(2)}, u32[]{:S(2)}) %collective-permute-start.16) | collective-permute-done | bytes 933920 | tf_op jit(solution)/shard_map/pick/exchange_x/ppermute | solution.py:357
  201.6 5.8 %collective-permute-start.23 = (bf16[8,7168]{1,0:T(8,128)(2,1)}, bf16[8,7168]{1,0:T(8,128)(2,1)}, u32[]{:S(2)}, u32[]{:S(2)}) collective-permute-start(bf16[8,7168]{1,0:T(8,128)(2,1)} %bitcast.39), channel_id=1, source_target_pairs={{32,0},{64,32},{96,64},{128,96},{160,128},{192,160},{224,192},{33,... | collective-permute-start | bytes 344072 | tf_op jit(solution)/shard_map/next_section/ppermute | solution.py:27
  207.4 6.8 %project.8 = (bf16[32,32,256]{2,1,0:T(8,128)(2,1)}, f32[32,1,32]{2,1,0:T(1,128)}, bf16[256,256]{1,0:T(8,128)(2,1)}) custom-call(s32[10]{0:T(128)} %pad_add_fusion.w_ref, bf16[64,7296]{1,0:T(8,128)(2,1)} %get-tuple-element.66.refs_5_.refs_0_.refs_4_.refs_8_.refs_9_, ...), custom_call_target="tpu_custom_call", output_to_operand_aliasing={{0}: (16, {}), {1}: (17, {})} | custom-call | flops 939524096 | bytes 7340032 | tf_op jit(solution)/shard_map/project/pallas_call | solution.py:238
  217.1 5.9 %project.9 = (bf16[32,32,256]{2,1,0:T(8,128)(2,1)}, f32[32,1,32]{2,1,0:T(1,128)}, bf16[256,128]{1,0:T(8,128)(2,1)}) custom-call(s32[10]{0:T(128)} %pad_add_fusion.w_ref, bf16[32,7296]{1,0:T(8,128)(2,1)} %get-tuple-element.77.refs_0_.refs_4_.refs_8_.refs_13_, ...), custom_call_target="tpu_custom_call", output_to_operand_aliasing={{0}: (16, {}), {1}: (17, {})} | custom-call | flops 469762048 | bytes 5505024 | tf_op jit(solution)/shard_map/project/pallas_call | solution.py:238
  223.0 7.7 %all-to-all-start.1 = ((f32[32,1,32]{2,1,0:T(1,128)}), f32[32,1,32]{2,1,0:T(1,128)}, u32[]{:S(2)}, u32[]{:S(2)}) async-start(f32[32,1,32]{2,1,0:T(1,128)} %get-tuple-element.88), calls=%async_computation.1 | async-start | bytes 32768 | tf_op jit(solution)/shard_map/gate_return/all_to_all | solution.py:391
  230.7 10.1 %weight_grad.1.refs_0_ = bf16[256,7168]{1,0:T(8,128)(2,1)} custom-call(s32[10]{0:T(128)} %pad_add_fusion.w_ref, bf16[128,7296]{1,0:T(8,128)(2,1)} %bitcast.6.refs_2_.refs_0_.refs_1_, bf16[64,7296]{1,0:T(8,128)(2,1)} %get-tuple-element.48.refs_3_.refs_0_.refs_4_.refs_8_.refs_1_, bf16[64,7296]{1,0:T(8,128)(2,1)} %collective-permute-done.4.refs_2_.refs_1_.refs_5_.refs_9_, ...), custom_call_target="tpu_custom_call" | custom-call | flops 3758096384 | bytes 18350080 | tf_op jit(solution)/shard_map/weight_grad/pallas_call | solution.py:277
  242.5 4.1 %collective-permute-start.24 = (bf16[24,128]{1,0:T(8,128)(2,1)}, bf16[24,128]{1,0:T(8,128)(2,1)S(1)}, u32[]{:S(2)}, u32[]{:S(2)}) collective-permute-start(bf16[24,128]{1,0:T(8,128)(2,1)} %input_grad.2), channel_id=1, source_target_pairs={{32,0},{64,32},{96,64},{128,96},{160,128},{192,160},{224,192},{33,... | collective-permute-start | bytes 18440 | tf_op jit(solution)/shard_map/input_grad/ppermute | solution.py:27
  249.3 3.5 %input_grad.3 = bf16[128,7168]{1,0:T(8,128)(2,1)} custom-call(s32[10]{0:T(128)S(1)} %copy-done, bf16[128,7168]{1,0:T(8,128)(2,1)} %collective-permute-done.22.g_ref, bf16[24,7168]{1,0:T(8,128)(2,1)S(1)} %pad_maximum_fusion.r_ref, bf16[24,128]{1,0:T(8,128)(2,1)S(1)} %collective-permute-done.24.l_ref), custom_call_target="tpu_custom_call" | custom-call | flops 44040192 | bytes 3670016 | tf_op jit(solution)/shard_map/input_grad/pallas_call | solution.py:296
  (53 shorter events, 22.0 us)
Async XLA Ops:
  0.6 47.2 %collective-permute-start = (bf16[128,7168]{1,0:T(8,128)(2,1)}, bf16[128,7168]{1,0:T(8,128)(2,1)}, u32[]{:S(2)}, u32[]{:S(2)}) collective-permute-start(bf16[128,7168]{1,0:T(8,128)(2,1)} %bitcast.3.g_ref), channel_id=1, source_target_pairs={{0,1},{1,2},{2,3},{3,4},{4,5},{5,6},{6,7},{7,0},{8,9},{9,10},{10,1... | collective-permute-start | bytes 5505032 | tf_op jit(solution)/shard_map/ring_z/ppermute | solution.py:373
  3.2 44.7 %collective-permute-start.1 = (bf16[128,7168]{1,0:T(8,128)(2,1)}, bf16[128,7168]{1,0:T(8,128)(2,1)}, u32[]{:S(2)}, u32[]{:S(2)}) collective-permute-start(bf16[128,7168]{1,0:T(8,128)(2,1)} %bitcast.3.g_ref), channel_id=1, source_target_pairs={{0,7},{1,0},{2,1},{3,2},{4,3},{5,4},{6,5},{7,6},{8,15},{9,8},{10,9... | collective-permute-start | bytes 5505032 | tf_op jit(solution)/shard_map/ring_z/ppermute | solution.py:374
  12.7 4.5 %copy-start.3 = (bf16[1,128,128]{2,1,0:T(8,128)(2,1)S(1)}, bf16[1,128,128]{2,1,0:T(8,128)(2,1)}, u32[]{:S(2)}) copy-start(bf16[1,128,128]{2,1,0:T(8,128)(2,1)} %get-tuple-element.47) | copy-start | bytes 98308
  12.7 42.3 %all-to-all-start = ((bf16[4,32,7296]{2,1,0:T(8,128)(2,1)}), bf16[4,32,7296]{2,1,0:T(8,128)(2,1)}, u32[]{:S(2)}, u32[]{:S(2)}) async-start(bf16[4,32,7296]{2,1,0:T(8,128)(2,1)} %get-tuple-element.46), calls=%async_computation | async-start | bytes 3735552 | tf_op jit(solution)/shard_map/exchange_x/all_to_all | solution.py:367
  17.2 30.7 %collective-permute-start.2 = (bf16[1,128,128]{2,1,0:T(8,128)(2,1)S(1)}, bf16[1,128,128]{2,1,0:T(8,128)(2,1)}, u32[]{:S(2)}, u32[]{:S(2)}) collective-permute-start(bf16[1,128,128]{2,1,0:T(8,128)(2,1)S(1)} %copy-done.3), channel_id=1, source_target_pairs={{0,1},{1,2},{2,3},{3,4},{4,5},{5,6},{6,7},{7,0},{8,9},{9,10},{10,1... | collective-permute-start | bytes 98312 | tf_op jit(solution)/shard_map/pick/ppermute | solution.py:363
  17.3 30.6 %collective-permute-start.3 = (bf16[1,128,128]{2,1,0:T(8,128)(2,1)S(1)}, bf16[1,128,128]{2,1,0:T(8,128)(2,1)}, u32[]{:S(2)}, u32[]{:S(2)}) collective-permute-start(bf16[1,128,128]{2,1,0:T(8,128)(2,1)S(1)} %copy-done.3), channel_id=1, source_target_pairs={{0,7},{1,0},{2,1},{3,2},{4,3},{5,4},{6,5},{7,6},{8,15},{9,8},{10,9... | collective-permute-start | bytes 98312 | tf_op jit(solution)/shard_map/pick/ppermute | solution.py:363
  54.9 42.5 %collective-permute-start.7 = (bf16[128,7296]{1,0:T(8,128)(2,1)}, bf16[128,7296]{1,0:T(8,128)(2,1)}, u32[]{:S(2)}, u32[]{:S(2)}) collective-permute-start(bf16[128,7296]{1,0:T(8,128)(2,1)} %get-tuple-element.54), channel_id=1, source_target_pairs={{0,1},{1,2},{2,3},{3,4},{4,5},{5,6},{6,7},{7,0},{8,9},{9,10},{10,1... | collective-permute-start | bytes 5603336 | tf_op jit(solution)/shard_map/ring_z/ppermute | solution.py:373
  55.0 42.5 %collective-permute-start.8 = (bf16[128,7296]{1,0:T(8,128)(2,1)}, bf16[128,7296]{1,0:T(8,128)(2,1)}, u32[]{:S(2)}, u32[]{:S(2)}) collective-permute-start(bf16[128,7296]{1,0:T(8,128)(2,1)} %get-tuple-element.55), channel_id=1, source_target_pairs={{0,7},{1,0},{2,1},{3,2},{4,3},{5,4},{6,5},{7,6},{8,15},{9,8},{10,9... | collective-permute-start | bytes 5603336 | tf_op jit(solution)/shard_map/ring_z/ppermute | solution.py:374
  57.6 45.6 %collective-permute-start.4 = (bf16[64,7296]{1,0:T(8,128)(2,1)}, bf16[64,7296]{1,0:T(8,128)(2,1)}, u32[]{:S(2)}, u32[]{:S(2)}) collective-permute-start(bf16[64,7296]{1,0:T(8,128)(2,1)} %get-tuple-element.49), channel_id=1, source_target_pairs={{0,8},{1,9},{2,10},{3,11},{4,12},{5,13},{6,14},{7,15},{8,16},{9,17... | collective-permute-start | bytes 2801672 | tf_op jit(solution)/shard_map/pick/exchange_x/ppermute | solution.py:357
  58.8 44.4 %collective-permute-start.5 = (bf16[64,7296]{1,0:T(8,128)(2,1)}, bf16[64,7296]{1,0:T(8,128)(2,1)}, u32[]{:S(2)}, u32[]{:S(2)}) collective-permute-start(bf16[64,7296]{1,0:T(8,128)(2,1)} %get-tuple-element.50), channel_id=1, source_target_pairs={{0,16},{1,17},{2,18},{3,19},{4,20},{5,21},{6,22},{7,23},{8,24},{9,... | collective-permute-start | bytes 2801672 | tf_op jit(solution)/shard_map/pick/exchange_x/ppermute | solution.py:357
  61.3 41.9 %collective-permute-start.6 = (bf16[64,7296]{1,0:T(8,128)(2,1)}, bf16[64,7296]{1,0:T(8,128)(2,1)}, u32[]{:S(2)}, u32[]{:S(2)}) collective-permute-start(bf16[64,7296]{1,0:T(8,128)(2,1)} %get-tuple-element.51), channel_id=1, source_target_pairs={{0,24},{1,25},{2,26},{3,27},{4,28},{5,29},{6,30},{7,31},{8,0},{9,1... | collective-permute-start | bytes 2801672 | tf_op jit(solution)/shard_map/pick/exchange_x/ppermute | solution.py:357
  103.2 41.7 %collective-permute-start.12 = (bf16[128,7296]{1,0:T(8,128)(2,1)}, bf16[128,7296]{1,0:T(8,128)(2,1)}, u32[]{:S(2)}, u32[]{:S(2)}) collective-permute-start(bf16[128,7296]{1,0:T(8,128)(2,1)} %get-tuple-element.61), channel_id=1, source_target_pairs={{0,1},{1,2},{2,3},{3,4},{4,5},{5,6},{6,7},{7,0},{8,9},{9,10},{10,1... | collective-permute-start | bytes 5603336 | tf_op jit(solution)/shard_map/ring_z/ppermute | solution.py:373
  104.2 40.7 %collective-permute-start.13 = (bf16[128,7296]{1,0:T(8,128)(2,1)}, bf16[128,7296]{1,0:T(8,128)(2,1)}, u32[]{:S(2)}, u32[]{:S(2)}) collective-permute-start(bf16[128,7296]{1,0:T(8,128)(2,1)} %get-tuple-element.62), channel_id=1, source_target_pairs={{0,7},{1,0},{2,1},{3,2},{4,3},{5,4},{6,5},{7,6},{8,15},{9,8},{10,9... | collective-permute-start | bytes 5603336 | tf_op jit(solution)/shard_map/ring_z/ppermute | solution.py:374
  106.0 45.3 %collective-permute-start.10 = (bf16[64,7296]{1,0:T(8,128)(2,1)}, bf16[64,7296]{1,0:T(8,128)(2,1)}, u32[]{:S(2)}, u32[]{:S(2)}) collective-permute-start(bf16[64,7296]{1,0:T(8,128)(2,1)} %get-tuple-element.59), channel_id=1, source_target_pairs={{0,16},{1,17},{2,18},{3,19},{4,20},{5,21},{6,22},{7,23},{8,24},{9,... | collective-permute-start | bytes 2801672 | tf_op jit(solution)/shard_map/pick/exchange_x/ppermute | solution.py:357
  108.7 42.5 %collective-permute-start.11 = (bf16[64,7296]{1,0:T(8,128)(2,1)}, bf16[64,7296]{1,0:T(8,128)(2,1)}, u32[]{:S(2)}, u32[]{:S(2)}) collective-permute-start(bf16[64,7296]{1,0:T(8,128)(2,1)} %get-tuple-element.60), channel_id=1, source_target_pairs={{0,24},{1,25},{2,26},{3,27},{4,28},{5,29},{6,30},{7,31},{8,0},{9,1... | collective-permute-start | bytes 2801672 | tf_op jit(solution)/shard_map/pick/exchange_x/ppermute | solution.py:357
  109.6 41.7 %collective-permute-start.9 = (bf16[64,7296]{1,0:T(8,128)(2,1)}, bf16[64,7296]{1,0:T(8,128)(2,1)}, u32[]{:S(2)}, u32[]{:S(2)}) collective-permute-start(bf16[64,7296]{1,0:T(8,128)(2,1)} %get-tuple-element.58), channel_id=1, source_target_pairs={{0,8},{1,9},{2,10},{3,11},{4,12},{5,13},{6,14},{7,15},{8,16},{9,17... | collective-permute-start | bytes 2801672 | tf_op jit(solution)/shard_map/pick/exchange_x/ppermute | solution.py:357
  151.3 7.6 %copy-start.1 = (s32[1,1,8,32]{3,2,1,0:T(8,128)S(1)}, s32[1,1,8,32]{3,2,1,0:T(8,128)}, u32[]{:S(2)}) copy-start(s32[1,1,8,32]{3,2,1,0:T(8,128)} %param.11) | copy-start | bytes 3076
  151.3 8.2 %copy-start.2 = (s32[1,1,8]{2,1,0:T(1,128)S(1)}, s32[1,1,8]{2,1,0:T(1,128)}, u32[]{:S(2)}) copy-start(s32[1,1,8]{2,1,0:T(1,128)} %param.12) | copy-start | bytes 100
  151.3 20.4 %collective-permute-start.17 = (bf16[128,3584]{1,0:T(8,128)(2,1)}, bf16[128,3584]{1,0:T(8,128)(2,1)}, u32[]{:S(2)}, u32[]{:S(2)}) collective-permute-start(bf16[128,3584]{1,0:T(8,128)(2,1)} %get-tuple-element.72), channel_id=1, source_target_pairs={{0,1},{1,2},{2,3},{3,4},{4,5},{5,6},{6,7},{7,0},{8,9},{9,10},{10,1... | collective-permute-start | bytes 2752520 | tf_op jit(solution)/shard_map/ring_z/ppermute | solution.py:373
  151.9 32.5 %collective-permute-start.18 = (bf16[128,3712]{1,0:T(8,128)(2,1)}, bf16[128,3712]{1,0:T(8,128)(2,1)}, u32[]{:S(2)}, u32[]{:S(2)}) collective-permute-start(bf16[128,3712]{1,0:T(8,128)(2,1)} %get-tuple-element.73), channel_id=1, source_target_pairs={{0,7},{1,0},{2,1},{3,2},{4,3},{5,4},{6,5},{7,6},{8,15},{9,8},{10,9... | collective-permute-start | bytes 2850824 | tf_op jit(solution)/shard_map/ring_z/ppermute | solution.py:374
  154.1 35.6 %collective-permute-start.14 = (bf16[64,7296]{1,0:T(8,128)(2,1)}, bf16[64,7296]{1,0:T(8,128)(2,1)}, u32[]{:S(2)}, u32[]{:S(2)}) collective-permute-start(bf16[64,7296]{1,0:T(8,128)(2,1)} %get-tuple-element.67), channel_id=1, source_target_pairs={{0,8},{1,9},{2,10},{3,11},{4,12},{5,13},{6,14},{7,15},{8,16},{9,17... | collective-permute-start | bytes 2801672 | tf_op jit(solution)/shard_map/pick/exchange_x/ppermute | solution.py:357
  155.3 39.9 %collective-permute-start.15 = (bf16[64,7296]{1,0:T(8,128)(2,1)}, bf16[64,7296]{1,0:T(8,128)(2,1)}, u32[]{:S(2)}, u32[]{:S(2)}) collective-permute-start(bf16[64,7296]{1,0:T(8,128)(2,1)} %get-tuple-element.68), channel_id=1, source_target_pairs={{0,16},{1,17},{2,18},{3,19},{4,20},{5,21},{6,22},{7,23},{8,24},{9,... | collective-permute-start | bytes 2801672 | tf_op jit(solution)/shard_map/pick/exchange_x/ppermute | solution.py:357
  157.7 43.8 %collective-permute-start.16 = (bf16[64,7296]{1,0:T(8,128)(2,1)}, bf16[64,7296]{1,0:T(8,128)(2,1)}, u32[]{:S(2)}, u32[]{:S(2)}) collective-permute-start(bf16[64,7296]{1,0:T(8,128)(2,1)} %get-tuple-element.69), channel_id=1, source_target_pairs={{0,24},{1,25},{2,26},{3,27},{4,28},{5,29},{6,30},{7,31},{8,0},{9,1... | collective-permute-start | bytes 2801672 | tf_op jit(solution)/shard_map/pick/exchange_x/ppermute | solution.py:357
  171.7 76.1 %collective-permute-start.22 = (bf16[128,7168]{1,0:T(8,128)(2,1)}, bf16[128,7168]{1,0:T(8,128)(2,1)}, u32[]{:S(2)}, u32[]{:S(2)}) collective-permute-start(bf16[128,7168]{1,0:T(8,128)(2,1)} %bitcast.3.g_ref), channel_id=1, source_target_pairs={{32,0},{64,32},{96,64},{128,96},{160,128},{192,160},{224,192},{33,... | collective-permute-start | bytes 5505032 | tf_op jit(solution)/shard_map/next_section/ppermute | solution.py:27
  188.5 25.8 %collective-permute-start.19 = (bf16[32,7296]{1,0:T(8,128)(2,1)}, bf16[32,7296]{1,0:T(8,128)(2,1)}, u32[]{:S(2)}, u32[]{:S(2)}) collective-permute-start(bf16[32,7296]{1,0:T(8,128)(2,1)} %get-tuple-element.78), channel_id=1, source_target_pairs={{0,8},{1,9},{2,10},{3,11},{4,12},{5,13},{6,14},{7,15},{8,16},{9,17... | collective-permute-start | bytes 1400840 | tf_op jit(solution)/shard_map/pick/exchange_x/ppermute | solution.py:357
  189.7 25.5 %collective-permute-start.20 = (bf16[32,7296]{1,0:T(8,128)(2,1)}, bf16[32,7296]{1,0:T(8,128)(2,1)}, u32[]{:S(2)}, u32[]{:S(2)}) collective-permute-start(bf16[32,7296]{1,0:T(8,128)(2,1)} %get-tuple-element.79), channel_id=1, source_target_pairs={{0,16},{1,17},{2,18},{3,19},{4,20},{5,21},{6,22},{7,23},{8,24},{9,... | collective-permute-start | bytes 1400840 | tf_op jit(solution)/shard_map/pick/exchange_x/ppermute | solution.py:357
  195.2 21.9 %collective-permute-start.21 = (bf16[32,7296]{1,0:T(8,128)(2,1)}, bf16[32,7296]{1,0:T(8,128)(2,1)}, u32[]{:S(2)}, u32[]{:S(2)}) collective-permute-start(bf16[32,7296]{1,0:T(8,128)(2,1)} %get-tuple-element.80), channel_id=1, source_target_pairs={{0,24},{1,25},{2,26},{3,27},{4,28},{5,29},{6,30},{7,31},{8,0},{9,1... | collective-permute-start | bytes 1400840 | tf_op jit(solution)/shard_map/pick/exchange_x/ppermute | solution.py:357
  201.6 45.1 %collective-permute-start.23 = (bf16[8,7168]{1,0:T(8,128)(2,1)}, bf16[8,7168]{1,0:T(8,128)(2,1)}, u32[]{:S(2)}, u32[]{:S(2)}) collective-permute-start(bf16[8,7168]{1,0:T(8,128)(2,1)} %bitcast.39), channel_id=1, source_target_pairs={{32,0},{64,32},{96,64},{128,96},{160,128},{192,160},{224,192},{33,... | collective-permute-start | bytes 344072 | tf_op jit(solution)/shard_map/next_section/ppermute | solution.py:27
  223.0 17.8 %all-to-all-start.1 = ((f32[32,1,32]{2,1,0:T(1,128)}), f32[32,1,32]{2,1,0:T(1,128)}, u32[]{:S(2)}, u32[]{:S(2)}) async-start(f32[32,1,32]{2,1,0:T(1,128)} %get-tuple-element.88), calls=%async_computation.1 | async-start | bytes 32768 | tf_op jit(solution)/shard_map/gate_return/all_to_all | solution.py:391
  240.8 8.5 %copy-start = (s32[10]{0:T(128)S(1)}, s32[10]{0:T(128)}, u32[]{:S(2)}) copy-start(s32[10]{0:T(128)} %pad_add_fusion.w_ref) | copy-start | bytes 124
  242.5 6.8 %collective-permute-start.24 = (bf16[24,128]{1,0:T(8,128)(2,1)}, bf16[24,128]{1,0:T(8,128)(2,1)S(1)}, u32[]{:S(2)}, u32[]{:S(2)}) collective-permute-start(bf16[24,128]{1,0:T(8,128)(2,1)} %input_grad.2), channel_id=1, source_target_pairs={{32,0},{64,32},{96,64},{128,96},{160,128},{192,160},{224,192},{33,... | collective-permute-start | bytes 18440 | tf_op jit(solution)/shard_map/input_grad/ppermute | solution.py:27
